TPU v7x, 32 devices: a whole 2x2x4 slice. The times are simulated.
32 devices in a mesh: seq: 16 (over z, y, x), rep: 2 (over core).
Axes of the slice: x: 2, y: 2, z: 4, core: 2. Of those that a mesh axis runs over, the one named last changes fastest.
Arguments:
- tokens: bfloat16 [2, 32768, 768], P('rep', 'seq'), may hold values from -8.5 to 8.5
- cotangent: bfloat16 [2, 32768, 768], P('rep', 'seq'), may hold values from -6 to 6
- attn_w: float32 [4, 768, 768], P(None, ('seq', 'rep')), may hold values from -0.21650635 to 0.21650635
- w_up: float32 [768, 3072], P(('seq', 'rep')), may hold values from -0.21875 to 0.21875
- w_down: float32 [3072, 768], P(('seq', 'rep')), may hold values from -0.109375 to 0.109375
- vectors: float32 [768, 35], P(('seq', 'rep')), may hold values from -1.5 to 1.5, as said below
- attn_m: float32 [4, 768, 768], P(None, ('seq', 'rep')), may hold values from -46.08 to 46.08
- attn_v: float32 [4, 768, 768], P(None, ('seq', 'rep')), may hold values from 1.31072 to 52.4288
- up_m: float32 [768, 3072], P(('seq', 'rep')), may hold values from -80 to 80
- up_v: float32 [768, 3072], P(('seq', 'rep')), may hold values from 13.1072 to 65.536
- down_m: float32 [3072, 768], P(('seq', 'rep')), may hold values from -64 to 64
- down_v: float32 [3072, 768], P(('seq', 'rep')), may hold values from 9.8304 to 52.4288
- vec_m: float32 [768, 35], P(('seq', 'rep')), may hold values from -160 to 160
- vec_v: float32 [768, 35], P(('seq', 'rep')), may hold values from 32.768 to 262.144
Outputs:
- output: bfloat16 [2, 32768, 768], P('rep', 'seq')
- input_grad: bfloat16 [2, 32768, 768], P('rep', 'seq')
- attn_new: float32 [4, 768, 768], P(None, ('seq', 'rep'))
- attn_m_new: float32 [4, 768, 768], P(None, ('seq', 'rep'))
- attn_v_new: float32 [4, 768, 768], P(None, ('seq', 'rep'))
- up_new: float32 [768, 3072], P(('seq', 'rep'))
- up_m_new: float32 [768, 3072], P(('seq', 'rep'))
- up_v_new: float32 [768, 3072], P(('seq', 'rep'))
- down_new: float32 [3072, 768], P(('seq', 'rep'))
- down_m_new: float32 [3072, 768], P(('seq', 'rep'))
- down_v_new: float32 [3072, 768], P(('seq', 'rep'))
- vec_new: float32 [768, 35], P(('seq', 'rep'))
- vec_m_new: float32 [768, 35], P(('seq', 'rep'))
- vec_v_new: float32 [768, 35], P(('seq', 'rep'))
Inputs may be any that keep to these rules, and one draw needn't show every extreme that they name: `vectors`: columns 0 and 1 lie near 1; the other 33 columns are of order 1 / sqrt(33).
All inputs are finite; a program needn't handle non-finite values.
Results may differ from a plain program's by a relative error of at most 0.012.
Values may be sent and summed in bfloat16 or wider, within the bound.
A program may use at most 320 MiB of HBM per device.

v0:
```python
import jax
import jax.numpy as jnp
from jax import lax
from jax.sharding import PartitionSpec as P

H = 12
HD = 64
M = 64
KC = 33
NSITER = 6
STEP = 10


EPS_NORM = 1e-05
BETA_ONE = 0.9
BETA_TWO = 0.999
ADAM_EPS = 1e-08
LEARN_RATE = 0.03
VECTOR_RATE = 0.15
DECAY_RATE = 0.1


def padded(cells, sides, width):
    for axis, dim in sides:
        count = lax.axis_size(axis)
        ends = count - 1
        head = lax.slice_in_dim(cells, 0, width, axis=dim)
        tail = lax.slice_in_dim(cells, cells.shape[dim] - width, cells.shape[dim], axis=dim)
        cells = jnp.concatenate(
            [
                lax.ppermute(tail, axis, [(i, (i + 1) % count) for i in range(ends)]),
                cells,
                lax.ppermute(head, axis, [((i + 1) % count, i) for i in range(ends)]),
            ],
            axis=dim,
        )
    return cells


def pseudo_inverse(matrix):
    column_sums = jnp.sum(matrix, axis=1)
    bound_value = jnp.sqrt(jnp.sum(column_sums * column_sums, axis=-1))
    iterate = jnp.swapaxes(matrix, 1, 2) / bound_value[:, None, None]
    identity = jnp.eye(matrix.shape[-1], dtype=matrix.dtype)
    for sweep_index in range(NSITER):
        product = jnp.einsum("hij,hjk->hik", matrix, iterate, precision=lax.Precision.HIGHEST)
        inner_term = 7.0 * identity - product
        inner_term = 15.0 * identity - jnp.einsum(
            "hij,hjk->hik", product, inner_term, precision=lax.Precision.HIGHEST
        )
        inner_term = 13.0 * identity - jnp.einsum(
            "hij,hjk->hik", product, inner_term, precision=lax.Precision.HIGHEST
        )
        iterate = 0.25 * jnp.einsum(
            "hij,hjk->hik", iterate, inner_term, precision=lax.Precision.HIGHEST
        )
    return iterate


def norm_forward(values, gain_vec):
    center = values - jnp.mean(values, axis=-1, keepdims=True)
    inverse_std = lax.rsqrt(jnp.mean(center * center, axis=-1, keepdims=True) + EPS_NORM)
    normal_x = center * inverse_std
    return (normal_x * gain_vec, normal_x, inverse_std)


def norm_backward(upstream, normal_x, inverse_std, gain_vec):
    scaled = upstream * gain_vec
    gain_grad = jnp.sum(upstream * normal_x, axis=0)
    centered = scaled - jnp.mean(scaled, axis=-1, keepdims=True)
    result = inverse_std * (
        centered - normal_x * jnp.mean(scaled * normal_x, axis=-1, keepdims=True)
    )
    return (result, gain_grad)


def mask_rims(extended, radius, keep_left, keep_right):
    tok_count = extended.shape[0] - 2 * radius
    left_part = jnp.where(keep_left, extended[:radius], jnp.zeros_like(extended[:radius]))
    right_part = jnp.where(
        keep_right, extended[radius + tok_count :], jnp.zeros_like(extended[:radius])
    )
    return jnp.concatenate([left_part, extended[radius : radius + tok_count], right_part], axis=0)


def gelu_exact(values):
    return jax.nn.gelu(values, approximate=False)


def adam_step(weight, grad_vec, moment, second, rate_value):
    moment_new = BETA_ONE * moment + (1.0 - BETA_ONE) * grad_vec
    second_new = BETA_TWO * second + (1.0 - BETA_TWO) * grad_vec * grad_vec
    first_hat = moment_new / (1.0 - BETA_ONE**STEP)
    second_hat = second_new / (1.0 - BETA_TWO**STEP)
    weight_new = weight - rate_value * (
        first_hat / (jnp.sqrt(second_hat) + ADAM_EPS) + DECAY_RATE * weight
    )
    return (weight_new, moment_new, second_new)


def per_device(
    tokens,
    cotangent,
    attn_w,
    w_up,
    w_down,
    vectors,
    attn_m,
    attn_v,
    up_m,
    up_v,
    down_m,
    down_v,
    vec_m,
    vec_v,
):
    highest_precision = lax.Precision.HIGHEST
    single_float = jnp.float32
    attn_full, up_full, down_full, vector_full = (
        lax.all_gather(attn_w.astype(jnp.bfloat16), ("seq", "rep"), axis=1, tiled=True),
        lax.all_gather(w_up.astype(jnp.bfloat16), ("seq", "rep"), axis=0, tiled=True),
        lax.all_gather(w_down.astype(jnp.bfloat16), ("seq", "rep"), axis=0, tiled=True),
        lax.all_gather(vectors.astype(jnp.bfloat16), ("seq", "rep"), axis=0, tiled=True),
    )
    weight_q = attn_full[0]
    weight_k = attn_full[1]
    weight_v = attn_full[2]
    weight_o = attn_full[3]
    small_f = vector_full.astype(single_float)
    gain_one = small_f[:, 0]
    gain_two = small_f[:, 1]
    kernel_t = jnp.transpose(small_f[:, 2:])
    inputs = tokens[0].astype(single_float)
    tok_count = inputs.shape[0]
    model_width = inputs.shape[1]
    seq_count = lax.axis_size("seq")
    rows_dev = max(M // seq_count, 1)
    per_mark = seq_count * rows_dev // M
    seg_len = tok_count * seq_count // M
    qk_scale = HD ** (-0.25)
    radius = (KC - 1) // 2
    seq_index = lax.axis_index("seq")
    keep_left = seq_index > 0
    keep_right = seq_index < seq_count - 1
    normed_f, normal_one, inv_one = norm_forward(inputs, gain_one)
    normed = normed_f.astype(jnp.bfloat16)
    queries = (jnp.dot(normed, weight_q, preferred_element_type=single_float) * qk_scale).astype(
        jnp.bfloat16
    )
    keys_local = (jnp.dot(normed, weight_k, preferred_element_type=single_float) * qk_scale).astype(
        jnp.bfloat16
    )
    values_local = jnp.dot(normed, weight_v, preferred_element_type=single_float).astype(
        jnp.bfloat16
    )
    local_q = jnp.mean(
        queries.reshape(rows_dev, tok_count // rows_dev, model_width), axis=1, dtype=single_float
    )
    local_k = jnp.mean(
        keys_local.reshape(rows_dev, tok_count // rows_dev, model_width), axis=1, dtype=single_float
    )
    all_q, all_k = (
        lax.all_gather(local_q, "seq", axis=0, tiled=True),
        lax.all_gather(local_k, "seq", axis=0, tiled=True),
    )
    marks_q = jnp.mean(all_q.reshape(M, per_mark, model_width), axis=1).astype(jnp.bfloat16)
    marks_k = jnp.mean(all_k.reshape(M, per_mark, model_width), axis=1).astype(jnp.bfloat16)
    query_heads = queries.reshape(tok_count, H, HD)
    key_heads = keys_local.reshape(tok_count, H, HD)
    value_heads = values_local.reshape(tok_count, H, HD)
    landmark_query_heads = marks_q.reshape(M, H, HD)
    landmark_key_heads = marks_k.reshape(M, H, HD)
    score_matrix = jnp.einsum(
        "ijo,njo->ijn", query_heads, landmark_key_heads, preferred_element_type=single_float
    )
    probs_f = jax.nn.softmax(score_matrix, axis=-1)
    weights_single = probs_f.astype(jnp.bfloat16)
    kernel_weights = jax.nn.softmax(
        jnp.einsum(
            "fwz,uwz->wfu",
            landmark_query_heads,
            landmark_key_heads,
            preferred_element_type=single_float,
        ),
        axis=-1,
    )
    inverse_matrix, inverse_pull = jax.vjp(pseudo_inverse, kernel_weights)
    second_score_matrix = jnp.einsum(
        "czf,qzf->zcq", landmark_query_heads, key_heads, preferred_element_type=single_float
    )
    exponent_values = jnp.exp(second_score_matrix)
    exponent_landmark = exponent_values.astype(jnp.bfloat16)
    partial_totals = jnp.einsum(
        "iuo,oiz->iuz", exponent_landmark, value_heads, preferred_element_type=single_float
    )
    part_total = jnp.sum(exponent_values, axis=-1)
    value_sum, value_total = lax.psum((partial_totals, part_total), "seq")
    value_mixture = value_sum / value_total[..., None]
    landmark_output = jnp.einsum(
        "zgw,zwx->zgx", inverse_matrix, value_mixture, precision=highest_precision
    ).astype(jnp.bfloat16)
    attended_rows = jnp.einsum(
        "loy,oyv->lov", weights_single, landmark_output, preferred_element_type=single_float
    ).reshape(tok_count, model_width)
    extended = mask_rims(padded(values_local, (("seq", 0),), radius), radius, keep_left, keep_right)
    ext_f = extended.astype(single_float)

    def conv_tap(tap_index, running):
        window = lax.dynamic_slice_in_dim(ext_f, tap_index, tok_count, 0)
        return running + window * lax.dynamic_slice_in_dim(kernel_t, tap_index, 1, 0)

    convolved = lax.fori_loop(0, KC, conv_tap, jnp.zeros((tok_count, model_width), single_float))
    mixture = (attended_rows + convolved).astype(jnp.bfloat16)
    residual = inputs + jnp.dot(mixture, weight_o, preferred_element_type=single_float)
    normed_two_f, normal_two, inv_two = norm_forward(residual, gain_two)
    normed_two = normed_two_f.astype(jnp.bfloat16)
    pre_act = jnp.dot(normed_two, up_full, preferred_element_type=single_float)
    activation, gelu_pull = jax.vjp(gelu_exact, pre_act)
    hidden = activation.astype(jnp.bfloat16)
    output = residual + jnp.dot(hidden, down_full, preferred_element_type=single_float)
    upstream = cotangent[0]
    grad_down = jnp.einsum("tf,td->fd", hidden, upstream, preferred_element_type=single_float)
    grad_hidden = jnp.einsum("td,fd->tf", upstream, down_full, preferred_element_type=single_float)
    grad_pre = gelu_pull(grad_hidden)[0].astype(jnp.bfloat16)
    grad_up = jnp.einsum("td,tf->df", normed_two, grad_pre, preferred_element_type=single_float)
    grad_normed_two = jnp.einsum(
        "tf,df->td", grad_pre, up_full, preferred_element_type=single_float
    )
    grad_res_norm, grad_gain_two = norm_backward(grad_normed_two, normal_two, inv_two, gain_two)
    grad_residual = grad_res_norm + upstream.astype(single_float)
    grad_branch = grad_residual.astype(jnp.bfloat16)
    grad_weight_o = jnp.einsum(
        "td,te->de", mixture, grad_branch, preferred_element_type=single_float
    )
    grad_mixture = jnp.einsum(
        "te,de->td", grad_branch, weight_o, preferred_element_type=single_float
    ).astype(jnp.bfloat16)
    head_gradient = grad_mixture.reshape(tok_count, H, HD)
    probability_gradient = jnp.einsum(
        "grs,rys->gry", head_gradient, landmark_output, preferred_element_type=single_float
    )
    partial_mixing = jnp.einsum(
        "sqk,sqi->qki", weights_single, head_gradient, preferred_element_type=single_float
    )
    score_gradient = (
        probs_f
        * (probability_gradient - jnp.sum(probability_gradient * probs_f, axis=-1, keepdims=True))
    ).astype(jnp.bfloat16)
    query_head_gradient = jnp.einsum(
        "ile,elq->ilq", score_gradient, landmark_key_heads, preferred_element_type=single_float
    )
    partial_landmark_keys = jnp.einsum(
        "bis,bie->sie", score_gradient, query_heads, preferred_element_type=single_float
    )
    mixing_gradient = lax.psum(partial_mixing, "seq")
    inverse_gradient = jnp.einsum(
        "gxf,gtf->gxt", mixing_gradient, value_mixture, precision=highest_precision
    )
    mixed_gradient = jnp.einsum(
        "zrl,zro->zlo", inverse_matrix, mixing_gradient, precision=highest_precision
    )
    sum_gradient = mixed_gradient / value_total[..., None]
    grad_total = -jnp.sum(mixed_gradient * value_mixture, axis=-1) / value_total
    grad_expo = (
        jnp.einsum(
            "wsu,owu->wso",
            sum_gradient,
            value_heads.astype(single_float),
            precision=highest_precision,
        )
        + grad_total[..., None]
    )
    second_score_gradient = (exponent_values * grad_expo).astype(jnp.bfloat16)
    value_head_gradient = jnp.einsum(
        "bun,bul->nbl",
        exponent_landmark.astype(single_float),
        sum_gradient,
        precision=highest_precision,
    )
    partial_landmark_queries = jnp.einsum(
        "uvp,pux->vux", second_score_gradient, key_heads, preferred_element_type=single_float
    )
    key_head_gradient = jnp.einsum(
        "qfs,fqr->sqr",
        second_score_gradient,
        landmark_query_heads,
        preferred_element_type=single_float,
    )
    grad_kernel_a = inverse_pull(inverse_gradient)[0]
    direct_gradient = kernel_weights * (
        grad_kernel_a - jnp.sum(grad_kernel_a * kernel_weights, axis=-1, keepdims=True)
    )
    direct_query_part = jnp.einsum(
        "qyl,lqc->yqc",
        direct_gradient,
        landmark_key_heads.astype(single_float),
        precision=highest_precision,
    )
    direct_key_part = jnp.einsum(
        "ejs,jeu->seu",
        direct_gradient,
        landmark_query_heads.astype(single_float),
        precision=highest_precision,
    )
    local_marks = jnp.concatenate(
        [
            partial_landmark_queries.reshape(M, model_width),
            partial_landmark_keys.reshape(M, model_width),
        ],
        axis=1,
    )
    spread_marks = jnp.repeat(local_marks, per_mark, axis=0)
    own_marks = lax.psum_scatter(spread_marks, "seq", scatter_dimension=0, tiled=True)
    direct_all = jnp.concatenate(
        [direct_query_part.reshape(M, model_width), direct_key_part.reshape(M, model_width)], axis=1
    )
    own_total = own_marks + lax.dynamic_slice_in_dim(
        jnp.repeat(direct_all, per_mark, axis=0), seq_index * rows_dev, rows_dev, 0
    )
    per_token = jnp.repeat(own_total / seg_len, tok_count // rows_dev, axis=0)
    grad_queries = (
        query_head_gradient.reshape(tok_count, model_width) + per_token[:, :model_width]
    ).astype(jnp.bfloat16)
    grad_keys = (
        key_head_gradient.reshape(tok_count, model_width) + per_token[:, model_width:]
    ).astype(jnp.bfloat16)
    grad_ext = mask_rims(
        padded(grad_mixture, (("seq", 0),), radius), radius, keep_left, keep_right
    ).astype(single_float)
    grad_mix_f = grad_mixture.astype(single_float)

    def back_tap(tap_index, loop_carry):
        running, kernel_grad = loop_carry
        window = lax.dynamic_slice_in_dim(grad_ext, 2 * radius - tap_index, tok_count, 0)
        running = running + window * lax.dynamic_slice_in_dim(kernel_t, tap_index, 1, 0)
        source = lax.dynamic_slice_in_dim(ext_f, tap_index, tok_count, 0)
        kernel_grad = lax.dynamic_update_slice_in_dim(
            kernel_grad, jnp.sum(grad_mix_f * source, axis=0, keepdims=True), tap_index, 0
        )
        return (running, kernel_grad)

    conv_grad_v, grad_kernel_t = lax.fori_loop(
        0,
        KC,
        back_tap,
        (
            jnp.zeros((tok_count, model_width), single_float),
            jnp.zeros((KC, model_width), single_float),
        ),
    )
    grad_values = (value_head_gradient.reshape(tok_count, model_width) + conv_grad_v).astype(
        jnp.bfloat16
    )
    grad_weight_q = (
        jnp.einsum("td,te->de", normed, grad_queries, preferred_element_type=single_float)
        * qk_scale
    )
    grad_weight_k = (
        jnp.einsum("td,te->de", normed, grad_keys, preferred_element_type=single_float) * qk_scale
    )
    grad_weight_v = jnp.einsum(
        "td,te->de", normed, grad_values, preferred_element_type=single_float
    )
    grad_normed = (
        jnp.einsum("te,de->td", grad_queries, weight_q, preferred_element_type=single_float)
        + jnp.einsum("te,de->td", grad_keys, weight_k, preferred_element_type=single_float)
    ) * qk_scale + jnp.einsum(
        "te,de->td", grad_values, weight_v, preferred_element_type=single_float
    )
    grad_in_norm, grad_gain_one = norm_backward(grad_normed, normal_one, inv_one, gain_one)
    grad_input = grad_in_norm + grad_residual
    vector_grad = jnp.concatenate(
        [grad_gain_one[:, None], grad_gain_two[:, None], jnp.transpose(grad_kernel_t)], axis=1
    )
    attn_grad = jnp.stack([grad_weight_q, grad_weight_k, grad_weight_v, grad_weight_o])
    red_attn, red_up, red_down, red_vec = (
        lax.psum_scatter(attn_grad, ("seq", "rep"), scatter_dimension=1, tiled=True),
        lax.psum_scatter(grad_up, ("seq", "rep"), scatter_dimension=0, tiled=True),
        lax.psum_scatter(grad_down, ("seq", "rep"), scatter_dimension=0, tiled=True),
        lax.psum_scatter(vector_grad, ("seq", "rep"), scatter_dimension=0, tiled=True),
    )
    attn_new, attn_m_new, attn_v_new = adam_step(attn_w, red_attn, attn_m, attn_v, LEARN_RATE)
    up_new, up_m_new, up_v_new = adam_step(w_up, red_up, up_m, up_v, LEARN_RATE)
    down_new, down_m_new, down_v_new = adam_step(w_down, red_down, down_m, down_v, LEARN_RATE)
    vec_new, vec_m_new, vec_v_new = adam_step(vectors, red_vec, vec_m, vec_v, VECTOR_RATE)
    return (
        output.astype(jnp.bfloat16)[None],
        grad_input.astype(jnp.bfloat16)[None],
        attn_new,
        attn_m_new,
        attn_v_new,
        up_new,
        up_m_new,
        up_v_new,
        down_new,
        down_m_new,
        down_v_new,
        vec_new,
        vec_m_new,
        vec_v_new,
    )


def solution(mesh):
    placed = (
        P("rep", "seq", None),
        P("rep", "seq", None),
        P(None, ("seq", "rep"), None),
        P(("seq", "rep"), None),
        P(("seq", "rep"), None),
        P(("seq", "rep"), None),
        P(None, ("seq", "rep"), None),
        P(None, ("seq", "rep"), None),
        P(("seq", "rep"), None),
        P(("seq", "rep"), None),
        P(("seq", "rep"), None),
        P(("seq", "rep"), None),
        P(("seq", "rep"), None),
        P(("seq", "rep"), None),
    )
    return jax.shard_map(
        per_device,
        mesh=mesh,
        in_specs=placed,
        out_specs=(
            P("rep", "seq", None),
            P("rep", "seq", None),
            P(None, ("seq", "rep"), None),
            P(None, ("seq", "rep"), None),
            P(None, ("seq", "rep"), None),
            P(("seq", "rep"), None),
            P(("seq", "rep"), None),
            P(("seq", "rep"), None),
            P(("seq", "rep"), None),
            P(("seq", "rep"), None),
            P(("seq", "rep"), None),
            P(("seq", "rep"), None),
            P(("seq", "rep"), None),
            P(("seq", "rep"), None),
        ),
        check_vma=False,
    )
```

profile of v0, /device:TPU:0, one launch (start us, length us, event | category | flops | bytes accessed | tf_op | source)
XLA Modules:
  0.0 2048.6 jit_solution(17246099061319267935)
XLA Ops:
  9.8 44.1 %all_gather.18 = bf16[768,35]{1,0:T(8,128)(2,1)S(1)} all-gather(bf16[24,35]{1,0:T(8,128)(2,1)S(1)} %convert_element_type.136), channel_id=1, replica_groups=mesh['seq'=16,'rep'=2] {'seq','rep'}, dimensions={0}, use_global_device_ids=true | all-gather | bytes 55440 | tf_op jit(solution)/shard_map/all_gather | solution.py:123
  58.4 19.5 all-gather.6.cloned.1.call-done
  83.5 41.3 %all-gather = bf16[16,4,768]{2,1,0:T(4,128)(2,1)} all-gather(bf16[1,4,768]{2,1,0:T(4,128)(2,1)S(1)} %multiply_bitcast_fusion.3), channel_id=1, replica_groups=mesh['seq'=16,'rep'=2] {'seq'}, dimensions={0}, use_global_device_ids=true | all-gather | bytes 104448 | tf_op jit(solution)/shard_map/all_gather | solution.py:163
  165.2 36.3 %all-gather.1 = bf16[16,4,768]{2,1,0:T(4,128)(2,1)S(1)} all-gather(bf16[1,4,768]{2,1,0:T(4,128)(2,1)S(1)} %multiply_bitcast_fusion.2), channel_id=1, replica_groups=mesh['seq'=16,'rep'=2] {'seq'}, dimensions={0}, use_global_device_ids=true | all-gather | bytes 104448 | tf_op jit(solution)/shard_map/all_gather | solution.py:164
  244.0 39.9 %psum.22 = f32[12,64]{1,0:T(8,128)S(1)} all-reduce(f32[12,64]{1,0:T(8,128)S(1)} %get-tuple-element.395), channel_id=1, replica_groups=mesh['seq'=16,'rep'=2] {'seq'}, use_global_device_ids=true, to_apply=%region_10.0 | all-reduce | flops 768 | bytes 6144 | tf_op jit(solution)/shard_map/psum | solution.py:197
  289.8 296.1 %while.32 = (s32[]{:T(128)}, f32[2048,768]{1,0:T(8,128)}, f32[2080,768]{1,0:T(8,128)}, f32[33,768]{1,0:T(8,128)}, s32[]{:T(128)}, /*index=5*/s32[]{:T(128)}) while((s32[]{:T(128)}, f32[2048,768]{1,0:T(8,128)}, f32[2080,768]{1,0:T(8,128)}, f32[33,768]{1,0:T(8,128)}, s32[]{:T(128)}, /*index=5*/s32[]{:T(128)}) %tuple.111), condition=%wide.region_14.0_spmd.clone, body=%wide.region_13.0_spmd.clone.sunk | while | flops 4718595 | bytes 18883676 | solution.py:212
  297.8 8.3 select_add_fusion.4
  306.8 8.9 select_add_fusion.4
  316.5 8.4 select_add_fusion.4
  325.6 8.4 select_add_fusion.4
  379.7 8.2 select_add_fusion.4
  388.7 8.2 select_add_fusion.4
  397.7 8.2 select_add_fusion.4
  406.7 8.2 select_add_fusion.4
  415.7 8.2 select_add_fusion.4
  424.7 8.2 select_add_fusion.4
  433.7 8.2 select_add_fusion.4
  442.7 8.2 select_add_fusion.4
  614.8 69.7 %multiply_convert_fusion = (bf16[2048,3072]{1,0:T(8,128)(2,1)S(1)}, f32[2048,3072]{1,0:T(8,128)}, f32[2048,3072]{1,0:T(8,128)}) fusion(bf16[768,3072]{1,0:T(8,128)(2,1)} %all-gather.8.cloned.1.call-done, f32[2048,768]{1,0:T(8,128)} %copy-done.12, f32[768]{0:T(1024)S(1)} %copy-done.107, f32[2048]{0:T(1024)S(1)} %add_rsqrt_fusion, ...), kind=kOutput, calls=%fused_computation.10 | convolution fusion | flops 10078912512 | bytes 73944064 | tf_op jit(solution)/shard_map/dot_general | solution.py:217
  689.0 13.2 fusion.38
  702.3 131.5 %reduce-scatter.12.cloned.1.call-done = f32[96,768]{1,0:T(8,128)} async-done(((f32[3072,768]{1,0:T(8,128)}), f32[96,768]{1,0:T(8,128)}) %reduce-scatter.12.cloned.1.call-update) | async-done | bytes 294928 | tf_op jit(solution)/shard_map/reduce_scatter | solution.py:379
  837.4 62.4 %all-gather.10.cloned.1.call-done = bf16[3072,768]{1,0:T(8,128)(2,1)} async-done(((bf16[96,768]{1,0:T(8,128)(2,1)}), bf16[3072,768]{1,0:T(8,128)(2,1)}) %all-gather.10.cloned.1.call-update) | async-done | bytes 4718608 | tf_op jit(solution)/shard_map/all_gather | solution.py:122
  899.8 26.7 %add_convert_fusion = bf16[2048,3072]{1,0:T(8,128)(2,1)} fusion(f32[2048,3072]{1,0:T(8,128)} %get-tuple-element.377, f32[2048,3072]{1,0:T(8,128)} %get-tuple-element.401, bf16[3072,768]{1,0:T(8,128)(2,1)} %all-gather.10.cloned.1.call-done, bf16[1,2048,768]{2,1,0:T(8,128)(2,1)S(1)} %copy-done.62), kind=kOutput, calls=%fused_computation.9 | convolution fusion | flops 9751756800 | bytes 70778880 | tf_op jit(solution)/shard_map/td,fd->tf/dot_general | solution.py:223
  926.5 16.1 multiply_reduce_fusion.1
  989.2 447.7 %while.33 = (s32[]{:T(128)}, f32[2048,768]{1,0:T(8,128)}, f32[33,768]{1,0:T(8,128)}, f32[2080,768]{1,0:T(8,128)}, f32[33,768]{1,0:T(8,128)}, /*index=5*/f32[2080...) while((s32[]{:T(128)}, f32[2048,768]{1,0:T(8,128)}, ...), condition=%wide.region_27.28_spmd.clone, body=%wide.region_25.0_spmd.clone.sunk | while | flops 7863559 | bytes 82206960 | solution.py:342
  1001.9 9.0 select_add_fusion.5
  1015.5 9.0 select_add_fusion.5
  1029.1 9.0 select_add_fusion.5
  1042.7 9.0 select_add_fusion.5
  1056.2 9.0 select_add_fusion.5
  1069.8 9.0 select_add_fusion.5
  1083.4 9.0 select_add_fusion.5
  1097.0 9.0 select_add_fusion.5
  1110.6 9.0 select_add_fusion.5
  1124.3 9.0 select_add_fusion.5
  1138.0 9.0 select_add_fusion.5
  1151.7 9.0 select_add_fusion.5
  1165.3 9.0 select_add_fusion.5
  1179.0 9.0 select_add_fusion.5
  1192.7 9.0 select_add_fusion.5
  1206.4 9.0 select_add_fusion.5
  1219.9 9.0 select_add_fusion.5
  1233.4 9.0 select_add_fusion.5
  1246.9 9.0 select_add_fusion.5
  1260.5 9.0 select_add_fusion.5
  1274.0 9.0 select_add_fusion.5
  1287.5 9.0 select_add_fusion.5
  1301.0 9.0 select_add_fusion.5
  1314.5 9.0 select_add_fusion.5
  1328.2 9.0 select_add_fusion.5
  1341.9 9.0 select_add_fusion.5
  1355.6 9.0 select_add_fusion.5
  1369.3 9.0 select_add_fusion.5
  1383.0 9.0 select_add_fusion.5
  1396.6 9.0 select_add_fusion.5
  1410.3 9.0 select_add_fusion.5
  1424.0 9.0 select_add_fusion.5
  1511.8 102.4 %all-reduce.10.cloned.1.call-done = f32[64,1536]{0,1:T(8,128)} async-done(((f32[64,1536]{0,1:T(8,128)}), f32[64,1536]{0,1:T(8,128)}) %all-reduce.10.cloned.1.call-update) | async-done | bytes 393232
  1622.0 15.6 copy.281
  1663.5 18.1 fusion.107
  1707.8 16.7 fusion.41
  1724.5 32.9 %reduce-scatter.14.cloned.1.call-done = f32[24,35]{1,0:T(8,128)} async-done(((f32[768,35]{1,0:T(8,128)}), f32[24,35]{1,0:T(8,128)}) %reduce-scatter.14.cloned.1.call-update) | async-done | bytes 3376
  1758.7 139.3 %reduce-scatter.10.cloned.1.call-done = f32[24,3072]{1,0:T(8,128)} async-done(((f32[768,3072]{1,0:T(8,128)}), f32[24,3072]{1,0:T(8,128)}) %reduce-scatter.10.cloned.1.call-update) | async-done | bytes 294928 | tf_op jit(solution)/shard_map/reduce_scatter | solution.py:378
  1900.1 139.4 %reduce-scatter.8.cloned.1.call-done = f32[4,24,768]{2,1,0:T(8,128)} async-done(((f32[4,768,768]{2,1,0:T(8,128)}), f32[4,24,768]{2,1,0:T(8,128)}) %reduce-scatter.8.cloned.1.call-update) | async-done | bytes 294928 | tf_op jit(solution)/shard_map/reduce_scatter | solution.py:377
  (774 shorter events, 677.2 us)
Async XLA Ops:
  7.2 50.1 %copy-start.4 = (bf16[1,2048,768]{2,1,0:T(8,128)(2,1)S(1)}, bf16[1,2048,768]{2,1,0:T(8,128)(2,1)}, u32[]{:S(2)}) copy-start(bf16[1,2048,768]{2,1,0:T(8,128)(2,1)} %param.18) | copy-start | bytes 9437188
  7.2 70.7 %all-gather.6.cloned.1.call-start = ((), (), s32[]{:S(2)}) async-start(), calls=%async_computation.4 | async-start | bytes 4866048 | tf_op jit(solution)/shard_map/all_gather | solution.py:120
  9.1 576.9 %all-reduce.6.cloned.1.call-start = ((), (), s32[]{:S(2)}) async-start(), calls=%async_computation.5 | async-start | bytes 786432 | tf_op jit(solution)/shard_map/psum | solution.py:197
  57.3 81.4 %copy-start.94 = (f32[2048]{0:T(1024)}, f32[2048]{0:T(1024)S(1)}, u32[]{:S(2)}) copy-start(f32[2048]{0:T(1024)S(1)} %broadcast_multiply_fusion.5) | copy-start | bytes 24580
  58.4 80.3 %copy-start.101 = (f32[2048]{0:T(1024)}, f32[2048]{0:T(1024)S(1)}, u32[]{:S(2)}) copy-start(f32[2048]{0:T(1024)S(1)} %add_rsqrt_fusion.1) | copy-start | bytes 24580
  157.4 457.3 %all-gather.8.cloned.1.call-start = ((), (), s32[]{:S(2)}) async-start(), calls=%async_computation.6 | async-start | bytes 4866048 | tf_op jit(solution)/shard_map/all_gather | solution.py:121
  159.1 674.7 %reduce-scatter.12.cloned.1.call-start = ((), (), s32[]{:S(2)}) async-start(), calls=%async_computation.11 | async-start | bytes 9732096 | tf_op jit(solution)/shard_map/reduce_scatter | solution.py:379
  203.9 17.0 copy-start.13
  204.0 17.0 copy-start.81
  235.9 48.0 %collective-permute-start.1 = (bf16[16,768]{1,0:T(8,128)(2,1)}, bf16[16,768]{1,0:T(8,128)(2,1)}, u32[]{:S(2)}, u32[]{:S(2)}) collective-permute-start(bf16[16,768]{1,0:T(8,128)(2,1)} %get-tuple-element.385), channel_id=1, source_target_pairs={{2,0},{4,2},{6,4},{8,6},{10,8},{12,10},{14,12},{16,14},{18,16},{20... | collective-permute-start | bytes 73736 | tf_op jit(solution)/shard_map/ppermute | solution.py:33
  239.4 45.2 %collective-permute-start = (bf16[16,768]{1,0:T(8,128)(2,1)}, bf16[16,768]{1,0:T(8,128)(2,1)S(1)}, u32[]{:S(2)}, u32[]{:S(2)}) collective-permute-start(bf16[16,768]{1,0:T(8,128)(2,1)} %get-tuple-element.384), channel_id=1, source_target_pairs={{0,2},{2,4},{4,6},{6,8},{8,10},{10,12},{12,14},{14,16},{16,18},{18... | collective-permute-start | bytes 73736 | tf_op jit(solution)/shard_map/ppermute | solution.py:31
  283.9 302.1 %copy-start.91 = (f32[12,64]{1,0:T(8,128)}, f32[12,64]{1,0:T(8,128)S(1)}, u32[]{:S(2)}) copy-start(f32[12,64]{1,0:T(8,128)S(1)} %psum.22) | copy-start | bytes 9220
  289.8 297.9 %copy-start.79 = (f32[2048,12]{0,1:T(8,128)S(1)}, f32[2048,12]{0,1:T(8,128)}, u32[]{:S(2)}) copy-start(f32[2048,12]{0,1:T(8,128)} %get-tuple-element.397) | copy-start | bytes 294916
  611.3 331.4 %copy-start.96 = (f32[2048]{0:T(1024)}, f32[2048]{0:T(1024)S(1)}, u32[]{:S(2)}) copy-start(f32[2048]{0:T(1024)S(1)} %broadcast_multiply_fusion.4) | copy-start | bytes 24580
  614.7 328.0 %copy-start.103 = (f32[2048]{0:T(1024)}, f32[2048]{0:T(1024)S(1)}, u32[]{:S(2)}) copy-start(f32[2048]{0:T(1024)S(1)} %add_rsqrt_fusion) | copy-start | bytes 24580
  614.7 74.3 %copy-start.62 = (bf16[1,2048,768]{2,1,0:T(8,128)(2,1)S(1)}, bf16[1,2048,768]{2,1,0:T(8,128)(2,1)}, u32[]{:S(2)}) copy-start(bf16[1,2048,768]{2,1,0:T(8,128)(2,1)} %param.19) | copy-start | bytes 9437188
  702.2 131.6 %copy-start.86 = (f32[96,768]{1,0:T(8,128)S(1)}, f32[96,768]{1,0:T(8,128)}, u32[]{:S(2)}) copy-start(f32[96,768]{1,0:T(8,128)} %param.22) | copy-start | bytes 884740
  702.2 134.0 %copy-start.120 = (u32[32]{0:T(128)S(1)}, u32[32]{0:T(128)}, u32[]{:S(2)}) copy-start(u32[32]{0:T(128)} %constant.271) | copy-start | bytes 388
  702.2 197.6 %all-gather.10.cloned.1.call-start = ((), (), s32[]{:S(2)}) async-start(), calls=%async_computation.7 | async-start | bytes 4866048 | tf_op jit(solution)/shard_map/all_gather | solution.py:122
  836.1 600.9 %all-reduce.8.cloned.1.call-start = ((), (), s32[]{:S(2)}) async-start(), calls=%async_computation.8 | async-start | bytes 786432 | tf_op jit(solution)/shard_map/psum | solution.py:255
  968.6 16.5 collective-permute-start.3
  979.9 634.3 %all-reduce.10.cloned.1.call-start = ((), (), s32[]{:S(2)}) async-start(), calls=%async_computation.12 | async-start | bytes 1572864
  979.9 6.0 collective-permute-start.2
  989.1 447.8 %copy-start.92 = (f32[12,64]{1,0:T(8,128)S(1)}, f32[12,64]{1,0:T(8,128)}, u32[]{:S(2)}) copy-start(f32[12,64]{1,0:T(8,128)} %copy-done.91) | copy-start | bytes 9220
  989.1 447.8 %copy-start.114 = (f32[12,64,64]{2,1,0:T(8,128)S(1)}, f32[12,64,64]{2,1,0:T(8,128)}, u32[]{:S(2)}) copy-start(f32[12,64,64]{2,1,0:T(8,128)} %all-reduce.6.cloned.1.call-done) | copy-start | bytes 589828
  989.1 449.8 %copy-start.61 = (f32[12,64,64]{2,1,0:T(8,128)S(1)}, f32[12,64,64]{2,1,0:T(8,128)}, u32[]{:S(2)}) copy-start(f32[12,64,64]{2,1,0:T(8,128)} %convolution_subtract_fusion) | copy-start | bytes 589828
  989.1 450.5 %copy-start.36 = (f32[12,64,64]{2,1,0:T(8,128)S(1)}, f32[12,64,64]{2,1,0:T(8,128)}, u32[]{:S(2)}) copy-start(f32[12,64,64]{2,1,0:T(8,128)} %copy-done.34) | copy-start | bytes 589828
  989.2 451.4 %copy-start.50 = (f32[12,64,64]{2,1,0:T(8,128)S(1)}, f32[12,64,64]{2,1,0:T(8,128)}, u32[]{:S(2)}) copy-start(f32[12,64,64]{2,1,0:T(8,128)} %copy-done.49) | copy-start | bytes 589828
  989.2 452.1 %copy-start.26 = (f32[12,64,64]{2,1,0:T(8,128)S(1)}, f32[12,64,64]{2,1,0:T(8,128)}, u32[]{:S(2)}) copy-start(f32[12,64,64]{2,1,0:T(8,128)} %copy-done.25) | copy-start | bytes 589828
  989.2 453.0 %copy-start.38 = (f32[64,64]{1,0:T(8,128)S(1)}, f32[64,64]{1,0:T(8,128)}, u32[]{:S(2)}) copy-start(f32[64,64]{1,0:T(8,128)} %get-tuple-element.414) | copy-start | bytes 49156
  1001.9 10.6 copy-start.1
  1015.5 10.6 copy-start.1
  1029.1 10.6 copy-start.1
  1042.7 10.5 copy-start.1
  1056.2 10.6 copy-start.1
  1069.8 10.6 copy-start.1
  1083.4 10.5 copy-start.1
  1097.0 10.5 copy-start.1
  1110.6 10.5 copy-start.1
  1165.3 10.5 copy-start.1
  1179.0 10.5 copy-start.1
  1192.7 10.5 copy-start.1
  1206.3 10.5 copy-start.1
  1274.0 10.5 copy-start.1
  1287.5 10.5 copy-start.1
  1301.0 10.5 copy-start.1
  1314.5 10.5 copy-start.1
  1328.2 10.5 copy-start.1
  1501.1 256.3 %reduce-scatter.14.cloned.1.call-start = ((), (), s32[]{:S(2)}) async-start(), calls=%async_computation.13 | async-start | bytes 405504
  1508.2 106.0 %copy-start.84 = (f32[12,64,64]{2,1,0:T(8,128)S(1)}, f32[12,64,64]{2,1,0:T(8,128)}, u32[]{:S(2)}) copy-start(f32[12,64,64]{2,1,0:T(8,128)} %fusion.100) | copy-start | bytes 589828
  1508.2 106.0 %copy-start.85 = (f32[12,64,64]{2,1,0:T(8,128)S(1)}, f32[12,64,64]{2,1,0:T(8,128)}, u32[]{:S(2)}) copy-start(f32[12,64,64]{2,1,0:T(8,128)} %fusion.101) | copy-start | bytes 589828
  1615.8 21.8 %slice-start.2 = ((s8[6291456]{0:T(1024)(128)(4,1)}), s8[4194304]{0:T(1024)(128)(4,1)S(1)}, s32[]{:S(2)}) async-start(s8[6291456]{0:T(1024)(128)(4,1)} %bitcast.349), calls=%async_computation.16 | async-start | bytes 8388608
  1622.0 15.6 slice-start.3
  1663.4 234.7 %reduce-scatter.10.cloned.1.call-start = ((), (), s32[]{:S(2)}) async-start(), calls=%async_computation.10 | async-start | bytes 9732096 | tf_op jit(solution)/shard_map/reduce_scatter | solution.py:378
  1681.6 357.9 %reduce-scatter.8.cloned.1.call-start = ((), (), s32[]{:S(2)}) async-start(), calls=%async_computation.9 | async-start | bytes 9732096 | tf_op jit(solution)/shard_map/reduce_scatter | solution.py:377
  1707.7 49.7 %copy-start.100 = (f32[24,35]{1,0:T(8,128)S(1)}, f32[24,35]{1,0:T(8,128)}, u32[]{:S(2)}) copy-start(f32[24,35]{1,0:T(8,128)} %param.23) | copy-start | bytes 10084
  1707.7 49.7 %copy-start.110 = (f32[24,35]{1,0:T(8,128)S(1)}, f32[24,35]{1,0:T(8,128)}, u32[]{:S(2)}) copy-start(f32[24,35]{1,0:T(8,128)} %param.30) | copy-start | bytes 10084
  1707.7 49.7 %copy-start.111 = (f32[24,35]{1,0:T(8,128)S(1)}, f32[24,35]{1,0:T(8,128)}, u32[]{:S(2)}) copy-start(f32[24,35]{1,0:T(8,128)} %param.31) | copy-start | bytes 10084
  1707.7 190.3 %copy-start.77 = (f32[24,3072]{1,0:T(8,128)S(1)}, f32[24,3072]{1,0:T(8,128)}, u32[]{:S(2)}) copy-start(f32[24,3072]{1,0:T(8,128)} %param.21) | copy-start | bytes 884740
  1707.7 190.3 %copy-start.87 = (f32[24,3072]{1,0:T(8,128)S(1)}, f32[24,3072]{1,0:T(8,128)}, u32[]{:S(2)}) copy-start(f32[24,3072]{1,0:T(8,128)} %param.26) | copy-start | bytes 884740
  1707.8 190.3 %copy-start.88 = (f32[24,3072]{1,0:T(8,128)S(1)}, f32[24,3072]{1,0:T(8,128)}, u32[]{:S(2)}) copy-start(f32[24,3072]{1,0:T(8,128)} %param.27) | copy-start | bytes 884740
  1707.8 331.8 %copy-start.78 = (f32[4,24,768]{2,1,0:T(8,128)S(1)}, f32[4,24,768]{2,1,0:T(8,128)}, u32[]{:S(2)}) copy-start(f32[4,24,768]{2,1,0:T(8,128)} %param.20) | copy-start | bytes 884740
  1707.8 331.8 %copy-start.89 = (f32[4,24,768]{2,1,0:T(8,128)S(1)}, f32[4,24,768]{2,1,0:T(8,128)}, u32[]{:S(2)}) copy-start(f32[4,24,768]{2,1,0:T(8,128)} %param.24) | copy-start | bytes 884740
  1707.8 331.7 %copy-start.90 = (f32[4,24,768]{2,1,0:T(8,128)S(1)}, f32[4,24,768]{2,1,0:T(8,128)}, u32[]{:S(2)}) copy-start(f32[4,24,768]{2,1,0:T(8,128)} %param.25) | copy-start | bytes 884740
  (142 other events, 973.2 us)
Sparse Core Ops, SparseCore 0:
  11.5 66.3 all-gather.5
  157.5 103.8 all-reduce.5
  265.3 62.6 all-gather.7
  702.4 131.4 reduce-scatter.11
  837.1 62.6 all-gather.9
  980.0 108.7 all-reduce.7
  1501.2 112.9 all-reduce.9
  1663.5 93.8 reduce-scatter.13
  1763.3 134.7 reduce-scatter.9
  1904.8 134.6 reduce-scatter.7
where the time goes:
time: 2060 us; the launch traced here: 2050 us
  other arithmetic  669 us (32%)
  waiting for transfers between devices  629 us (31%)
  matrix products  336 us (16%)
  local copies, waits for them, and re-layouts  223 us (11%)
  blocking collectives  162 us (8%)
    add x33, other arithmetic, back_tap(): running + window * lax.dynamic_slice_in_dim(kernel_t, tap_index, 1, 0)  295 us
    add x33, other arithmetic, conv_tap(): running + window * lax.dynamic_slice_in_dim(kernel_t, tap_index, 1, 0)  271 us
    reduce_scatter x1, waiting for transfers between devices, per_device(): lax.psum_scatter(attn_grad, ('seq', 'rep'), scatter_dimension=1, tiled=True)  139 us
    reduce_scatter x1, waiting for transfers between devices, per_device(): lax.psum_scatter(grad_up, ('seq', 'rep'), scatter_dimension=0, tiled=True)  139 us
    unnamed x12, waiting for transfers between devices  135 us
    reduce_scatter x1, waiting for transfers between devices, per_device(): lax.psum_scatter(grad_down, ('seq', 'rep'), scatter_dimension=0, tiled=True)  132 us
    dot_general x1, matrix products, per_device(): pre_act = jnp.dot(normed_two, up_full, preferred_element_type=single_float)  69.7 us
    all_gather x1, waiting for transfers between devices, per_device(): lax.all_gather(w_down.astype(jnp.bfloat16), ('seq', 'rep'), axis=0, tiled...  62.4 us
  transfers between devices with their start and end apart: 14, of which 8 were waited for; matrix products, arithmetic and copies ran while one was open for 42% of the time, Pallas kernels for 0%

commit v1 on v0

v1 whole, which is shorter than its diff:
```python
import functools

import jax
import jax.numpy as jnp
from jax import lax
from jax.experimental import pallas as pl
from jax.experimental.pallas import tpu as pltpu
from jax.sharding import PartitionSpec as P

H = 12
HD = 64
M = 64
KC = 33
NSITER = 6
STEP = 10
EPS_NORM = 1e-05
BETA_ONE = 0.9
BETA_TWO = 0.999
ADAM_EPS = 1e-08
LEARN_RATE = 0.03
VECTOR_RATE = 0.15
DECAY_RATE = 0.1

F32 = jnp.float32
BF16 = jnp.bfloat16
GROUP = 256
NG = 3
RAD = 16
QK_SCALE = HD ** (-0.25)
HI = lax.Precision.HIGHEST
VMEM_LIMIT = 58 * 1024 * 1024


def dot(a, b, precision=None):
    return lax.dot_general(a, b, (((1,), (0,)), ((), ())), precision=precision, preferred_element_type=F32)


def dot_nt(a, b, precision=None):
    return lax.dot_general(a, b, (((1,), (1,)), ((), ())), precision=precision, preferred_element_type=F32)


def dot_tn(a, b, precision=None):
    return lax.dot_general(a, b, (((0,), (0,)), ((), ())), precision=precision, preferred_element_type=F32)


def head_mask(shape=(GROUP, GROUP)):
    rows = lax.broadcasted_iota(jnp.int32, shape, 0)
    cols = lax.broadcasted_iota(jnp.int32, shape, 1)
    return lax.shift_right_logical(rows, 6) == lax.shift_right_logical(cols, 6)


def spread(wide):
    tall = jnp.concatenate([wide, wide, wide, wide], axis=0)
    return jnp.where(head_mask(), tall, jnp.zeros_like(tall))


def collect(full):
    kept = jnp.where(head_mask(), full, jnp.zeros_like(full))
    return (kept[0:64] + kept[64:128]) + (kept[128:192] + kept[192:256])


def flip(wide):
    turned = jnp.transpose(spread(wide))
    return (turned[0:64] + turned[64:128]) + (turned[128:192] + turned[192:256])


def gs(g):
    return slice(g * GROUP, (g + 1) * GROUP)


def half_reduce(x, op, init):
    parts = []
    for c in range(x.shape[1] // 128):
        col = x[:, c * 128 : (c + 1) * 128]
        low = lax.broadcasted_iota(jnp.int32, col.shape, 1) < 64
        a = op(jnp.where(low, col, init), axis=1, keepdims=True)
        b = op(jnp.where(low, init, col), axis=1, keepdims=True)
        parts.append(jnp.where(low, a, b))
    return jnp.concatenate(parts, axis=1)


def normalize(x):
    center = x - jnp.mean(x, axis=-1, keepdims=True)
    inv = lax.rsqrt(jnp.mean(center * center, axis=-1, keepdims=True) + EPS_NORM)
    return center * inv, inv


def norm_back(up, normal, inv, gain):
    scaled = up * gain
    centered = scaled - jnp.mean(scaled, axis=-1, keepdims=True)
    return inv * (centered - normal * jnp.mean(scaled * normal, axis=-1, keepdims=True))


def rowsum8(x):
    return jnp.sum(x.reshape(x.shape[0] // 8, 8, x.shape[1]), axis=0)


def gelu_parts(a):
    z = jnp.abs(a)
    t = 1.0 / (1.0 + (0.3275911 * 0.7071067811865476) * z)
    e = jnp.exp(-0.5 * a * a)
    poly = t * (0.127414796 + t * (-0.142248368 + t * (0.7107068705 + t * (-0.7265760135 + t * 0.5307027145))))
    tail = poly * e
    phi = jnp.where(a >= 0, 1.0 - tail, tail)
    return a * phi, phi + a * (e * 0.3989422804014327)


def whole(shape):
    zeros = (0,) * len(shape)
    return pl.BlockSpec(shape, lambda i: zeros, pipeline_mode=pl.Buffered(1))


def rows(tile, width):
    return pl.BlockSpec((tile, width), lambda i: (i, 0))


def sds(shape, dtype):
    return jax.ShapeDtypeStruct(shape, dtype)


def params():
    return pltpu.CompilerParams(dimension_semantics=("arbitrary",), vmem_limit_bytes=VMEM_LIMIT)


def project_kernel(x_ref, w_ref, gain_ref, h_ref, q_ref, k_ref, v_ref, mean_ref):
    i = pl.program_id(0)
    x = x_ref[...].astype(F32)
    normal, _ = normalize(x)
    h = (normal * gain_ref[0:1, :]).astype(BF16)
    h_ref[...] = h
    q = (dot(h, w_ref[0]) * QK_SCALE).astype(BF16)
    q_ref[...] = q
    mean_ref[pl.ds(i, 1), :] = jnp.mean(q.astype(F32), axis=0, keepdims=True)
    k = (dot(h, w_ref[1]) * QK_SCALE).astype(BF16)
    k_ref[...] = k
    mean_ref[pl.ds(i + 4, 1), :] = jnp.mean(k.astype(F32), axis=0, keepdims=True)
    v_ref[...] = dot(h, w_ref[2]).astype(BF16)


def project(x, w_attn, gains):
    t, d = x.shape
    tile = t // 4
    return pl.pallas_call(
        project_kernel,
        grid=(4,),
        in_specs=[rows(tile, d), whole(w_attn.shape), whole(gains.shape)],
        out_specs=[rows(tile, d)] * 4 + [whole((8, d))],
        out_shape=[sds((t, d), BF16)] * 4 + [sds((8, d), F32)],
        compiler_params=params(),
        name="project",
    )(x, w_attn, gains)


def pinv_kernel(mq_ref, mk_ref, a_ref, p_ref, z_ref, az_ref, t2_ref, t3_ref):
    eye = jnp.where(
        (lax.broadcasted_iota(jnp.int32, (M, GROUP), 1) & 63) == lax.broadcasted_iota(jnp.int32, (M, GROUP), 0),
        1.0,
        0.0,
    )
    ones = jnp.where(head_mask(), 1.0, 0.0)
    a, z = [], []
    for g in range(NG):
        s = dot_nt(mq_ref[:, gs(g)], spread(mk_ref[:, gs(g)]))
        e = jnp.exp(s - half_reduce(s, jnp.max, -jnp.inf))
        ag = e / half_reduce(e, jnp.sum, 0.0)
        a_ref[:, gs(g)] = ag
        col = jnp.sum(ag, axis=0, keepdims=True)
        sq = dot(jnp.broadcast_to(col * col, (8, GROUP)), ones, HI)[0:1]
        a.append(ag)
        z.append(flip(ag) / jnp.sqrt(sq))
    for it in range(NSITER):
        for g in range(NG):
            z_ref[it, :, gs(g)] = z[g]
        az = [dot(a[g], spread(z[g]), HI) for g in range(NG)]
        t1 = [7.0 * eye - az[g] for g in range(NG)]
        t2 = [15.0 * eye - dot(az[g], spread(t1[g]), HI) for g in range(NG)]
        t3 = [13.0 * eye - dot(az[g], spread(t2[g]), HI) for g in range(NG)]
        z = [0.25 * dot(z[g], spread(t3[g]), HI) for g in range(NG)]
        for g in range(NG):
            az_ref[it, :, gs(g)] = az[g]
            t2_ref[it, :, gs(g)] = t2[g]
            t3_ref[it, :, gs(g)] = t3[g]
    for g in range(NG):
        p_ref[:, gs(g)] = z[g]


def pinv(mq, mk):
    d = mq.shape[1]
    vm = pl.BlockSpec(memory_space=pltpu.VMEM)
    return pl.pallas_call(
        pinv_kernel,
        in_specs=[vm] * 2,
        out_specs=[vm] * 6,
        out_shape=[sds((M, d), F32)] * 2 + [sds((NSITER, M, d), F32)] * 4,
        compiler_params=pltpu.CompilerParams(vmem_limit_bytes=VMEM_LIMIT),
        name="pinv",
    )(mq, mk)


def pinv_back_kernel(mq_ref, mk_ref, a_ref, p_ref, z_ref, az_ref, t2_ref, t3_ref, gw_ref, u_ref, zt_ref, dq_ref, dk_ref, *, inv_n):
    eye = jnp.where(
        (lax.broadcasted_iota(jnp.int32, (M, GROUP), 1) & 63) == lax.broadcasted_iota(jnp.int32, (M, GROUP), 0),
        1.0,
        0.0,
    )
    ones = jnp.where(head_mask(), 1.0, 0.0)
    R = range(NG)
    a = [a_ref[:, gs(g)] for g in R]
    gz = []
    for g in R:
        bv = u_ref[:, gs(g)] / widen(zt_ref[...], g)
        gz.append(flip(dot_nt(gw_ref[:, gs(g)], spread(bv), HI)))
    da = [jnp.zeros((M, GROUP), F32) for _ in R]
    for it in reversed(range(NSITER)):
        z = [z_ref[it, :, gs(g)] for g in R]
        az = [az_ref[it, :, gs(g)] for g in R]
        t2 = [t2_ref[it, :, gs(g)] for g in R]
        t3 = [t3_ref[it, :, gs(g)] for g in R]
        bg = [spread(0.25 * gz[g]) for g in R]
        d3 = [dot(0.25 * gz[g], spread(z[g]), HI) for g in R]
        baz = [spread(az[g]) for g in R]
        d2 = [-dot(d3[g], baz[g], HI) for g in R]
        d1 = [-dot(d2[g], baz[g], HI) for g in R]
        daz = [
            -dot(t2[g], spread(d3[g]), HI) - dot(7.0 * eye - az[g], spread(d2[g]), HI) - d1[g] for g in R
        ]
        da = [da[g] + dot(z[g], spread(daz[g]), HI) for g in R]
        gz = [dot(t3[g], bg[g], HI) + dot(daz[g], spread(a[g]), HI) for g in R]
    for g in R:
        col = jnp.sum(a[g], axis=0, keepdims=True)
        sq = dot(jnp.broadcast_to(col * col, (8, GROUP)), ones, HI)[0:1]
        bound = jnp.sqrt(sq)
        tot = jnp.sum(gz[g] * a[g], axis=0, keepdims=True)
        tot = dot(jnp.broadcast_to(tot, (8, GROUP)), ones, HI)[0:1]
        full = flip(da[g]) + gz[g] / bound - (tot / (bound * bound * bound)) * col
        ds = a[g] * (full - half_reduce(full * a[g], jnp.sum, 0.0))
        dq_ref[:, gs(g)] = dot(ds, spread(mk_ref[:, gs(g)].astype(F32)), HI) * inv_n
        dk_ref[:, gs(g)] = dot(flip(ds), spread(mq_ref[:, gs(g)].astype(F32)), HI) * inv_n


def pinv_back(mq, mk, saved, gw, u, zt, inv_n):
    d = mq.shape[1]
    vm = pl.BlockSpec(memory_space=pltpu.VMEM)
    return pl.pallas_call(
        functools.partial(pinv_back_kernel, inv_n=inv_n),
        in_specs=[vm] * 11,
        out_specs=[vm] * 2,
        out_shape=[sds((M, d), F32)] * 2,
        compiler_params=pltpu.CompilerParams(vmem_limit_bytes=VMEM_LIMIT),
        name="pinv_back",
    )(mq, mk, *saved, gw, u, zt)


def widen(zt, g):
    return jnp.concatenate(
        [jnp.broadcast_to(zt[:, h : h + 1], (M, HD)) for h in range(4 * g, 4 * g + 4)], axis=1
    )


def attend_kernel(q_ref, k_ref, v_ref, mq_ref, mk_ref, f_ref, e_ref, u_ref, zt_ref, uacc, zacc):
    i = pl.program_id(0)
    n = pl.num_programs(0)

    @pl.when(i == 0)
    def _():
        uacc[...] = jnp.zeros_like(uacc)
        zacc[...] = jnp.zeros_like(zacc)

    ones_bd = jnp.where(head_mask(), 1.0, 0.0).astype(BF16)
    ones = jnp.ones((q_ref.shape[0], 128), BF16)
    for g in range(NG):
        s = dot_nt(q_ref[:, gs(g)], spread(mk_ref[:, gs(g)]))
        ex = jnp.exp(s - half_reduce(s, jnp.max, -jnp.inf))
        den = dot(ex.astype(BF16), ones_bd)
        f_ref[:, gs(g)] = (ex / den).astype(BF16)
        e = jnp.exp(dot_nt(k_ref[:, gs(g)], spread(mq_ref[:, gs(g)]))).astype(BF16)
        e_ref[:, gs(g)] = e
        uacc[g] += dot_tn(e, v_ref[:, gs(g)])
        zacc[g] += dot_tn(e, ones)

    @pl.when(i == n - 1)
    def _():
        lane = lax.broadcasted_iota(jnp.int32, (M, 128), 1)
        total = jnp.zeros((M, 128), F32)
        for g in range(NG):
            u_ref[:, gs(g)] = collect(uacc[g])
            for h in range(4):
                total = total + jnp.where(lane == 4 * g + h, zacc[g, h * 64 : h * 64 + 64, :], 0.0)
        zt_ref[...] = total


def attend(q, k, v, mq, mk):
    t, d = q.shape
    tile = t // 4
    return pl.pallas_call(
        attend_kernel,
        grid=(4,),
        in_specs=[rows(tile, d)] * 3 + [whole((M, d))] * 2,
        out_specs=[rows(tile, d)] * 2 + [whole((M, d)), whole((M, 128))],
        out_shape=[sds((t, d), BF16)] * 2 + [sds((M, d), F32), sds((M, 128), F32)],
        scratch_shapes=[pltpu.VMEM((NG, GROUP, GROUP), F32), pltpu.VMEM((NG, GROUP, 128), F32)],
        compiler_params=params(),
        name="attend",
    )(q, k, v, mq, mk)


CHUNK = 64


def fill_extended(ext, body_ref, left_ref, right_ref, i, n, tile):
    start = pl.multiple_of(i * tile, tile)
    for c in range(ext.shape[0]):
        cols = slice(c * 128, (c + 1) * 128)
        ext[c, RAD : RAD + tile, :] = body_ref[pl.ds(start, tile), cols].astype(F32)
        before = body_ref[pl.ds(pl.multiple_of(jnp.maximum(start - RAD, 0), RAD), RAD), cols].astype(F32)
        ext[c, 0:RAD, :] = jnp.where(i == 0, left_ref[:, cols].astype(F32), before)
        last = body_ref.shape[0] - RAD
        after = body_ref[pl.ds(pl.multiple_of(jnp.minimum(start + tile, last), RAD), RAD), cols].astype(F32)
        ext[c, RAD + tile : 2 * RAD + tile, :] = jnp.where(i == n - 1, right_ref[:, cols].astype(F32), after)


def conv_forward(ext, tap_ref, out, tile):
    def step(r, _):
        base = pl.multiple_of(r * CHUNK, CHUNK)
        for c in range(ext.shape[0]):
            cols = slice(c * 128, (c + 1) * 128)
            acc = jnp.zeros((CHUNK, 128), F32)
            for b in range(8):
                reach = 4 if b == 0 else 3
                win = ext[c, pl.ds(base + b, CHUNK + 8 * reach), :]
                for m in range(reach + 1):
                    o = 8 * m + b
                    acc = acc + tap_ref[o : o + 1, cols] * win[8 * m : 8 * m + CHUNK]
            out[c, pl.ds(base, CHUNK), :] = acc
        return 0

    lax.fori_loop(0, tile // CHUNK, step, 0)


def conv_backward(vext, gext, tap_ref, out, tapacc, tile):
    def step(r, _):
        base = pl.multiple_of(r * CHUNK, CHUNK)
        for c in range(vext.shape[0]):
            cols = slice(c * 128, (c + 1) * 128)
            acc = jnp.zeros((CHUNK, 128), F32)
            here = gext[c, pl.ds(base + RAD, CHUNK), :]
            for b in range(8):
                reach = 4 if b == 0 else 3
                win = gext[c, pl.ds(base + b, CHUNK + 8 * reach), :]
                for m in range(reach + 1):
                    o = KC - 1 - (8 * m + b)
                    acc = acc + tap_ref[o : o + 1, cols] * win[8 * m : 8 * m + CHUNK]
                win = vext[c, pl.ds(base + b, CHUNK + 8 * reach), :]
                for m in range(reach + 1):
                    o = 8 * m + b
                    tapacc[o, :, cols] += rowsum8(here * win[8 * m : 8 * m + CHUNK])
            out[c, pl.ds(base, CHUNK), :] = acc
        return 0

    lax.fori_loop(0, tile // CHUNK, step, 0)


FCHUNK = 512


def middle_kernel(
    x_ref, dy_ref, f_ref, q_ref, v_ref, left_ref, right_ref, wo_ref, up_ref, down_ref, gain_ref, tap_ref,
    mk_ref, u_ref, zt_ref, p_ref,
    out_ref, act_ref, da_ref, h2_ref, mix_ref, dx_ref, dmix_ref, dqf_ref, gw_ref, dkt_ref, dg_ref,
    ext, conv, wbd, gwacc, dktacc, dgacc, oacc, hacc,
):
    i = pl.program_id(0)
    n = pl.num_programs(0)
    tile = x_ref.shape[0]
    d = x_ref.shape[1]

    @pl.when(i == 0)
    def _():
        gwacc[...] = jnp.zeros_like(gwacc)
        dktacc[...] = jnp.zeros_like(dktacc)
        dgacc[...] = jnp.zeros_like(dgacc)
        for g in range(NG):
            bv = u_ref[:, gs(g)] / widen(zt_ref[...], g)
            wbd[g] = spread(dot(p_ref[:, gs(g)], spread(bv), HI)).astype(BF16)

    fill_extended(ext, v_ref, left_ref, right_ref, i, n, tile)
    conv_forward(ext, tap_ref, conv, tile)
    for g in range(NG):
        att = dot(f_ref[:, gs(g)], wbd[g])
        for s in range(2):
            c = 2 * g + s
            mix_ref[:, c * 128 : (c + 1) * 128] = (att[:, s * 128 : (s + 1) * 128] + conv[c]).astype(BF16)
    x1 = x_ref[...].astype(F32) + dot(mix_ref[...], wo_ref[...])
    normal, inv = normalize(x1)
    gain = gain_ref[1:2, :]
    h2 = (normal * gain).astype(BF16)
    h2_ref[...] = h2
    dy = dy_ref[...]
    ff = up_ref.shape[1]
    for j in range(ff // FCHUNK):
        cols = slice(j * FCHUNK, (j + 1) * FCHUNK)
        a = dot(h2, up_ref[:, cols])
        act, slope = gelu_parts(a)
        act = act.astype(BF16)
        act_ref[:, cols] = act
        da = (dot_nt(dy, down_ref[cols, :]) * slope).astype(BF16)
        da_ref[:, cols] = da
        o = dot(act, down_ref[cols, :])
        h = dot_nt(da, up_ref[:, cols])
        if j == 0:
            oacc[...] = o
            hacc[...] = h
        else:
            oacc[...] += o
            hacc[...] += h
    out_ref[...] = (x1 + oacc[...]).astype(BF16)
    dh2 = hacc[...]
    dgacc[...] += rowsum8(dh2 * normal)
    dx1 = norm_back(dh2, normal, inv, gain) + dy.astype(F32)
    do = dx1.astype(BF16)
    dx_ref[...] = do
    dmix = dot_nt(do, wo_ref[...]).astype(BF16)
    dmix_ref[...] = dmix
    ones_bd = jnp.where(head_mask(), 1.0, 0.0).astype(BF16)
    for g in range(NG):
        dm = dmix[:, gs(g)]
        f = f_ref[:, gs(g)]
        df = dot_nt(dm, wbd[g])
        gwacc[g] += dot_tn(f, dm)
        ff32 = f.astype(F32)
        prod = df * ff32
        hi = prod.astype(BF16)
        lo = (prod - hi.astype(F32)).astype(BF16)
        ds = (ff32 * (df - (dot(hi, ones_bd) + dot(lo, ones_bd)))).astype(BF16)
        dqf_ref[:, gs(g)] = dot(ds, spread(mk_ref[:, gs(g)])).astype(BF16)
        dktacc[g] += dot_tn(ds, q_ref[:, gs(g)])

    @pl.when(i == n - 1)
    def _():
        for g in range(NG):
            gw_ref[:, gs(g)] = collect(gwacc[g])
            dkt_ref[:, gs(g)] = collect(dktacc[g])
        dg_ref[...] = jnp.broadcast_to(jnp.sum(dgacc[...], axis=0, keepdims=True), (8, d))


def middle(x, dy, f, q, v, left, right, wo, up, down, gains, taps, mk, u, zt, p):
    t, d = x.shape
    ff = up.shape[1]
    tile = 256
    r = rows(tile, d)
    rf = rows(tile, ff)
    return pl.pallas_call(
        middle_kernel,
        grid=(t // tile,),
        in_specs=[r, r, r, r, whole((t, d)), whole((RAD, d)), whole((RAD, d)), whole((d, d)), whole(up.shape), whole(down.shape),
                  whole(gains.shape), whole(taps.shape), whole((M, d)), whole((M, d)), whole((M, 128)), whole((M, d))],
        out_specs=[r, rf, rf, r, r, r, r, r, whole((M, d)), whole((M, d)), whole((8, d))],
        out_shape=[sds((t, d), BF16), sds((t, ff), BF16), sds((t, ff), BF16)] + [sds((t, d), BF16)] * 5
        + [sds((M, d), F32), sds((M, d), F32), sds((8, d), F32)],
        scratch_shapes=[
            pltpu.VMEM((6, tile + 2 * RAD, 128), F32),
            pltpu.VMEM((6, tile, 128), F32),
            pltpu.VMEM((NG, GROUP, GROUP), BF16),
            pltpu.VMEM((NG, GROUP, GROUP), F32),
            pltpu.VMEM((NG, GROUP, GROUP), F32),
            pltpu.VMEM((8, d), F32),
            pltpu.VMEM((tile, d), F32),
            pltpu.VMEM((tile, d), F32),
        ],
        compiler_params=params(),
        name="middle",
    )(x, dy, f, q, v, left, right, wo, up, down, gains, taps, mk, u, zt, p)


def back_kernel(
    e_ref, k_ref, v_ref, vl_ref, vr_ref, g_ref, gl_ref, gr_ref, tap_ref, mq_ref, u_ref, zt_ref, p_ref, gw_ref,
    dv_ref, dkb_ref, dqt_ref, dtap_ref,
    vext, gext, conv, tapacc, dubd, rowadd, dqtacc,
):
    i = pl.program_id(0)
    n = pl.num_programs(0)
    tile = e_ref.shape[0]

    @pl.when(i == 0)
    def _():
        dqtacc[...] = jnp.zeros_like(dqtacc)
        tapacc[...] = jnp.zeros_like(tapacc)
        for g in range(NG):
            z = widen(zt_ref[...], g)
            bv = u_ref[:, gs(g)] / z
            dbv = dot(flip(p_ref[:, gs(g)]), spread(gw_ref[:, gs(g)]), HI)
            dubd[g] = spread(dbv / z).astype(BF16)
            rowadd[g] = dot_nt(jnp.ones((8, GROUP), F32), spread(dbv * bv / z), HI)

    fill_extended(vext, v_ref, vl_ref, vr_ref, i, n, tile)
    fill_extended(gext, g_ref, gl_ref, gr_ref, i, n, tile)
    conv_backward(vext, gext, tap_ref, conv, tapacc, tile)
    here = pl.ds(pl.multiple_of(i * tile, tile), tile)
    for g in range(NG):
        e = e_ref[:, gs(g)]
        de = dot_nt(v_ref[here, gs(g)], dubd[g]) - rowadd[g, 0:1, :]
        ds = (e.astype(F32) * de).astype(BF16)
        dvb = dot(e, dubd[g])
        for s in range(2):
            c = 2 * g + s
            dv_ref[:, c * 128 : (c + 1) * 128] = (dvb[:, s * 128 : (s + 1) * 128] + conv[c]).astype(BF16)
        dkb_ref[:, gs(g)] = dot(ds, spread(mq_ref[:, gs(g)])).astype(BF16)
        dqtacc[g] += dot_tn(ds, k_ref[:, gs(g)])

    @pl.when(i == n - 1)
    def _():
        for g in range(NG):
            dqt_ref[:, gs(g)] = collect(dqtacc[g])
        dtap_ref[...] = jnp.sum(tapacc[...], axis=1)


def back(e, k, v, vl, vr, dmix, gl, gr, taps, mq, u, zt, p, gw):
    t, d = e.shape
    tile = 256
    r = rows(tile, d)
    w = whole((M, d))
    return pl.pallas_call(
        back_kernel,
        grid=(t // tile,),
        in_specs=[r, r, whole((t, d)), whole((RAD, d)), whole((RAD, d)), whole((t, d)), whole((RAD, d)), whole((RAD, d)),
                  whole(taps.shape), w, w, whole((M, 128)), w, w],
        out_specs=[r, r, w, whole((40, d))],
        out_shape=[sds((t, d), BF16), sds((t, d), BF16), sds((M, d), F32), sds((40, d), F32)],
        scratch_shapes=[
            pltpu.VMEM((6, tile + 2 * RAD, 128), F32),
            pltpu.VMEM((6, tile + 2 * RAD, 128), F32),
            pltpu.VMEM((6, tile, 128), F32),
            pltpu.VMEM((40, 8, d), F32),
            pltpu.VMEM((NG, GROUP, GROUP), BF16),
            pltpu.VMEM((NG, 8, GROUP), F32),
            pltpu.VMEM((NG, GROUP, GROUP), F32),
        ],
        compiler_params=params(),
        name="back",
    )(e, k, v, vl, vr, dmix, gl, gr, taps, mq, u, zt, p, gw)


def last_kernel(x_ref, dx_ref, dqf_ref, dkb_ref, dv_ref, own_ref, w_ref, gain_ref, dq_ref, dk_ref, ig_ref, dg_ref, dgacc, *, seg_len, rows_dev):
    i = pl.program_id(0)
    n = pl.num_programs(0)
    tile, d = x_ref.shape

    @pl.when(i == 0)
    def _():
        dgacc[...] = jnp.zeros_like(dgacc)

    at = i * rows_dev // 4
    scale = 1.0 / seg_len
    dq = (dqf_ref[...].astype(F32) + own_ref[pl.ds(at, 1), :] * scale).astype(BF16)
    dk = (dkb_ref[...].astype(F32) + own_ref[pl.ds(at + 4, 1), :] * scale).astype(BF16)
    dq_ref[...] = dq
    dk_ref[...] = dk
    dh = (dot_nt(dq, w_ref[0]) + dot_nt(dk, w_ref[1])) * QK_SCALE + dot_nt(dv_ref[...], w_ref[2])
    normal, inv = normalize(x_ref[...].astype(F32))
    dgacc[...] += rowsum8(dh * normal)
    ig = norm_back(dh, normal, inv, gain_ref[0:1, :]) + dx_ref[...].astype(F32)
    ig_ref[...] = ig.astype(BF16)

    @pl.when(i == n - 1)
    def _():
        dg_ref[...] = jnp.broadcast_to(jnp.sum(dgacc[...], axis=0, keepdims=True), (8, d))


def last(x, dx, dqf, dkb, dv, own, w_attn, gains, seg_len, rows_dev):
    t, d = x.shape
    tile = t // 4
    r = rows(tile, d)
    return pl.pallas_call(
        functools.partial(last_kernel, seg_len=seg_len, rows_dev=rows_dev),
        grid=(4,),
        in_specs=[r, r, r, r, r, whole((8, d)), whole(w_attn.shape), whole(gains.shape)],
        out_specs=[r, r, r, whole((8, d))],
        out_shape=[sds((t, d), BF16)] * 3 + [sds((8, d), F32)],
        scratch_shapes=[pltpu.VMEM((8, d), F32)],
        compiler_params=params(),
        name="last",
    )(x, dx, dqf, dkb, dv, own, w_attn, gains)


def adam_step(weight, grad_vec, moment, second, rate_value):
    moment_new = BETA_ONE * moment + (1.0 - BETA_ONE) * grad_vec
    second_new = BETA_TWO * second + (1.0 - BETA_TWO) * grad_vec * grad_vec
    first_hat = moment_new / (1.0 - BETA_ONE**STEP)
    second_hat = second_new / (1.0 - BETA_TWO**STEP)
    weight_new = weight - rate_value * (
        first_hat / (jnp.sqrt(second_hat) + ADAM_EPS) + DECAY_RATE * weight
    )
    return (weight_new, moment_new, second_new)


def halos(cells, index, count):
    left = lax.ppermute(cells[-RAD:], "seq", [(i, (i + 1) % count) for i in range(count)])
    right = lax.ppermute(cells[:RAD], "seq", [((i + 1) % count, i) for i in range(count)])
    left = jnp.where(index > 0, left, jnp.zeros_like(left))
    right = jnp.where(index < count - 1, right, jnp.zeros_like(right))
    return left, right


def per_device(tokens, cotangent, attn_w, w_up, w_down, vectors, attn_m, attn_v, up_m, up_v, down_m, down_v, vec_m, vec_v):
    both = ("seq", "rep")
    x = tokens[0]
    dy = cotangent[0]
    t, d = x.shape
    count = lax.axis_size("seq")
    index = lax.axis_index("seq")
    rows_dev = max(M // count, 1)
    per_mark = count * rows_dev // M
    seg_len = t * count // M

    w_attn = lax.all_gather(attn_w.astype(BF16), both, axis=1, tiled=True)
    up = lax.all_gather(w_up.astype(BF16), both, axis=0, tiled=True)
    down = lax.all_gather(w_down.astype(BF16), both, axis=0, tiled=True)
    vec = lax.all_gather(vectors.astype(BF16), both, axis=0, tiled=True)
    vec_t = jnp.transpose(vec.astype(F32))
    gains = jnp.concatenate([vec_t[:2], jnp.zeros((6, d), F32)], axis=0)
    taps = jnp.concatenate([vec_t[2:], jnp.zeros((7, d), F32)], axis=0)

    h1, q, k, v, means = project(x, w_attn, gains)
    marks = lax.all_gather(means, "seq", axis=0)
    marks = jnp.transpose(marks.reshape(count, 2, 4, d), (1, 0, 2, 3)).reshape(2, M, count * 4 // M, d)
    marks = jnp.mean(marks, axis=2).astype(BF16)
    mq, mk = marks[0], marks[1]
    vl, vr = halos(v, index, count)
    f, e, u, zt = attend(q, k, v, mq, mk)
    u, zt = lax.psum((u, zt), "seq")
    a, p, zs, azs, t2s, t3s = pinv(mq, mk)
    out, act, da, h2, mix, dx, dmix, dqf, gw, dkt, dg2 = middle(
        x, dy, f, q, v, vl, vr, w_attn[3], up, down, gains, taps, mk, u, zt, p
    )
    gw = lax.psum(gw, "seq")
    gl, gr = halos(dmix, index, count)
    dot_xla = functools.partial(jnp.einsum, "ta,tb->ab", preferred_element_type=F32)
    g_down = dot_xla(act, dy).astype(BF16)
    g_up = dot_xla(h2, da).astype(BF16)
    g_o = dot_xla(mix, dx)
    dqt_a, dkt_a = pinv_back(mq, mk, (a, p, zs, azs, t2s, t3s), gw, u, zt, 1.0 / count)
    dv, dkb, dqt, dtap = back(e, k, v, vl, vr, dmix, gl, gr, taps, mq, u, zt, p, gw)
    spread_marks = jnp.stack([dqt + dqt_a, dkt + dkt_a])
    spread_marks = jnp.repeat(spread_marks, per_mark, axis=1).reshape(2, count, rows_dev, d)
    spread_marks = jnp.transpose(spread_marks, (1, 0, 2, 3))
    own = lax.psum_scatter(spread_marks, "seq", scatter_dimension=0, tiled=True)[0]
    own = jnp.pad(own, ((0, 0), (0, 4 - rows_dev), (0, 0))).reshape(8, d)
    dq, dk, ig, dg1 = last(x, dx, dqf, dkb, dv, own, w_attn, gains, seg_len, rows_dev)
    g_q = dot_xla(h1, dq) * QK_SCALE
    g_k = dot_xla(h1, dk) * QK_SCALE
    g_v = dot_xla(h1, dv)
    g_attn = jnp.stack([g_q, g_k, g_v, g_o]).astype(BF16)
    g_vec = jnp.transpose(jnp.concatenate([dg1[:1], dg2[:1], dtap[:KC]], axis=0))
    red_attn = lax.psum_scatter(g_attn, both, scatter_dimension=1, tiled=True).astype(F32)
    red_up = lax.psum_scatter(g_up, both, scatter_dimension=0, tiled=True).astype(F32)
    red_down = lax.psum_scatter(g_down, both, scatter_dimension=0, tiled=True).astype(F32)
    red_vec = lax.psum_scatter(g_vec, both, scatter_dimension=0, tiled=True)
    return (
        out[None],
        ig[None],
        *adam_step(attn_w, red_attn, attn_m, attn_v, LEARN_RATE),
        *adam_step(w_up, red_up, up_m, up_v, LEARN_RATE),
        *adam_step(w_down, red_down, down_m, down_v, LEARN_RATE),
        *adam_step(vectors, red_vec, vec_m, vec_v, VECTOR_RATE),
    )


def solution(mesh):
    tok = P("rep", "seq", None)
    att = P(None, ("seq", "rep"), None)
    mat = P(("seq", "rep"), None)
    return jax.shard_map(
        per_device,
        mesh=mesh,
        in_specs=(tok, tok, att, mat, mat, mat, att, att, mat, mat, mat, mat, mat, mat),
        out_specs=(tok, tok, att, att, att) + (mat,) * 9,
        check_vma=False,
    )
```

time: 2060 us -> 1200 us (0.58)
  other arithmetic: 669 us -> 20 us
  matrix products: 336 us -> 42.4 us
  Pallas kernels: 0 us -> 219 us
  local copies, waits for them, and re-layouts: 223 us -> 22.8 us
  waiting for transfers between devices: 629 us -> 708 us
    add x67 -> x2, other arithmetic: 571 us -> 1.9 us  [per_device(): spread_marks = jnp.stack([dqt + dqt_a, dkt + dkt_a])]
    dot_general x106 -> x6, matrix products: 327 us -> 42.4 us  [the longest x1 15 us: per_device(): g_down = dot_xla(act, dy).astype(BF16)]
    pallas_call x0 -> x7, Pallas kernels: none -> 219 us  [the longest x1 97.4 us: middle(): pl.pallas_call(middle_kernel, grid=(t // tile,), in_specs=[r, r, r, r, wh...]
    reduce_scatter x3 -> x2, waiting for transfers between devices: 410 us -> 222 us  [the longest x1 112 us: per_device(): lax.psum_scatter(g_down, both, scatter_dimension=0, tiled=True).astype(F32)]
    psum x2, waiting for transfers between devices: 0.02 us -> 178 us  [the longest x1 96.1 us: per_device(): gw = lax.psum(gw, 'seq')]
    unnamed x12 -> x13, waiting for transfers between devices: 135 us -> 282 us
    all_gather x3, waiting for transfers between devices: 81.9 us -> 18.9 us  [the longest x1 18.9 us: per_device(): w_attn = lax.all_gather(attn_w.astype(BF16), both, axis=1, tiled=True)]
    while x132 -> x0, local copies, waits for them, and re-layouts: 50.2 us -> none
  transfers between devices with their start and end apart: 14 -> 14, of which waited for: 8 -> 10; matrix products, arithmetic and copies ran while one was open for 42% -> 6% of each run, Pallas kernels for 0% -> 3%
where the time goes in v1:
time: 1200 us; the launch traced here: 1190 us
  waiting for transfers between devices  708 us (59%)
  Pallas kernels  219 us (18%)
  blocking collectives  161 us (13%)
  matrix products  42.4 us (4%)
  local copies, waits for them, and re-layouts  22.8 us (2%)
  other arithmetic  20 us (2%)
  between operations  14.8 us (1%)
    unnamed x13, waiting for transfers between devices  282 us
    reduce_scatter x1, waiting for transfers between devices, per_device(): lax.psum_scatter(g_down, both, scatter_dimension=0, tiled=True).astype(F32)  112 us
    reduce_scatter x1, waiting for transfers between devices, per_device(): lax.psum_scatter(g_up, both, scatter_dimension=0, tiled=True).astype(F32)  110 us
    pallas_call x1, Pallas kernels, middle(): pl.pallas_call(middle_kernel, grid=(t // tile,), in_specs=[r, r, r, r, wh...  97.4 us
    psum x1, waiting for transfers between devices, per_device(): gw = lax.psum(gw, 'seq')  96.1 us
    psum x1, waiting for transfers between devices, per_device(): u, zt = lax.psum((u, zt), 'seq')  81.8 us
    psum x1, blocking collectives, per_device(): u, zt = lax.psum((u, zt), 'seq')  76.8 us
    pallas_call x1, Pallas kernels, back(): pl.pallas_call(back_kernel, grid=(t // tile,), in_specs=[r, r, whole((t,...  45 us
  transfers between devices with their start and end apart: 14, of which 10 were waited for; matrix products, arithmetic and copies ran while one was open for 6% of the time, Pallas kernels for 3%

profile of v1, /device:TPU:0, one launch (start us, length us, event | category | flops | bytes accessed | tf_op | source)
XLA Modules:
  0.0 1193.1 jit_solution(13016740773624214872)
XLA Ops:
  7.2 1.6 convert_element_type.39
  8.9 1.6 convert_element_type.44
  10.7 1.6 convert_element_type.45
  12.4 0.7 convert_element_type.40
  13.1 43.8 %all_gather.19 = bf16[768,35]{1,0:T(8,128)(2,1)S(1)} all-gather(bf16[24,35]{1,0:T(8,128)(2,1)S(1)} %convert_element_type.40), channel_id=1, replica_groups=mesh['seq'=16,'rep'=2] {'seq','rep'}, dimensions={0}, use_global_device_ids=true | all-gather | bytes 55440 | tf_op jit(solution)/shard_map/all_gather | solution.py:618
  57.1 0.7 concatenate.11.tap_ref
  57.7 1.3 slice_select_fusion.gain_ref
  59.1 18.9 %all-gather.5.cloned.1.call-done.w_ref = bf16[4,768,768]{2,1,0:T(8,128)(2,1)} async-done(((bf16[4,24,768]{2,1,0:T(8,128)(2,1)}), bf16[4,768,768]{2,1,0:T(8,128)(2,1)}) %all-gather.5.cloned.1.call-update) | async-done | bytes 4718608 | tf_op jit(solution)/shard_map/all_gather | solution.py:615
  77.9 13.1 %project.1 = (bf16[2048,768]{1,0:T(8,128)(2,1)}, bf16[2048,768]{1,0:T(8,128)(2,1)}, bf16[2048,768]{1,0:T(8,128)(2,1)}, bf16[2048,768]{1,0:T(8,128)(2,1)}, f32[8,768]{1,0:T(8,128)}) custom-call(bf16[2048,768]{1,0:T(8,128)(2,1)} %bitcast.46, bf16[4,768,768]{2,1,0:T(8,128)(2,1)} %all-gather.5.cloned.1.call-done.w_ref, f32[8,768]{1,0:T(8,128)} %slice_select_fusion.gain_ref), custom_call_target="tpu_custom_call" | custom-call | tf_op jit(solution)/shard_map/project/pallas_call | solution.py:143
  91.0 0.7 convert.33
  91.8 40.1 %all-gather = bf16[128,768]{1,0:T(8,128)(2,1)S(1)} all-gather(bf16[8,768]{1,0:T(8,128)(2,1)S(1)} %convert.33), channel_id=2, replica_groups=mesh['seq'=16,'rep'=2] {'seq'}, dimensions={0}, use_global_device_ids=true | all-gather | bytes 208896 | tf_op jit(solution)/shard_map/all_gather | solution.py:624
  132.1 0.7 squeeze.18.mq_ref
  132.8 0.7 squeeze.19.mk_ref
  133.5 0.8 fusion.20
  134.2 2.2 collective-permute-start
  136.4 12.0 %pinv.1 = (f32[64,768]{1,0:T(8,128)}, f32[64,768]{1,0:T(8,128)}, f32[6,64,768]{2,1,0:T(8,128)}, f32[6,64,768]{2,1,0:T(8,128)}, f32[6,64,768]{2,1,0:T(8,128)}, /*index=5*/f32[6,64,768]{2,1,0:T(8,128)}) custom-call(bf16[64,768]{1,0:T(8,128)(2,1)} %squeeze.18.mq_ref, bf16[64,768]{1,0:T(8,128)(2,1)} %squeeze.19.mk_ref), custom_call_target="tpu_custom_call" | custom-call | tf_op jit(solution)/shard_map/pinv/pallas_call | solution.py:190
  148.5 12.5 %attend.1 = (bf16[2048,768]{1,0:T(8,128)(2,1)}, bf16[2048,768]{1,0:T(8,128)(2,1)}, f32[64,768]{1,0:T(8,128)}, f32[64,128]{1,0:T(8,128)}) custom-call(bf16[2048,768]{1,0:T(8,128)(2,1)} %get-tuple-element.50.q_ref, bf16[2048,768]{1,0:T(8,128)(2,1)} %get-tuple-element.51.k_ref, bf16[2048,768]{1,0:T(8,128)(2,1)} %get-tuple-element.52.v_ref, ...), custom_call_target="tpu_custom_call" | custom-call | tf_op jit(solution)/shard_map/attend/pallas_call | solution.py:295
  161.0 2.4 slice_bitcast_fusion.wo_ref
  163.4 76.8 %psum.22.zt_ref = f32[64,128]{1,0:T(8,128)} all-reduce(f32[64,128]{1,0:T(8,128)} %get-tuple-element.56), channel_id=1, replica_groups=mesh['seq'=16,'rep'=2] {'seq'}, use_global_device_ids=true, to_apply=%region_1.2 | all-reduce | flops 8192 | bytes 65536 | tf_op jit(solution)/shard_map/psum | solution.py:630
  240.2 0.6 broadcast_select_fusion.1.right_ref.vr_ref
  240.8 0.6 broadcast_select_fusion.3.left_ref.vl_ref
  241.4 81.8 %all-reduce.8.cloned.1.call-done.u_ref = f32[64,768]{1,0:T(8,128)} async-done(((f32[64,768]{1,0:T(8,128)}), f32[64,768]{1,0:T(8,128)}) %all-reduce.8.cloned.1.call-update) | async-done | bytes 196624 | tf_op jit(solution)/shard_map/psum | solution.py:630
  323.2 97.4 %middle.1 = (bf16[2048,768]{1,0:T(8,128)(2,1)}, bf16[2048,3072]{1,0:T(8,128)(2,1)}, bf16[2048,3072]{1,0:T(8,128)(2,1)}, bf16[2048,768]{1,0:T(8,128)(2,1)}, bf16[...) custom-call(bf16[2048,768]{1,0:T(8,128)(2,1)} %bitcast.47, ...), custom_call_target="tpu_custom_call" | custom-call | tf_op jit(solution)/shard_map/middle/pallas_call | solution.py:452
  420.6 0.8 fusion.19
  421.4 3.3 collective-permute-start.3
  424.8 1.4 collective-permute-done.3
  426.2 0.6 broadcast_select_fusion.gr_ref
  426.8 5.4 collective-permute-done.2
  432.2 0.6 broadcast_select_fusion.2.gl_ref
  432.8 96.1 %all-reduce.10.cloned.1.call-done.gw_ref = f32[64,768]{1,0:T(8,128)} async-done(((f32[64,768]{1,0:T(8,128)}), f32[64,768]{1,0:T(8,128)}) %all-reduce.10.cloned.1.call-update) | async-done | bytes 196624 | tf_op jit(solution)/shard_map/psum | solution.py:635
  528.9 45.0 %back.1 = (bf16[2048,768]{1,0:T(8,128)(2,1)}, bf16[2048,768]{1,0:T(8,128)(2,1)}, f32[64,768]{1,0:T(8,128)}, f32[40,768]{1,0:T(8,128)}) custom-call(bf16[2048,768]{1,0:T(8,128)(2,1)} %get-tuple-element.61.e_ref, bf16[2048,768]{1,0:T(8,128)(2,1)} %get-tuple-element.51.k_ref, bf16[2048,768]{1,0:T(8,128)(2,1)} %get-tuple-element.52.v_ref, ...), custom_call_target="tpu_custom_call" | custom-call | tf_op jit(solution)/shard_map/back/pallas_call | solution.py:522
  573.9 22.4 %pinv_back.1 = (f32[64,768]{1,0:T(8,128)}, f32[64,768]{1,0:T(8,128)}) custom-call(bf16[64,768]{1,0:T(8,128)(2,1)} %squeeze.18.mq_ref, bf16[64,768]{1,0:T(8,128)(2,1)} %squeeze.19.mk_ref, f32[64,768]{1,0:T(8,128)} %get-tuple-element.67.a_ref, f32[64,768]{1,0:T(8,128)} %get-tuple-element.57.p_ref, f32[6,64,768]{2,1,0:T(8,128)} %get-tuple-element.68.z_ref, ...), custom_call_target="tpu_custom_call" | custom-call | tf_op jit(solution)/shard_map/pinv_back/pallas_call | solution.py:244
  596.3 0.9 add.84
  597.3 1.0 add.85
  598.4 0.8 maximum_bitcast_fusion
  599.3 0.6 dynamic-slice
  599.9 0.7 slice.49
  600.6 105.7 %all-reduce.12.cloned.1.call-done = f32[16,2,4,768]{3,2,1,0:T(4,128)} async-done(((f32[16,2,4,768]{3,2,1,0:T(4,128)}), f32[16,2,4,768]{3,2,1,0:T(4,128)}) %all-reduce.12.cloned.1.call-update) | async-done | bytes 393232
  706.3 1.4 constant_dynamic-slice_fusion.1
  707.7 0.6 reshape.46.own_ref
  708.3 16.3 %last.1 = (bf16[2048,768]{1,0:T(8,128)(2,1)}, bf16[2048,768]{1,0:T(8,128)(2,1)}, bf16[2048,768]{1,0:T(8,128)(2,1)}, f32[8,768]{1,0:T(8,128)}) custom-call(bf16[2048,768]{1,0:T(8,128)(2,1)} %bitcast.48, bf16[2048,768]{1,0:T(8,128)(2,1)} %get-tuple-element.59.dx_ref, bf16[2048,768]{1,0:T(8,128)(2,1)} %get-tuple-element.60.dqf_ref, ...), custom_call_target="tpu_custom_call" | custom-call | tf_op jit(solution)/shard_map/last/pallas_call | solution.py:573
  724.7 0.7 slice.48
  725.4 0.7 maximum_bitcast_fusion.1
  726.2 15.0 %convolution_convert_fusion = bf16[3072,768]{1,0:T(8,128)(2,1)} fusion(bf16[2048,3072]{1,0:T(8,128)(2,1)} %get-tuple-element.82, bf16[1,2048,768]{2,1,0:T(8,128)(2,1)S(1)} %copy-done), kind=kOutput, calls=%fused_computation | convolution fusion | flops 9666035712 | bytes 20447232 | tf_op jit(solution)/shard_map/ta,tb->ab/dot_general | solution.py:638
  741.3 1.8 copy-done.19
  743.1 14.4 %convolution_convert_fusion.1 = bf16[768,3072]{1,0:T(8,128)(2,1)} fusion(bf16[2048,768]{1,0:T(8,128)(2,1)S(1)} %copy-done.19, bf16[2048,3072]{1,0:T(8,128)(2,1)} %get-tuple-element.81), kind=kOutput, calls=%fused_computation.1 | convolution fusion | flops 9666035712 | bytes 20447232 | tf_op jit(solution)/shard_map/ta,tb->ab/dot_general | solution.py:639
  757.8 1.6 copy-done.1
  759.4 4.7 fusion.1
  764.2 2.7 fusion
  766.9 2.7 fusion.2
  769.7 2.7 fusion.3
  772.4 0.9 pad_maximum_fusion
  773.3 3.6 copy.57
  776.9 3.2 copy.61
  780.3 66.3 %all-reduce.14.cloned.1.call-done = f32[768,35]{0,1:T(8,128)} async-done(((f32[768,35]{0,1:T(8,128)}), f32[768,35]{0,1:T(8,128)}) %all-reduce.14.cloned.1.call-update) | async-done | bytes 107536
  846.6 0.9 constant_dynamic-slice_fusion
  847.5 0.6 multiply_subtract_fusion.3
  848.1 112.0 %reduce-scatter.9.cloned.1.call-done = bf16[96,768]{1,0:T(8,128)(2,1)} async-done(((bf16[3072,768]{1,0:T(8,128)(2,1)}), bf16[96,768]{1,0:T(8,128)(2,1)}) %reduce-scatter.9.cloned.1.call-update) | async-done | bytes 147472 | tf_op jit(solution)/shard_map/reduce_scatter | solution.py:656
  960.1 2.0 multiply_subtract_fusion
  962.1 109.6 %reduce-scatter.7.cloned.1.call-done = bf16[24,3072]{1,0:T(8,128)(2,1)} async-done(((bf16[768,3072]{1,0:T(8,128)(2,1)}), bf16[24,3072]{1,0:T(8,128)(2,1)}) %reduce-scatter.7.cloned.1.call-update) | async-done | bytes 147472 | tf_op jit(solution)/shard_map/reduce_scatter | solution.py:655
  1071.7 2.0 multiply_subtract_fusion.1
  1073.7 110.3 %reduce-scatter.11.cloned.1.call-done = bf16[24,3072]{1,0:T(8,128)(2,1)} async-done(((bf16[768,3072]{1,0:T(8,128)(2,1)}), bf16[24,3072]{1,0:T(8,128)(2,1)}) %reduce-scatter.11.cloned.1.call-update) | async-done | bytes 147472
  1184.0 1.0 reshape.51
  1185.0 1.1 multiply_subtract_fusion.2
  (79 shorter events, 1.5 us)
Async XLA Ops:
  7.2 70.8 %all-gather.5.cloned.1.call-start = ((), (), s32[]{:S(2)}) async-start(), calls=%async_computation.3 | async-start | bytes 4866048 | tf_op jit(solution)/shard_map/all_gather | solution.py:615
  8.9 232.5 %all-gather.7.cloned.1.call-start = ((), (), s32[]{:S(2)}) async-start(), calls=%async_computation.4 | async-start | bytes 4866048 | tf_op jit(solution)/shard_map/all_gather | solution.py:616
  10.6 230.8 %all-gather.9.cloned.1.call-start = ((), (), s32[]{:S(2)}) async-start(), calls=%async_computation.5 | async-start | bytes 4866048 | tf_op jit(solution)/shard_map/all_gather | solution.py:617
  12.3 310.8 %all-reduce.8.cloned.1.call-start = ((), (), s32[]{:S(2)}) async-start(), calls=%async_computation.6 | async-start | bytes 393216 | tf_op jit(solution)/shard_map/psum | solution.py:630
  134.2 105.9 %collective-permute-start.1 = (bf16[16,768]{1,0:T(8,128)(2,1)S(1)}, bf16[16,768]{1,0:T(8,128)(2,1)S(1)}, u32[]{:S(2)}, u32[]{:S(2)}) collective-permute-start(bf16[16,768]{1,0:T(8,128)(2,1)S(1)} %get-tuple-element.128), channel_id=1, source_target_pairs={{2,0},{4,2},{6,4},{8,6},{10,8},{12,10},{14,12},{16,14},{18,16},{20... | collective-permute-start | bytes 73736 | tf_op jit(solution)/shard_map/ppermute | solution.py:598
  134.2 106.5 %collective-permute-start = (bf16[16,768]{1,0:T(8,128)(2,1)S(1)}, bf16[16,768]{1,0:T(8,128)(2,1)S(1)}, u32[]{:S(2)}, u32[]{:S(2)}) collective-permute-start(bf16[16,768]{1,0:T(8,128)(2,1)S(1)} %get-tuple-element.129), channel_id=1, source_target_pairs={{0,2},{2,4},{4,6},{6,8},{8,10},{10,12},{12,14},{14,16},{16,18},{18... | collective-permute-start | bytes 73736 | tf_op jit(solution)/shard_map/ppermute | solution.py:597
  161.0 367.9 %all-reduce.10.cloned.1.call-start = ((), (), s32[]{:S(2)}) async-start(), calls=%async_computation.7 | async-start | bytes 393216 | tf_op jit(solution)/shard_map/psum | solution.py:635
  421.4 4.8 collective-permute-start.3
  424.7 281.7 %all-reduce.12.cloned.1.call-start = ((), (), s32[]{:S(2)}) async-start(), calls=%async_computation.11 | async-start | bytes 786432
  424.7 7.5 collective-permute-start.2
  573.9 22.4 %copy-start.13 = (f32[64,768]{1,0:T(8,128)S(1)}, f32[64,768]{1,0:T(8,128)}, u32[]{:S(2)}) copy-start(f32[64,768]{1,0:T(8,128)} %get-tuple-element.66) | copy-start | bytes 589828
  573.9 23.4 %copy-start.12 = (f32[64,768]{1,0:T(8,128)S(1)}, f32[64,768]{1,0:T(8,128)}, u32[]{:S(2)}) copy-start(f32[64,768]{1,0:T(8,128)} %get-tuple-element.73) | copy-start | bytes 589828
  573.9 25.4 %copy-start.22 = (u32[32]{0:T(128)S(1)}, u32[32]{0:T(128)}, u32[]{:S(2)}) copy-start(u32[32]{0:T(128)} %constant.85) | copy-start | bytes 388
  599.2 247.3 %all-reduce.14.cloned.1.call-start = ((), (), s32[]{:S(2)}) async-start(), calls=%async_computation.12 | async-start | bytes 245760
  708.3 17.1 %copy-start.14 = (f32[40,768]{1,0:T(8,128)S(1)}, f32[40,768]{1,0:T(8,128)}, u32[]{:S(2)}) copy-start(f32[40,768]{1,0:T(8,128)} %get-tuple-element.85) | copy-start | bytes 368644
  708.3 17.8 %copy-start = (bf16[1,2048,768]{2,1,0:T(8,128)(2,1)S(1)}, bf16[1,2048,768]{2,1,0:T(8,128)(2,1)}, u32[]{:S(2)}) copy-start(bf16[1,2048,768]{2,1,0:T(8,128)(2,1)} %param.15) | copy-start | bytes 9437188
  726.1 234.0 %reduce-scatter.9.cloned.1.call-start = ((), (), s32[]{:S(2)}) async-start(), calls=%async_computation.9 | async-start | bytes 4866048 | tf_op jit(solution)/shard_map/reduce_scatter | solution.py:656
  741.2 1.9 copy-start.19
  741.2 330.5 %reduce-scatter.7.cloned.1.call-start = ((), (), s32[]{:S(2)}) async-start(), calls=%async_computation.8 | async-start | bytes 4866048 | tf_op jit(solution)/shard_map/reduce_scatter | solution.py:655
  757.5 1.9 copy-start.1
  757.6 426.4 %reduce-scatter.11.cloned.1.call-start = ((), (), s32[]{:S(2)}) async-start(), calls=%async_computation.10 | async-start | bytes 4866048
  759.4 4.7 copy-start.2
  759.4 4.7 copy-start.18
  764.2 2.8 copy-start.21
  766.9 2.8 copy-start.20
  780.2 67.3 %copy-start.15 = (f32[24,35]{1,0:T(8,128)S(1)}, f32[24,35]{1,0:T(8,128)}, u32[]{:S(2)}) copy-start(f32[24,35]{1,0:T(8,128)} %param.19) | copy-start | bytes 10084
  780.2 67.3 %copy-start.16 = (f32[24,35]{1,0:T(8,128)S(1)}, f32[24,35]{1,0:T(8,128)}, u32[]{:S(2)}) copy-start(f32[24,35]{1,0:T(8,128)} %param.26) | copy-start | bytes 10084
  780.2 67.3 %copy-start.17 = (f32[24,35]{1,0:T(8,128)S(1)}, f32[24,35]{1,0:T(8,128)}, u32[]{:S(2)}) copy-start(f32[24,35]{1,0:T(8,128)} %param.27) | copy-start | bytes 10084
  780.2 180.0 %copy-start.3 = (f32[96,768]{1,0:T(8,128)S(1)}, f32[96,768]{1,0:T(8,128)}, u32[]{:S(2)}) copy-start(f32[96,768]{1,0:T(8,128)} %param.18) | copy-start | bytes 884740
  780.2 180.0 %copy-start.6 = (f32[96,768]{1,0:T(8,128)S(1)}, f32[96,768]{1,0:T(8,128)}, u32[]{:S(2)}) copy-start(f32[96,768]{1,0:T(8,128)} %param.24) | copy-start | bytes 884740
  780.2 180.0 %copy-start.7 = (f32[96,768]{1,0:T(8,128)S(1)}, f32[96,768]{1,0:T(8,128)}, u32[]{:S(2)}) copy-start(f32[96,768]{1,0:T(8,128)} %param.25) | copy-start | bytes 884740
  780.2 291.5 %copy-start.4 = (f32[24,3072]{1,0:T(8,128)S(1)}, f32[24,3072]{1,0:T(8,128)}, u32[]{:S(2)}) copy-start(f32[24,3072]{1,0:T(8,128)} %param.17) | copy-start | bytes 884740
  780.2 291.5 %copy-start.8 = (f32[24,3072]{1,0:T(8,128)S(1)}, f32[24,3072]{1,0:T(8,128)}, u32[]{:S(2)}) copy-start(f32[24,3072]{1,0:T(8,128)} %param.22) | copy-start | bytes 884740
  780.2 291.5 %copy-start.9 = (f32[24,3072]{1,0:T(8,128)S(1)}, f32[24,3072]{1,0:T(8,128)}, u32[]{:S(2)}) copy-start(f32[24,3072]{1,0:T(8,128)} %param.23) | copy-start | bytes 884740
  780.3 404.7 %copy-start.5 = (f32[4,24,768]{2,1,0:T(8,128)S(1)}, f32[4,24,768]{2,1,0:T(8,128)}, u32[]{:S(2)}) copy-start(f32[4,24,768]{2,1,0:T(8,128)} %param.16) | copy-start | bytes 884740
  780.3 404.7 %copy-start.10 = (f32[4,24,768]{2,1,0:T(8,128)S(1)}, f32[4,24,768]{2,1,0:T(8,128)}, u32[]{:S(2)}) copy-start(f32[4,24,768]{2,1,0:T(8,128)} %param.20) | copy-start | bytes 884740
  780.3 404.7 %copy-start.11 = (f32[4,24,768]{2,1,0:T(8,128)S(1)}, f32[4,24,768]{2,1,0:T(8,128)}, u32[]{:S(2)}) copy-start(f32[4,24,768]{2,1,0:T(8,128)} %param.21) | copy-start | bytes 884740
Sparse Core Ops, SparseCore 0:
  11.5 66.3 all-gather.4
  81.4 63.5 all-gather.6
  148.5 63.2 all-gather.8
  217.4 105.6 all-reduce.7
  424.8 104.0 all-reduce.9
  599.3 106.9 all-reduce.11
  726.2 120.3 all-reduce.13
  852.9 107.1 reduce-scatter.8
  965.6 106.0 reduce-scatter.6
  1077.9 106.0 reduce-scatter.10

commit v2 on v1

--- a/solution.py
+++ b/solution.py
@@ -582,6 +582,546 @@
     )(x, dx, dqf, dkb, dv, own, w_attn, gains)
 
 
+MESH = pl.DeviceIdType.MESH
+
+
+def remote(src, dst, send, recv, where):
+    return pltpu.make_async_remote_copy(
+        src_ref=src, dst_ref=dst, send_sem=send, recv_sem=recv, device_id=where, device_id_type=MESH
+    )
+
+
+def greet(peers):
+    bar = pltpu.get_barrier_semaphore()
+    for peer in peers:
+        pl.semaphore_signal(bar, inc=1, device_id=peer, device_id_type=MESH)
+    pl.semaphore_wait(bar, len(peers))
+
+
+def greet_all(me, n):
+    bar = pltpu.get_barrier_semaphore()
+
+    def hello(j, _):
+        pl.semaphore_signal(bar, inc=1, device_id={"seq": lax.rem(me + j, n)}, device_id_type=MESH)
+        return 0
+
+    lax.fori_loop(1, n, hello, 0)
+    pl.semaphore_wait(bar, n - 1)
+
+
+def each_peer(me, n, make, act):
+    def body(j, _):
+        act(make(j, lax.rem(me + j, n)))
+        return 0
+
+    lax.fori_loop(1, n, body, 0)
+
+
+def halo_copies(body_ref, left_ref, right_ref, me, n, sems):
+    t = body_ref.shape[0]
+    right = {"seq": lax.rem(me + 1, n)}
+    left = {"seq": lax.rem(me + n - 1, n)}
+    return (
+        remote(body_ref.at[pl.ds(t - RAD, RAD)], left_ref, sems.at[0], sems.at[1], right),
+        remote(body_ref.at[pl.ds(0, RAD)], right_ref, sems.at[2], sems.at[3], left),
+    )
+
+
+def mask_halos(left_ref, right_ref, me, n):
+    left_ref[...] = jnp.where(me > 0, left_ref[...], jnp.zeros_like(left_ref))
+    right_ref[...] = jnp.where(me < n - 1, right_ref[...], jnp.zeros_like(right_ref))
+
+
+def marks_kernel(mean_ref, v_ref, mq_ref, mk_ref, left_ref, right_ref, pay, slots, send, recv, hsem, *, n):
+    me = lax.axis_index("seq")
+    d = mean_ref.shape[1]
+    half = d // 2
+    greet_all(me, n)
+    halos = halo_copies(v_ref, left_ref, right_ref, me, n, hsem)
+    pay[...] = jnp.concatenate([mean_ref[:, :half], mean_ref[:, half:]], axis=0).astype(BF16)
+
+    def make(j, peer):
+        return remote(pay, slots.at[me], send.at[j], recv.at[j], {"seq": peer})
+
+    each_peer(me, n, make, lambda c: c.start())
+    for c in halos:
+        c.start()
+    slots[pl.ds(me, 1)] = pay[...][None]
+    each_peer(me, n, make, lambda c: c.wait())
+    per = 4 * n // M
+    for out, base in ((mq_ref, 0), (mk_ref, 4)):
+        if per == 1:
+            got = [slots[i].astype(F32) for i in range(n)]
+            for h in range(2):
+                tall = jnp.concatenate([x[8 * h + base : 8 * h + base + 4] for x in got], axis=0)
+                out[:, h * half : (h + 1) * half] = tall.astype(BF16)
+        else:
+            for h in range(2):
+                lines = []
+                for m in range(M):
+                    total = jnp.zeros((1, half), F32)
+                    for s in range(per // 4):
+                        part = slots[m * (per // 4) + s].astype(F32)[8 * h + base : 8 * h + base + 4]
+                        total = total + jnp.sum(part, axis=0, keepdims=True)
+                    lines.append(total * (1.0 / per))
+                out[:, h * half : (h + 1) * half] = jnp.concatenate(lines, axis=0).astype(BF16)
+    for c in halos:
+        c.wait()
+    mask_halos(left_ref, right_ref, me, n)
+
+
+def exchange_marks(means, v, n):
+    d = v.shape[1]
+    vm = pl.BlockSpec(memory_space=pltpu.VMEM)
+    anyw = pl.BlockSpec(memory_space=pl.ANY)
+    return pl.pallas_call(
+        functools.partial(marks_kernel, n=n),
+        in_specs=[vm, anyw],
+        out_specs=[vm] * 4,
+        out_shape=[sds((M, d), BF16)] * 2 + [sds((RAD, d), BF16)] * 2,
+        scratch_shapes=[
+            pltpu.VMEM((16, d // 2), BF16),
+            pltpu.VMEM((n, 16, d // 2), BF16),
+            pltpu.SemaphoreType.DMA((n,)),
+            pltpu.SemaphoreType.DMA((n,)),
+            pltpu.SemaphoreType.DMA((4,)),
+        ],
+        compiler_params=pltpu.CompilerParams(collective_id=1, has_side_effects=True, vmem_limit_bytes=VMEM_LIMIT),
+        name="exchange_marks",
+    )(means, v)
+
+
+def sum_kernel(x_ref, *rest, n, with_halo):
+    if with_halo:
+        body_ref, out_ref, left_ref, right_ref, slots, total, send, recv, send2, recv2, hsem = rest
+    else:
+        out_ref, slots, total, send, recv, send2, recv2 = rest
+    me = lax.axis_index("seq")
+    chunk = x_ref.shape[0] // n
+    greet_all(me, n)
+
+    def part(ref, i):
+        return ref.at[pl.ds(pl.multiple_of(i * chunk, 8), chunk)]
+
+    def first(j, peer):
+        return remote(part(x_ref, peer), slots.at[me], send.at[j], recv.at[j], {"seq": peer})
+
+    def second(j, peer):
+        return remote(total, part(out_ref, me), send2.at[j], recv2.at[j], {"seq": peer})
+
+    each_peer(me, n, first, lambda c: c.start())
+    if with_halo:
+        halos = halo_copies(body_ref, left_ref, right_ref, me, n, hsem)
+        for c in halos:
+            c.start()
+    here = pl.ds(pl.multiple_of(me * chunk, 8), chunk)
+    slots[pl.ds(me, 1)] = x_ref[here, :][None]
+    each_peer(me, n, first, lambda c: c.wait())
+
+    def add(i, acc):
+        return acc + slots[i]
+
+    summed = lax.fori_loop(1, n, add, slots[0])
+    total[...] = summed
+    each_peer(me, n, second, lambda c: c.start())
+    out_ref[here, :] = summed
+    each_peer(me, n, second, lambda c: c.wait())
+    if with_halo:
+        for c in halos:
+            c.wait()
+        mask_halos(left_ref, right_ref, me, n)
+
+
+def padded_rows(r, n):
+    return -(-r // (8 * n)) * 8 * n
+
+
+def sum_over_seq(x, n, ident, body=None):
+    r = x.shape[0]
+    vm = pl.BlockSpec(memory_space=pltpu.VMEM)
+    anyw = pl.BlockSpec(memory_space=pl.ANY)
+    with_halo = body is not None
+    out_shape = [sds((r, 128), F32)]
+    if with_halo:
+        out_shape += [sds((RAD, body.shape[1]), BF16)] * 2
+    dma = pltpu.SemaphoreType.DMA
+    res = pl.pallas_call(
+        functools.partial(sum_kernel, n=n, with_halo=with_halo),
+        in_specs=[vm] + [anyw] * with_halo,
+        out_specs=[vm] * len(out_shape),
+        out_shape=out_shape,
+        scratch_shapes=[pltpu.VMEM((n, r // n, 128), F32), pltpu.VMEM((r // n, 128), F32)]
+        + [dma((n,))] * 4
+        + [dma((4,))] * with_halo,
+        compiler_params=pltpu.CompilerParams(collective_id=ident, has_side_effects=True, vmem_limit_bytes=VMEM_LIMIT),
+        name="sum_over_seq",
+    )(*((x, body) if with_halo else (x,)))
+    return res if with_halo else res[0]
+
+
+def own_kernel(dq_ref, dk_ref, dqa_ref, dka_ref, out_ref, pay, slots, send, recv, *, n):
+    me = lax.axis_index("seq")
+    rows_dev = max(M // n, 1)
+    per_mark = n * rows_dev // M
+    dq = dq_ref[...] + dqa_ref[...]
+    dk = dk_ref[...] + dka_ref[...]
+    if rows_dev < 4:
+        pay[...] = jnp.zeros_like(pay)
+    for i in range(n):
+        at = i * rows_dev // per_mark
+        pay[i, 0:rows_dev, :] = dq[at : at + rows_dev]
+        pay[i, 4 : 4 + rows_dev, :] = dk[at : at + rows_dev]
+    greet_all(me, n)
+
+    def make(j, peer):
+        return remote(pay.at[peer], slots.at[me], send.at[j], recv.at[j], {"seq": peer})
+
+    each_peer(me, n, make, lambda c: c.start())
+    slots[pl.ds(me, 1)] = pay[pl.ds(me, 1)]
+    each_peer(me, n, make, lambda c: c.wait())
+    out_ref[...] = lax.fori_loop(1, n, lambda i, acc: acc + slots[i], slots[0])
+
+
+def own_marks(dq, dk, dqa, dka, n):
+    d = dq.shape[1]
+    vm = pl.BlockSpec(memory_space=pltpu.VMEM)
+    return pl.pallas_call(
+        functools.partial(own_kernel, n=n),
+        in_specs=[vm] * 4,
+        out_specs=vm,
+        out_shape=sds((8, d), F32),
+        scratch_shapes=[
+            pltpu.VMEM((n, 8, d), F32),
+            pltpu.VMEM((n, 8, d), F32),
+            pltpu.SemaphoreType.DMA((n,)),
+            pltpu.SemaphoreType.DMA((n,)),
+        ],
+        compiler_params=pltpu.CompilerParams(collective_id=4, has_side_effects=True, vmem_limit_bytes=VMEM_LIMIT),
+        name="own_marks",
+    )(dq, dk, dqa, dka)
+
+
+RING = 16
+
+
+def ring_pos(seq):
+    x = lax.rem(seq, 2)
+    y = lax.rem(lax.div(seq, 2), 2)
+    z = lax.div(seq, 4)
+    col = x * 3 + y * (1 - 2 * x)
+    return col * 4 + z + lax.rem(col, 2) * (3 - 2 * z)
+
+
+def ring_seq(pos):
+    pos = lax.rem(pos + 2 * RING, RING)
+    col = lax.div(pos, 4)
+    zz = lax.rem(pos, 4)
+    z = zz + lax.rem(col, 2) * (3 - 2 * zz)
+    x = lax.div(col, 2)
+    y = lax.rem(lax.div(col + 1, 2), 2)
+    return z * 4 + y * 2 + x
+
+
+def at(i, size, unit):
+    return pl.ds(pl.multiple_of(i * size, unit), size)
+
+
+def piece(kind, ref, seq, rep):
+    if kind == 0:
+        half = ref.shape[2] // 2
+        return ref.at[:, at(seq, ref.shape[1] // RING, 16), at(rep, half, 128)]
+    if kind == 1:
+        half = ref.shape[1] // 2
+        return ref.at[at(seq, ref.shape[0] // RING, 16), at(rep, half, 128)]
+    return ref.at[at(seq * 2 + rep, ref.shape[0] // (2 * RING), 8 if kind == 3 else 16), :]
+
+
+def gather_kernel(wa, wu, wd, wv, oa, ou, od, ov, sa, su, ca, cu, cd, psem, lsem, send, recv, ssend, srecv):
+    seq = lax.axis_index("seq")
+    rep = lax.axis_index("rep")
+    pos = ring_pos(seq)
+    right, left, twin = {"seq": ring_seq(pos + 1)}, {"seq": ring_seq(pos - 1)}, {"rep": 1 - rep}
+    greet([right, left, twin])
+    ra, ru = wa.shape[1], wu.shape[0]
+    ha, hu = wa.shape[2] // 2, wu.shape[1] // 2
+    mine_a, mine_u = at(rep, ra, 8), at(rep, ru, 8)
+    swap = (
+        remote(wa.at[:, :, at(1 - rep, ha, 128)], sa.at[:, mine_a, :], psem.at[0], psem.at[1], twin),
+        remote(wu.at[:, at(1 - rep, hu, 128)], su.at[mine_u, :], psem.at[2], psem.at[3], twin),
+    )
+    for c in swap:
+        c.start()
+    sa[:, mine_a, :] = wa[:, :, at(rep, ha, 128)]
+    su[mine_u, :] = wu[:, at(rep, hu, 128)]
+    cd[...] = wd[...].astype(BF16)
+    for c in swap:
+        c.wait()
+    ca[...] = sa[...].astype(BF16)
+    cu[...] = su[...].astype(BF16)
+    outs = (oa, ou, od, ov)
+    own = (ca, cu, cd, wv)
+    where = (right, left)
+    local = [pltpu.make_async_copy(own[k], piece(k, outs[k], seq, rep), lsem.at[k]) for k in range(4)]
+
+    def origin(way, s):
+        return ring_seq(pos - s) if way == 0 else ring_seq(pos + s)
+
+    def hop(way, s, k, src=None):
+        block = piece(k, outs[k], origin(way, s), rep)
+        return remote(block if src is None else src, block, send.at[way, s, k], recv.at[way, s, k], where[way])
+
+    def share(way, s, k, src=None):
+        block = piece(k, outs[k], origin(way, s), rep)
+        return remote(block if src is None else src, block, ssend.at[way, s, k], srecv.at[way, s, k], twin)
+
+    def share_in(way, s, k):
+        block = piece(k, outs[k], origin(way, s), 1 - rep)
+        return remote(block, block, ssend.at[way, s, k], srecv.at[way, s, k], twin)
+
+    for k in range(4):
+        hop(0, 0, k, own[k]).start()
+        hop(1, 0, k, own[k]).start()
+        share(0, 0, k, own[k]).start()
+        local[k].start()
+
+    def step(s, _):
+        for k in range(4):
+            for way in range(2):
+                last = 8 if way == 0 else 7
+
+                @pl.when(s <= last)
+                def _():
+                    block = piece(k, outs[k], origin(way, s), rep)
+                    remote(block, block, send.at[way, s - 1, k], recv.at[way, s - 1, k], where[way]).wait_recv()
+
+                    @pl.when(s < last)
+                    def _():
+                        hop(way, s, k).start()
+
+                    share(way, s, k).start()
+        return 0
+
+    lax.fori_loop(1, 9, step, 0)
+    for k in range(4):
+        local[k].wait()
+        hop(0, 0, k, own[k]).wait_send()
+        hop(1, 0, k, own[k]).wait_send()
+        share(0, 0, k, own[k]).wait_send()
+        share_in(0, 0, k).wait_recv()
+
+    def finish(s, _):
+        for k in range(4):
+            for way in range(2):
+                last = 8 if way == 0 else 7
+
+                @pl.when(s <= last)
+                def _():
+                    @pl.when(s < last)
+                    def _():
+                        hop(way, s, k).wait_send()
+
+                    share(way, s, k).wait_send()
+                    share_in(way, s, k).wait_recv()
+
+        return 0
+
+    lax.fori_loop(1, 9, finish, 0)
+
+
+def gather_weights(wa, wu, wd, wv):
+    d = wa.shape[2]
+    ff = wu.shape[1]
+    vm = pl.BlockSpec(memory_space=pltpu.VMEM)
+    anyw = pl.BlockSpec(memory_space=pl.ANY)
+    dma = pltpu.SemaphoreType.DMA
+    return pl.pallas_call(
+        gather_kernel,
+        in_specs=[vm] * 4,
+        out_specs=[anyw] * 4,
+        out_shape=[sds((4, d, d), BF16), sds((d, ff), BF16), sds((ff, d), BF16), sds((d, 128), F32)],
+        scratch_shapes=[
+            pltpu.VMEM((4, d // RING, d // 2), F32),
+            pltpu.VMEM((d // RING, ff // 2), F32),
+            pltpu.VMEM((4, d // RING, d // 2), BF16),
+            pltpu.VMEM((d // RING, ff // 2), BF16),
+            pltpu.VMEM((ff // (2 * RING), d), BF16),
+            dma((4,)),
+            dma((4,)),
+            dma((2, 9, 4)),
+            dma((2, 9, 4)),
+            dma((2, 9, 4)),
+            dma((2, 9, 4)),
+        ],
+        compiler_params=pltpu.CompilerParams(collective_id=5, has_side_effects=True, vmem_limit_bytes=VMEM_LIMIT),
+        name="gather_weights",
+    )(wa, wu, wd, wv)
+
+
+def adam_refs(grad, w, m, v, wo, mo, vo, rate):
+    moment = BETA_ONE * m[...] + (1.0 - BETA_ONE) * grad
+    second = BETA_TWO * v[...] + (1.0 - BETA_TWO) * grad * grad
+    first_hat = moment * (1.0 / (1.0 - BETA_ONE**STEP))
+    second_hat = second * (1.0 / (1.0 - BETA_TWO**STEP))
+    wo[...] = w[...] - rate * (first_hat / (jnp.sqrt(second_hat) + ADAM_EPS) + DECAY_RATE * w[...])
+    mo[...] = moment
+    vo[...] = second
+
+
+def scatter_kernel(
+    ga, gu, gd, gv, *rest
+):
+    state, rest = rest[:12], rest[12:]
+    news, rest = rest[:12], rest[12:]
+    mine, rest = rest[:4], rest[4:]
+    twins, rest = rest[:4], rest[4:]
+    inbox, rest = rest[:4], rest[4:]
+    first, rest = rest[:4], rest[4:]
+    fa, fu, lsem, tsend, trecv, send, recv, fsem = rest
+    grads = (ga, gu, gd, gv)
+    seq = lax.axis_index("seq")
+    rep = lax.axis_index("rep")
+    pos = ring_pos(seq)
+    right, left, twin = {"seq": ring_seq(pos + 1)}, {"seq": ring_seq(pos - 1)}, {"rep": 1 - rep}
+    where = (left, right)
+    greet([right, left, twin])
+
+    def chip(j):
+        return ring_seq(pos + 8 - j)
+
+    def load(j, k):
+        return pltpu.make_async_copy(piece(k, grads[k], chip(j), rep), mine[k].at[j], lsem.at[j, k])
+
+    def give(j, k):
+        return remote(piece(k, grads[k], chip(j), 1 - rep), twins[k].at[j], tsend.at[j, k], trecv.at[j, k], twin)
+
+    def start_all(j, _):
+        for k in range(4):
+            for jj in (j, 15 - j):
+                give(jj, k).start()
+                load(jj, k).start()
+        return 0
+
+    lax.fori_loop(0, 8, start_all, 0)
+
+    def slot(way, s):
+        return lax.rem(17 - s, RING) if way == 0 else s
+
+    def hop(way, s, k, src):
+        return remote(src, inbox[k].at[way, s], send.at[way, s, k], recv.at[way, s, k], where[way])
+
+    def ready(j, k):
+        load(j, k).wait()
+        give(j, k).wait()
+
+    def one(way, s, k):
+        j = slot(way, s)
+        ready(j, k)
+        own = mine[k][pl.ds(j, 1)].astype(F32) + twins[k][pl.ds(j, 1)].astype(F32)
+
+        @pl.when(s == 1)
+        def _():
+            first[k][pl.ds(way, 1)] = own.astype(first[k].dtype)
+            hop(way, 1, k, first[k].at[way]).start()
+
+        @pl.when(s > 1)
+        def _():
+            hop(way, s - 1, k, first[k].at[way]).wait_recv()
+            box = inbox[k].at[way]
+            box[pl.ds(s - 1, 1)] = (own + box[pl.ds(s - 1, 1)].astype(F32)).astype(first[k].dtype)
+            hop(way, s, k, inbox[k].at[way, s - 1]).start()
+
+    def step(s, _):
+        for k in range(4):
+            one(0, s, k)
+
+            @pl.when(s < 8)
+            def _():
+                one(1, s, k)
+
+        return 0
+
+    lax.fori_loop(1, 9, step, 0)
+    sums = []
+    for k in range(4):
+        ready(8, k)
+        hop(0, 8, k, first[k].at[0]).wait_recv()
+        hop(1, 7, k, first[k].at[1]).wait_recv()
+        sums.append(
+            (mine[k][8].astype(F32) + twins[k][8].astype(F32))
+            + (inbox[k][0, 8].astype(F32) + inbox[k][1, 7].astype(F32))
+        )
+    w, m, v = state[0::3], state[1::3], state[2::3]
+    wo, mo, vo = news[0::3], news[1::3], news[2::3]
+    ra, ru = w[0].shape[1], w[1].shape[0]
+    ha, hu = w[0].shape[2] // 2, w[1].shape[1] // 2
+    fa[0] = sums[0]
+    fu[0] = sums[1]
+    back = (
+        remote(fa.at[0, :, at(1 - rep, ra, 8), :], fa.at[1, :, at(1 - rep, ra, 8), :], fsem.at[0], fsem.at[1], twin),
+        remote(fu.at[0, at(1 - rep, ru, 8), :], fu.at[1, at(1 - rep, ru, 8), :], fsem.at[2], fsem.at[3], twin),
+    )
+    for c in back:
+        c.start()
+    adam_refs(sums[2], w[2], m[2], v[2], wo[2], mo[2], vo[2], LEARN_RATE)
+    adam_refs(sums[3], w[3], m[3], v[3], wo[3], mo[3], vo[3], VECTOR_RATE)
+    for c in back:
+        c.wait()
+    mine_a, mine_u = at(rep, ra, 8), at(rep, ru, 8)
+    for side in range(2):
+        ca, cu = pl.ds(side * ha, ha), pl.ds(side * hu, hu)
+        pick = jnp.where(rep == side, 0, 1)
+        for q in range(4):
+            adam_refs(fa[pick, q, mine_a, :], *(r.at[q, :, ca] for r in (w[0], m[0], v[0], wo[0], mo[0], vo[0])), LEARN_RATE)
+        adam_refs(fu[pick, mine_u, :], *(r.at[:, cu] for r in (w[1], m[1], v[1], wo[1], mo[1], vo[1])), LEARN_RATE)
+
+    def done(s, _):
+        for k in range(4):
+            hop(0, s, k, first[k].at[0]).wait_send()
+
+            @pl.when(s < 8)
+            def _():
+                hop(1, s, k, first[k].at[1]).wait_send()
+
+        return 0
+
+    lax.fori_loop(1, 9, done, 0)
+
+
+def scatter_step(ga, gu, gd, gv, state):
+    d = ga.shape[2]
+    ff = gu.shape[1]
+    vm = pl.BlockSpec(memory_space=pltpu.VMEM)
+    anyw = pl.BlockSpec(memory_space=pl.ANY)
+    dma = pltpu.SemaphoreType.DMA
+    blocks = [((4, d // RING, d // 2), BF16), ((d // RING, ff // 2), BF16), ((ff // (2 * RING), d), BF16), ((d // (2 * RING), 128), F32)]
+    return pl.pallas_call(
+        scatter_kernel,
+        in_specs=[anyw] * 4 + [vm] * 12,
+        out_specs=[vm] * 12,
+        out_shape=[sds(x.shape, F32) for x in state],
+        scratch_shapes=[pltpu.VMEM((RING, *s), t) for s, t in blocks]
+        + [pltpu.VMEM((RING, *s), t) for s, t in blocks]
+        + [pltpu.VMEM((2, 9, *s), t) for s, t in blocks]
+        + [pltpu.VMEM((2, *s), t) for s, t in blocks]
+        + [pltpu.VMEM((2, *blocks[0][0]), F32), pltpu.VMEM((2, *blocks[1][0]), F32)]
+        + [dma((RING, 4)), dma((RING, 4)), dma((RING, 4)), dma((2, 9, 4)), dma((2, 9, 4)), dma((4,))],
+        compiler_params=pltpu.CompilerParams(collective_id=6, has_side_effects=True, vmem_limit_bytes=VMEM_LIMIT),
+        name="scatter_step",
+    )(ga, gu, gd, gv, *state)
+
+
+def stack_tall(x):
+    return jnp.concatenate([x[:, c : c + 128] for c in range(0, x.shape[1], 128)], axis=0)
+
+
+def unstack(x, k):
+    return jnp.concatenate([x[c * M : (c + 1) * M] for c in range(k)], axis=1)
+
+
+def pad_rows(x, r):
+    return jnp.pad(x, ((0, r - x.shape[0]), (0, 0))) if r > x.shape[0] else x
+
+
 def adam_step(weight, grad_vec, moment, second, rate_value):
     moment_new = BETA_ONE * moment + (1.0 - BETA_ONE) * grad_vec
     second_new = BETA_TWO * second + (1.0 - BETA_TWO) * grad_vec * grad_vec
@@ -593,76 +1133,72 @@
     return (weight_new, moment_new, second_new)
 
 
-def halos(cells, index, count):
-    left = lax.ppermute(cells[-RAD:], "seq", [(i, (i + 1) % count) for i in range(count)])
-    right = lax.ppermute(cells[:RAD], "seq", [((i + 1) % count, i) for i in range(count)])
-    left = jnp.where(index > 0, left, jnp.zeros_like(left))
-    right = jnp.where(index < count - 1, right, jnp.zeros_like(right))
-    return left, right
-
-
 def per_device(tokens, cotangent, attn_w, w_up, w_down, vectors, attn_m, attn_v, up_m, up_v, down_m, down_v, vec_m, vec_v):
     both = ("seq", "rep")
     x = tokens[0]
     dy = cotangent[0]
     t, d = x.shape
-    count = lax.axis_size("seq")
-    index = lax.axis_index("seq")
-    rows_dev = max(M // count, 1)
-    per_mark = count * rows_dev // M
-    seg_len = t * count // M
-
-    w_attn = lax.all_gather(attn_w.astype(BF16), both, axis=1, tiled=True)
-    up = lax.all_gather(w_up.astype(BF16), both, axis=0, tiled=True)
-    down = lax.all_gather(w_down.astype(BF16), both, axis=0, tiled=True)
-    vec = lax.all_gather(vectors.astype(BF16), both, axis=0, tiled=True)
+    n = lax.axis_size("seq")
+    rows_dev = max(M // n, 1)
+    seg_len = t * n // M
+    ring = n == RING and lax.axis_size("rep") == 2
+
+    if ring:
+        wide = [jnp.pad(a, ((0, 0), (0, 128 - a.shape[1]))) for a in (vectors, vec_m, vec_v)]
+        w_attn, up, down, vec = gather_weights(attn_w, w_up, w_down, wide[0])
+        vec = vec.astype(BF16)
+    else:
+        w_attn = lax.all_gather(attn_w.astype(BF16), both, axis=1, tiled=True)
+        up = lax.all_gather(w_up.astype(BF16), both, axis=0, tiled=True)
+        down = lax.all_gather(w_down.astype(BF16), both, axis=0, tiled=True)
+        vec = lax.all_gather(vectors.astype(BF16), both, axis=0, tiled=True)
     vec_t = jnp.transpose(vec.astype(F32))
     gains = jnp.concatenate([vec_t[:2], jnp.zeros((6, d), F32)], axis=0)
-    taps = jnp.concatenate([vec_t[2:], jnp.zeros((7, d), F32)], axis=0)
+    taps = jnp.concatenate([vec_t[2 : 2 + KC], jnp.zeros((7, d), F32)], axis=0)
 
     h1, q, k, v, means = project(x, w_attn, gains)
-    marks = lax.all_gather(means, "seq", axis=0)
-    marks = jnp.transpose(marks.reshape(count, 2, 4, d), (1, 0, 2, 3)).reshape(2, M, count * 4 // M, d)
-    marks = jnp.mean(marks, axis=2).astype(BF16)
-    mq, mk = marks[0], marks[1]
-    vl, vr = halos(v, index, count)
+    mq, mk, vl, vr = exchange_marks(means, v, n)
     f, e, u, zt = attend(q, k, v, mq, mk)
-    u, zt = lax.psum((u, zt), "seq")
     a, p, zs, azs, t2s, t3s = pinv(mq, mk)
+    r = padded_rows(7 * M, n)
+    uz = sum_over_seq(pad_rows(jnp.concatenate([stack_tall(u), zt], axis=0), r), n, 2)
+    u, zt = unstack(uz, 6), uz[6 * M : 7 * M]
     out, act, da, h2, mix, dx, dmix, dqf, gw, dkt, dg2 = middle(
         x, dy, f, q, v, vl, vr, w_attn[3], up, down, gains, taps, mk, u, zt, p
     )
-    gw = lax.psum(gw, "seq")
-    gl, gr = halos(dmix, index, count)
+    r = padded_rows(6 * M, n)
+    gw, gl, gr = sum_over_seq(pad_rows(stack_tall(gw), r), n, 3, dmix)
+    gw = unstack(gw, 6)
     dot_xla = functools.partial(jnp.einsum, "ta,tb->ab", preferred_element_type=F32)
     g_down = dot_xla(act, dy).astype(BF16)
     g_up = dot_xla(h2, da).astype(BF16)
     g_o = dot_xla(mix, dx)
-    dqt_a, dkt_a = pinv_back(mq, mk, (a, p, zs, azs, t2s, t3s), gw, u, zt, 1.0 / count)
+    dqt_a, dkt_a = pinv_back(mq, mk, (a, p, zs, azs, t2s, t3s), gw, u, zt, 1.0 / n)
     dv, dkb, dqt, dtap = back(e, k, v, vl, vr, dmix, gl, gr, taps, mq, u, zt, p, gw)
-    spread_marks = jnp.stack([dqt + dqt_a, dkt + dkt_a])
-    spread_marks = jnp.repeat(spread_marks, per_mark, axis=1).reshape(2, count, rows_dev, d)
-    spread_marks = jnp.transpose(spread_marks, (1, 0, 2, 3))
-    own = lax.psum_scatter(spread_marks, "seq", scatter_dimension=0, tiled=True)[0]
-    own = jnp.pad(own, ((0, 0), (0, 4 - rows_dev), (0, 0))).reshape(8, d)
+    own = own_marks(dqt, dkt, dqt_a, dkt_a, n)
     dq, dk, ig, dg1 = last(x, dx, dqf, dkb, dv, own, w_attn, gains, seg_len, rows_dev)
     g_q = dot_xla(h1, dq) * QK_SCALE
     g_k = dot_xla(h1, dk) * QK_SCALE
     g_v = dot_xla(h1, dv)
     g_attn = jnp.stack([g_q, g_k, g_v, g_o]).astype(BF16)
-    g_vec = jnp.transpose(jnp.concatenate([dg1[:1], dg2[:1], dtap[:KC]], axis=0))
-    red_attn = lax.psum_scatter(g_attn, both, scatter_dimension=1, tiled=True).astype(F32)
-    red_up = lax.psum_scatter(g_up, both, scatter_dimension=0, tiled=True).astype(F32)
-    red_down = lax.psum_scatter(g_down, both, scatter_dimension=0, tiled=True).astype(F32)
-    red_vec = lax.psum_scatter(g_vec, both, scatter_dimension=0, tiled=True)
-    return (
-        out[None],
-        ig[None],
-        *adam_step(attn_w, red_attn, attn_m, attn_v, LEARN_RATE),
-        *adam_step(w_up, red_up, up_m, up_v, LEARN_RATE),
-        *adam_step(w_down, red_down, down_m, down_v, LEARN_RATE),
-        *adam_step(vectors, red_vec, vec_m, vec_v, VECTOR_RATE),
-    )
+    g_vec = jnp.concatenate([dg1[:1], dg2[:1], dtap[:KC]], axis=0)
+    if ring:
+        g_vec = jnp.transpose(pad_rows(g_vec, 128))
+        state = (attn_w, attn_m, attn_v, w_up, up_m, up_v, w_down, down_m, down_v, *wide)
+        news = scatter_step(g_attn, g_up, g_down, g_vec, state)
+        news = tuple(news[:9]) + tuple(a[:, : vectors.shape[1]] for a in news[9:])
+    else:
+        red_attn = lax.psum_scatter(g_attn, both, scatter_dimension=1, tiled=True).astype(F32)
+        red_up = lax.psum_scatter(g_up, both, scatter_dimension=0, tiled=True).astype(F32)
+        red_down = lax.psum_scatter(g_down, both, scatter_dimension=0, tiled=True).astype(F32)
+        red_vec = lax.psum_scatter(jnp.transpose(g_vec), both, scatter_dimension=0, tiled=True)
+        news = (
+            *adam_step(attn_w, red_attn, attn_m, attn_v, LEARN_RATE),
+            *adam_step(w_up, red_up, up_m, up_v, LEARN_RATE),
+            *adam_step(w_down, red_down, down_m, down_v, LEARN_RATE),
+            *adam_step(vectors, red_vec, vec_m, vec_v, VECTOR_RATE),
+        )
+    return (out[None], ig[None], *news)
 
 
 def solution(mesh):

time: 1200 us -> 558 us (0.47)
  waiting for transfers between devices: 708 us -> 0 us
  Pallas kernels: 219 us -> 462 us
  blocking collectives: 161 us -> 0 us
  local copies, waits for them, and re-layouts: 22.8 us -> 44.9 us
  other arithmetic: 20 us -> 4.01 us
  between operations: 14.8 us -> 1.49 us
    unnamed x13 -> x0, waiting for transfers between devices: 282 us -> none
    pallas_call x0 -> x6, Pallas kernels: none -> 243 us  [the longest x1 91.6 us: scatter_step(): pl.pallas_call(scatter_kernel, in_specs=[anyw] * 4 + [vm] * 12, out_specs...]
    reduce_scatter x2 -> x0, waiting for transfers between devices: 222 us -> none  [the longest x1 112 us: per_device(): lax.psum_scatter(g_down, both, scatter_dimension=0, tiled=True).astype(F32)]
    psum x2 -> x0, waiting for transfers between devices: 178 us -> none  [the longest x1 96.1 us: per_device(): gw = lax.psum(gw, 'seq')]
    all_gather x2 -> x0, blocking collectives: 83.9 us -> none  [the longest x1 43.8 us: per_device(): vec = lax.all_gather(vectors.astype(BF16), both, axis=0, tiled=True)]
    psum x1 -> x0, blocking collectives: 76.8 us -> none  [per_device(): u, zt = lax.psum((u, zt), 'seq')]
    all_gather x3 -> x0, waiting for transfers between devices: 18.9 us -> none  [the longest x1 18.9 us: per_device(): w_attn = lax.all_gather(attn_w.astype(BF16), both, axis=1, tiled=True)]
    unnamed x52 -> x79, local copies, waits for them, and re-layouts: 14.3 us -> 31.4 us
  transfers between devices with their start and end apart: 14 -> 0, of which waited for: 10 -> 0; matrix products, arithmetic and copies ran while one was open for 6% -> 0% of each run, Pallas kernels for 3% -> 0%
where the time goes in v2:
time: 558 us; the launch traced here: 551 us
  Pallas kernels  462 us (83%)
  local copies, waits for them, and re-layouts  44.9 us (8%)
  matrix products  39.2 us (7%)
    pallas_call x1, Pallas kernels, middle(): pl.pallas_call(middle_kernel, grid=(t // tile,), in_specs=[r, r, r, r, wh...  97.7 us
    pallas_call x1, Pallas kernels, scatter_step(): pl.pallas_call(scatter_kernel, in_specs=[anyw] * 4 + [vm] * 12, out_specs...  91.6 us
    pallas_call x1, Pallas kernels, gather_weights(): pl.pallas_call(gather_kernel, in_specs=[vm] * 4, out_specs=[anyw] * 4, ou...  90.1 us
    pallas_call x1, Pallas kernels, back(): pl.pallas_call(back_kernel, grid=(t // tile,), in_specs=[r, r, whole((t,...  44.9 us
    pallas_call x2, Pallas kernels, sum_over_seq(): pl.pallas_call(functools.partial(sum_kernel, n=n, with_halo=with_halo), i...  38.4 us
    unnamed x79, local copies, waits for them, and re-layouts  31.4 us
    pallas_call x1, Pallas kernels, pinv_back(): pl.pallas_call(functools.partial(pinv_back_kernel, inv_n=inv_n), in_specs...  22.3 us
    pallas_call x1, Pallas kernels, last(): pl.pallas_call(functools.partial(last_kernel, seg_len=seg_len, rows_dev=r...  16.5 us

profile of v2, /device:TPU:0, one launch (start us, length us, event | category | flops | bytes accessed | tf_op | source)
XLA Modules:
  0.0 551.2 jit_solution(15724769665387753861)
XLA Ops:
  0.6 1.3 pad.20.wv.rest_9_
  2.0 90.1 %gather_weights.1 = (bf16[4,768,768]{2,1,0:T(8,128)(2,1)}, bf16[768,3072]{1,0:T(8,128)(2,1)}, bf16[3072,768]{1,0:T(8,128)(2,1)}, f32[768,128]{1,0:T(8,128)}) custom-call(f32[4,24,768]{2,1,0:T(8,128)} %rest_0_.1, f32[24,3072]{1,0:T(8,128)} %rest_3_.1, f32[96,768]{1,0:T(8,128)} %rest_6_.1, f32[24,128]{1,0:T(8,128)} %pad.20.wv.rest_9_), custom_call_target="tpu_custom_call" | custom-call | tf_op jit(solution)/shard_map/gather_weights/pallas_call | solution.py:937
  92.0 1.1 copy.32
  93.2 1.3 slice_select_fusion.gain_ref
  94.5 13.1 %project.1 = (bf16[2048,768]{1,0:T(8,128)(2,1)}, bf16[2048,768]{1,0:T(8,128)(2,1)}, bf16[2048,768]{1,0:T(8,128)(2,1)}, bf16[2048,768]{1,0:T(8,128)(2,1)}, f32[8,768]{1,0:T(8,128)}) custom-call(bf16[2048,768]{1,0:T(8,128)(2,1)} %bitcast.35, bf16[4,768,768]{2,1,0:T(8,128)(2,1)} %get-tuple-element.73.w_ref, f32[8,768]{1,0:T(8,128)} %slice_select_fusion.gain_ref), custom_call_target="tpu_custom_call" | custom-call | tf_op jit(solution)/shard_map/project/pallas_call | solution.py:143
  107.7 12.4 %exchange_marks.1 = (bf16[64,768]{1,0:T(8,128)(2,1)}, bf16[64,768]{1,0:T(8,128)(2,1)}, bf16[16,768]{1,0:T(8,128)(2,1)}, bf16[16,768]{1,0:T(8,128)(2,1)}) custom-call(f32[8,768]{1,0:T(8,128)} %get-tuple-element.78.mean_ref, bf16[2048,768]{1,0:T(8,128)(2,1)} %get-tuple-element.77.v_ref), custom_call_target="tpu_custom_call" | custom-call | tf_op jit(solution)/shard_map/exchange_marks/pallas_call | solution.py:677
  120.0 12.5 %attend.1 = (bf16[2048,768]{1,0:T(8,128)(2,1)}, bf16[2048,768]{1,0:T(8,128)(2,1)}, f32[64,768]{1,0:T(8,128)}, f32[64,128]{1,0:T(8,128)}) custom-call(bf16[2048,768]{1,0:T(8,128)(2,1)} %get-tuple-element.75.q_ref, bf16[2048,768]{1,0:T(8,128)(2,1)} %get-tuple-element.76.k_ref, bf16[2048,768]{1,0:T(8,128)(2,1)} %get-tuple-element.77.v_ref, ...), custom_call_target="tpu_custom_call" | custom-call | tf_op jit(solution)/shard_map/attend/pallas_call | solution.py:295
  132.5 0.8 constant_dynamic-update-slice_fusion.6
  133.3 0.8 constant_dynamic-update-slice_fusion.5
  134.0 0.8 constant_dynamic-update-slice_fusion.4
  134.8 0.8 constant_dynamic-update-slice_fusion.3
  135.6 0.8 constant_dynamic-update-slice_fusion.2
  136.3 0.8 constant_dynamic-update-slice_fusion.1
  137.1 0.8 constant_dynamic-update-slice_fusion
  137.8 0.7 pad.21.x_ref
  138.6 20.8 %sum_over_seq.2 = f32[512,128]{1,0:T(8,128)} custom-call(f32[512,128]{1,0:T(8,128)} %pad.21.x_ref), custom_call_target="tpu_custom_call" | custom-call | tf_op jit(solution)/shard_map/sum_over_seq/pallas_call | solution.py:748
  159.4 0.8 constant_dynamic-update-slice_fusion.12
  160.2 0.8 constant_dynamic-update-slice_fusion.11
  160.9 0.8 constant_dynamic-update-slice_fusion.10
  161.7 0.8 constant_dynamic-update-slice_fusion.9
  162.5 0.8 constant_dynamic-update-slice_fusion.8
  163.2 1.4 fusion.5
  164.6 12.1 %pinv.1 = (f32[64,768]{1,0:T(8,128)}, f32[64,768]{1,0:T(8,128)}, f32[6,64,768]{2,1,0:T(8,128)}, f32[6,64,768]{2,1,0:T(8,128)}, f32[6,64,768]{2,1,0:T(8,128)}, /*index=5*/f32[6,64,768]{2,1,0:T(8,128)}) custom-call(bf16[64,768]{1,0:T(8,128)(2,1)} %get-tuple-element.79.mq_ref, bf16[64,768]{1,0:T(8,128)(2,1)} %get-tuple-element.80.mk_ref), custom_call_target="tpu_custom_call" | custom-call | tf_op jit(solution)/shard_map/pinv/pallas_call | solution.py:190
  176.7 2.4 slice_bitcast_fusion.wo_ref
  179.7 97.7 %middle.1 = (bf16[2048,768]{1,0:T(8,128)(2,1)}, bf16[2048,3072]{1,0:T(8,128)(2,1)}, bf16[2048,3072]{1,0:T(8,128)(2,1)}, bf16[2048,768]{1,0:T(8,128)(2,1)}, bf16[...) custom-call(bf16[2048,768]{1,0:T(8,128)(2,1)} %bitcast.36, ...), custom_call_target="tpu_custom_call" | custom-call | tf_op jit(solution)/shard_map/middle/pallas_call | solution.py:452
  277.4 0.8 constant_dynamic-update-slice_fusion.18
  278.2 0.8 constant_dynamic-update-slice_fusion.17
  278.9 0.8 constant_dynamic-update-slice_fusion.16
  279.7 0.8 constant_dynamic-update-slice_fusion.15
  280.4 0.8 constant_dynamic-update-slice_fusion.14
  281.2 0.8 constant_dynamic-update-slice_fusion.13.x_ref
  282.6 17.6 %sum_over_seq.3 = (f32[384,128]{1,0:T(8,128)}, bf16[16,768]{1,0:T(8,128)(2,1)}, bf16[16,768]{1,0:T(8,128)(2,1)}) custom-call(f32[384,128]{1,0:T(8,128)} %copy-done.9, bf16[2048,768]{1,0:T(8,128)(2,1)} %get-tuple-element.93.rest_0_.g_ref), custom_call_target="tpu_custom_call" | custom-call | tf_op jit(solution)/shard_map/sum_over_seq/pallas_call | solution.py:748
  300.2 0.8 constant_dynamic-update-slice_fusion.24
  301.0 0.8 constant_dynamic-update-slice_fusion.23
  301.7 0.8 constant_dynamic-update-slice_fusion.22
  302.5 0.8 constant_dynamic-update-slice_fusion.21
  303.3 0.8 constant_dynamic-update-slice_fusion.20
  304.0 0.8 constant_dynamic-update-slice_fusion.19.gw_ref
  304.8 0.7 copy-done.4
  305.5 22.3 %pinv_back.1 = (f32[64,768]{1,0:T(8,128)}, f32[64,768]{1,0:T(8,128)}) custom-call(bf16[64,768]{1,0:T(8,128)(2,1)} %get-tuple-element.79.mq_ref, bf16[64,768]{1,0:T(8,128)(2,1)} %get-tuple-element.80.mk_ref, f32[64,768]{1,0:T(8,128)} %get-tuple-element.102.a_ref, f32[64,768]{1,0:T(8,128)} %get-tuple-element.88.p_ref, f32[6,64,768]{2,1,0:T(8,128)} %get-tuple-element.103.z_ref, ...), custom_call_target="tpu_custom_call" | custom-call | tf_op jit(solution)/shard_map/pinv_back/pallas_call | solution.py:244
  327.8 44.9 %back.1 = (bf16[2048,768]{1,0:T(8,128)(2,1)}, bf16[2048,768]{1,0:T(8,128)(2,1)}, f32[64,768]{1,0:T(8,128)}, f32[40,768]{1,0:T(8,128)}) custom-call(bf16[2048,768]{1,0:T(8,128)(2,1)} %get-tuple-element.92.e_ref, bf16[2048,768]{1,0:T(8,128)(2,1)} %get-tuple-element.76.k_ref, bf16[2048,768]{1,0:T(8,128)(2,1)} %get-tuple-element.77.v_ref, ...), custom_call_target="tpu_custom_call" | custom-call | tf_op jit(solution)/shard_map/back/pallas_call | solution.py:522
  372.6 10.1 %own_marks.1.own_ref = f32[8,768]{1,0:T(8,128)} custom-call(f32[64,768]{1,0:T(8,128)} %get-tuple-element.100.dq_ref, f32[64,768]{1,0:T(8,128)} %get-tuple-element.101.dk_ref, f32[64,768]{1,0:T(8,128)} %get-tuple-element.107.dqa_ref, f32[64,768]{1,0:T(8,128)} %get-tuple-element.108.dka_ref), custom_call_target="tpu_custom_call" | custom-call | tf_op jit(solution)/shard_map/own_marks/pallas_call | solution.py:788
  382.8 16.5 %last.1 = (bf16[2048,768]{1,0:T(8,128)(2,1)}, bf16[2048,768]{1,0:T(8,128)(2,1)}, bf16[2048,768]{1,0:T(8,128)(2,1)}, f32[8,768]{1,0:T(8,128)}) custom-call(bf16[2048,768]{1,0:T(8,128)(2,1)} %bitcast.37, bf16[2048,768]{1,0:T(8,128)(2,1)} %get-tuple-element.90.dx_ref, bf16[2048,768]{1,0:T(8,128)(2,1)} %get-tuple-element.91.dqf_ref, ...), custom_call_target="tpu_custom_call" | custom-call | tf_op jit(solution)/shard_map/last/pallas_call | solution.py:573
  399.3 0.7 slice.131
  400.1 0.7 slice.132
  401.0 0.8 pad_bitcast_fusion.gv
  401.8 15.8 %convolution_convert_fusion.1.gu = bf16[768,3072]{1,0:T(8,128)(2,1)} fusion(bf16[2048,768]{1,0:T(8,128)(2,1)} %get-tuple-element.114, bf16[2048,3072]{1,0:T(8,128)(2,1)} %get-tuple-element.115), kind=kOutput, calls=%fused_computation.1 | convolution fusion | flops 9666035712 | bytes 20447232 | tf_op jit(solution)/shard_map/ta,tb->ab/dot_general | solution.py:1174
  417.7 2.7 fusion.2
  420.5 2.7 fusion.3
  423.2 2.7 fusion
  426.0 2.7 fusion.1
  428.8 2.6 pad_maximum_fusion.ga
  431.4 0.7 copy-done
  432.1 12.5 %convolution_convert_fusion.gd = bf16[3072,768]{1,0:T(8,128)(2,1)} fusion(bf16[2048,3072]{1,0:T(8,128)(2,1)S(1)} %bitcast.44, bf16[1,2048,768]{2,1,0:T(8,128)(2,1)S(1)} %copy-done), kind=kOutput, calls=%fused_computation | convolution fusion | flops 9666035712 | bytes 20447232 | tf_op jit(solution)/shard_map/ta,tb->ab/dot_general | solution.py:1173
  445.9 91.6 %scatter_step.1 = (f32[4,24,768]{2,1,0:T(8,128)}, f32[4,24,768]{2,1,0:T(8,128)}, f32[4,24,768]{2,1,0:T(8,128)}, f32[24,3072]{1,0:T(8,128)}, f32[24,3072]{1,0:T(8...) custom-call(bf16[4,768,768]{2,1,0:T(8,128)(2,1)} %pad_maximum_fusion, ...), custom_call_target="tpu_custom_call" | custom-call | tf_op jit(solution)/shard_map/scatter_step/pallas_call | solution.py:1097
  537.5 1.8 copy.67
  539.3 1.7 copy.68
  541.0 1.7 copy.69
  542.6 1.7 copy.70
  544.3 1.7 copy.71
  546.0 0.7 copy.72
  546.8 0.7 copy.73
  547.5 0.7 copy.74
  548.2 0.7 copy.75
  (55 shorter events, 4.7 us)
Async XLA Ops:
  164.6 15.1 %copy-start.3 = (f32[64,768]{1,0:T(8,128)}, f32[64,768]{1,0:T(8,128)S(1)}, u32[]{:S(2)}) copy-start(f32[64,768]{1,0:T(8,128)S(1)} %get-tuple-element.133.u_ref) | copy-start | bytes 589828
  282.0 0.7 copy-start.9
  304.8 0.7 copy-start.4
  382.8 18.0 %copy-start.10 = (f32[40,768]{1,0:T(8,128)S(1)}, f32[40,768]{1,0:T(8,128)}, u32[]{:S(2)}) copy-start(f32[40,768]{1,0:T(8,128)} %get-tuple-element.119) | copy-start | bytes 368644
  401.8 15.8 %copy-start.16 = (bf16[2048,768]{1,0:T(8,128)(2,1)S(1)}, bf16[2048,768]{1,0:T(8,128)(2,1)}, u32[]{:S(2)}) copy-start(bf16[2048,768]{1,0:T(8,128)(2,1)} %get-tuple-element.110) | copy-start | bytes 9437188
  401.8 15.8 %copy-start.19 = (bf16[2048,768]{1,0:T(8,128)(2,1)S(1)}, bf16[2048,768]{1,0:T(8,128)(2,1)}, u32[]{:S(2)}) copy-start(bf16[2048,768]{1,0:T(8,128)(2,1)} %get-tuple-element.111) | copy-start | bytes 9437188
  417.7 2.7 copy-start.18
  420.4 2.8 copy-start.2
  420.4 5.5 %copy-start.17 = (bf16[2048,768]{1,0:T(8,128)(2,1)S(1)}, bf16[2048,768]{1,0:T(8,128)(2,1)}, u32[]{:S(2)}) copy-start(bf16[2048,768]{1,0:T(8,128)(2,1)} %get-tuple-element.113) | copy-start | bytes 9437188
  420.5 10.9 %slice-start = ((s8[12582912]{0:T(1024)(128)(4,1)}), s8[4194304]{0:T(1024)(128)(4,1)S(1)}, s32[]{:S(2)}) async-start(s8[12582912]{0:T(1024)(128)(4,1)} %bitcast.43), calls=%async_computation | async-start | bytes 8388608
  423.2 2.8 copy-start.1
  423.2 8.2 %slice-start.1 = ((s8[12582912]{0:T(1024)(128)(4,1)}), s8[4194304]{0:T(1024)(128)(4,1)S(1)}, s32[]{:S(2)}) async-start(s8[12582912]{0:T(1024)(128)(4,1)} %bitcast.43), calls=%async_computation.1 | async-start | bytes 8388608
  426.0 5.4 slice-start.2
  428.7 3.4 copy-start
  432.1 12.5 %copy-start.11 = (f32[24,35]{1,0:T(8,128)S(1)}, f32[24,35]{1,0:T(8,128)}, u32[]{:S(2)}) copy-start(f32[24,35]{1,0:T(8,128)} %param.26) | copy-start | bytes 10084
  432.1 13.1 %copy-start.12 = (f32[24,35]{1,0:T(8,128)S(1)}, f32[24,35]{1,0:T(8,128)}, u32[]{:S(2)}) copy-start(f32[24,35]{1,0:T(8,128)} %param.27) | copy-start | bytes 10084
  537.4 8.6 %copy-start.8 = (f32[24,3072]{1,0:T(8,128)S(1)}, f32[24,3072]{1,0:T(8,128)}, u32[]{:S(2)}) copy-start(f32[24,3072]{1,0:T(8,128)} %get-tuple-element.155) | copy-start | bytes 884740
  537.4 9.3 %copy-start.7 = (f32[96,768]{1,0:T(8,128)S(1)}, f32[96,768]{1,0:T(8,128)}, u32[]{:S(2)}) copy-start(f32[96,768]{1,0:T(8,128)} %get-tuple-element.156) | copy-start | bytes 884740
  537.4 10.0 %copy-start.6 = (f32[96,768]{1,0:T(8,128)S(1)}, f32[96,768]{1,0:T(8,128)}, u32[]{:S(2)}) copy-start(f32[96,768]{1,0:T(8,128)} %get-tuple-element.157) | copy-start | bytes 884740
  537.4 10.7 %copy-start.5 = (f32[96,768]{1,0:T(8,128)S(1)}, f32[96,768]{1,0:T(8,128)}, u32[]{:S(2)}) copy-start(f32[96,768]{1,0:T(8,128)} %get-tuple-element.158) | copy-start | bytes 884740
  537.5 11.5 %copy-start.15 = (f32[24,128]{1,0:T(8,128)S(1)}, f32[24,128]{1,0:T(8,128)}, u32[]{:S(2)}) copy-start(f32[24,128]{1,0:T(8,128)} %get-tuple-element.129) | copy-start | bytes 36868
  537.5 12.0 %copy-start.14 = (f32[24,128]{1,0:T(8,128)S(1)}, f32[24,128]{1,0:T(8,128)}, u32[]{:S(2)}) copy-start(f32[24,128]{1,0:T(8,128)} %get-tuple-element.130) | copy-start | bytes 36868
  537.5 12.6 %copy-start.13 = (f32[24,128]{1,0:T(8,128)S(1)}, f32[24,128]{1,0:T(8,128)}, u32[]{:S(2)}) copy-start(f32[24,128]{1,0:T(8,128)} %get-tuple-element.131) | copy-start | bytes 36868

commit v3 on v1

v3 whole, which is shorter than its diff:
```python
import functools

import jax
import jax.numpy as jnp
from jax import lax
from jax.experimental import pallas as pl
from jax.experimental.pallas import tpu as pltpu
from jax.sharding import PartitionSpec as P

H = 12
HD = 64
M = 64
KC = 33
NSITER = 6
STEP = 10
EPS_NORM = 1e-05
BETA_ONE = 0.9
BETA_TWO = 0.999
ADAM_EPS = 1e-08
LEARN_RATE = 0.03
VECTOR_RATE = 0.15
DECAY_RATE = 0.1

F32 = jnp.float32
BF16 = jnp.bfloat16
GROUP = 256
NG = 3
RAD = 16
QK_SCALE = HD ** (-0.25)
HI = lax.Precision.HIGHEST
VMEM_LIMIT = 58 * 1024 * 1024


def dot(a, b, precision=None):
    return lax.dot_general(a, b, (((1,), (0,)), ((), ())), precision=precision, preferred_element_type=F32)


def dot_nt(a, b, precision=None):
    return lax.dot_general(a, b, (((1,), (1,)), ((), ())), precision=precision, preferred_element_type=F32)


def dot_tn(a, b, precision=None):
    return lax.dot_general(a, b, (((0,), (0,)), ((), ())), precision=precision, preferred_element_type=F32)


def head_mask(shape=(GROUP, GROUP)):
    rows = lax.broadcasted_iota(jnp.int32, shape, 0)
    cols = lax.broadcasted_iota(jnp.int32, shape, 1)
    return lax.shift_right_logical(rows, 6) == lax.shift_right_logical(cols, 6)


def spread(wide):
    tall = jnp.concatenate([wide, wide, wide, wide], axis=0)
    return jnp.where(head_mask(), tall, jnp.zeros_like(tall))


def collect(full):
    kept = jnp.where(head_mask(), full, jnp.zeros_like(full))
    return (kept[0:64] + kept[64:128]) + (kept[128:192] + kept[192:256])


def flip(wide):
    turned = jnp.transpose(spread(wide))
    return (turned[0:64] + turned[64:128]) + (turned[128:192] + turned[192:256])


def gs(g):
    return slice(g * GROUP, (g + 1) * GROUP)


def half_reduce(x, op, init):
    parts = []
    for c in range(x.shape[1] // 128):
        col = x[:, c * 128 : (c + 1) * 128]
        low = lax.broadcasted_iota(jnp.int32, col.shape, 1) < 64
        a = op(jnp.where(low, col, init), axis=1, keepdims=True)
        b = op(jnp.where(low, init, col), axis=1, keepdims=True)
        parts.append(jnp.where(low, a, b))
    return jnp.concatenate(parts, axis=1)


def normalize(x):
    center = x - jnp.mean(x, axis=-1, keepdims=True)
    inv = lax.rsqrt(jnp.mean(center * center, axis=-1, keepdims=True) + EPS_NORM)
    return center * inv, inv


def norm_back(up, normal, inv, gain):
    scaled = up * gain
    centered = scaled - jnp.mean(scaled, axis=-1, keepdims=True)
    return inv * (centered - normal * jnp.mean(scaled * normal, axis=-1, keepdims=True))


def rowsum8(x):
    return jnp.sum(x.reshape(x.shape[0] // 8, 8, x.shape[1]), axis=0)


def gelu_parts(a):
    z = jnp.abs(a)
    t = 1.0 / (1.0 + (0.3275911 * 0.7071067811865476) * z)
    e = jnp.exp(-0.5 * a * a)
    poly = t * (0.127414796 + t * (-0.142248368 + t * (0.7107068705 + t * (-0.7265760135 + t * 0.5307027145))))
    tail = poly * e
    phi = jnp.where(a >= 0, 1.0 - tail, tail)
    return a * phi, phi + a * (e * 0.3989422804014327)


def whole(shape):
    zeros = (0,) * len(shape)
    return pl.BlockSpec(shape, lambda i: zeros, pipeline_mode=pl.Buffered(1))


def rows(tile, width):
    return pl.BlockSpec((tile, width), lambda i: (i, 0))


def sds(shape, dtype):
    return jax.ShapeDtypeStruct(shape, dtype)


def params():
    return pltpu.CompilerParams(dimension_semantics=("arbitrary",), vmem_limit_bytes=VMEM_LIMIT)


def widen(zt, g):
    return jnp.concatenate(
        [jnp.broadcast_to(zt[:, h : h + 1], (M, HD)) for h in range(4 * g, 4 * g + 4)], axis=1
    )


def u_group(ref, g):
    return jnp.concatenate([ref[2 * g * M : (2 * g + 1) * M, :], ref[(2 * g + 1) * M : (2 * g + 2) * M, :]], axis=1)


def zt_group(ref, g):
    return widen(ref[6 * M : 7 * M, :], g)


def put_tall(ref, g, wide):
    ref[2 * g * M : (2 * g + 1) * M, :] = wide[:, :128]
    ref[(2 * g + 1) * M : (2 * g + 2) * M, :] = wide[:, 128:]


def padded_rows(r, n):
    return -(-r // (8 * n)) * 8 * n


MESH = pl.DeviceIdType.MESH
DMA = pltpu.SemaphoreType.DMA
VM = pl.BlockSpec(memory_space=pltpu.VMEM)
ANYW = pl.BlockSpec(memory_space=pl.ANY)


def remote(src, dst, send, recv, where):
    return pltpu.make_async_remote_copy(
        src_ref=src, dst_ref=dst, send_sem=send, recv_sem=recv, device_id=where, device_id_type=MESH
    )


def greet(me, n, others):
    bar = pltpu.get_barrier_semaphore()

    def hello(j, _):
        pl.semaphore_signal(bar, inc=1, device_id={"seq": lax.rem(me + j, n)}, device_id_type=MESH)
        return 0

    lax.fori_loop(1, n, hello, 0)
    for peer in others:
        pl.semaphore_signal(bar, inc=1, device_id=peer, device_id_type=MESH)
    pl.semaphore_wait(bar, n - 1 + len(others))


def each_peer(me, n, make, act):
    def body(j, _):
        act(make(j, lax.rem(me + j, n)))
        return 0

    lax.fori_loop(1, n, body, 0)


def halo_copies(body_ref, left_ref, right_ref, me, n, sems):
    t = body_ref.shape[0]
    right = {"seq": lax.rem(me + 1, n)}
    left = {"seq": lax.rem(me + n - 1, n)}
    return (
        remote(body_ref.at[pl.ds(t - RAD, RAD)], left_ref, sems.at[0], sems.at[1], right),
        remote(body_ref.at[pl.ds(0, RAD)], right_ref, sems.at[2], sems.at[3], left),
    )


def mask_halos(left_ref, right_ref, me, n):
    left_ref[...] = jnp.where(me > 0, left_ref[...], jnp.zeros_like(left_ref))
    right_ref[...] = jnp.where(me < n - 1, right_ref[...], jnp.zeros_like(right_ref))


class SeqSum:
    def __init__(self, me, n, x, out, slots, total, sems):
        self.me, self.n, self.x, self.out, self.slots, self.total, self.sems = me, n, x, out, slots, total, sems
        self.chunk = x.shape[0] // n
        self.here = pl.ds(pl.multiple_of(me * self.chunk, 8), self.chunk)

    def first(self, j, peer):
        src = self.x.at[pl.ds(pl.multiple_of(peer * self.chunk, 8), self.chunk)]
        return remote(src, self.slots.at[self.me], self.sems.at[0, j], self.sems.at[1, j], {"seq": peer})

    def second(self, j, peer):
        return remote(self.total, self.out.at[self.here], self.sems.at[2, j], self.sems.at[3, j], {"seq": peer})

    def start(self):
        each_peer(self.me, self.n, self.first, lambda c: c.start())
        self.slots[pl.ds(self.me, 1)] = self.x[self.here, :][None]

    def turn(self):
        each_peer(self.me, self.n, self.first, lambda c: c.wait())
        summed = lax.fori_loop(1, self.n, lambda i, acc: acc + self.slots[i], self.slots[0])
        self.total[...] = summed
        each_peer(self.me, self.n, self.second, lambda c: c.start())
        self.out[self.here, :] = summed

    def finish(self):
        each_peer(self.me, self.n, self.second, lambda c: c.wait())

    @staticmethod
    def scratch(r, n):
        return [pltpu.VMEM((n, r // n, 128), F32), pltpu.VMEM((r // n, 128), F32), DMA((4, n))]


RING = 16


def ring_pos(seq):
    x = lax.rem(seq, 2)
    y = lax.rem(lax.div(seq, 2), 2)
    z = lax.div(seq, 4)
    col = x * 3 + y * (1 - 2 * x)
    return col * 4 + z + lax.rem(col, 2) * (3 - 2 * z)


def ring_seq(pos):
    pos = lax.rem(pos + 2 * RING, RING)
    col = lax.div(pos, 4)
    zz = lax.rem(pos, 4)
    z = zz + lax.rem(col, 2) * (3 - 2 * zz)
    x = lax.div(col, 2)
    y = lax.rem(lax.div(col + 1, 2), 2)
    return z * 4 + y * 2 + x


def at(i, size, unit):
    return pl.ds(pl.multiple_of(i * size, unit), size)


STACK, HALF, ROWS, LINES = range(4)


def piece(kind, ref, seq, rep):
    if kind == STACK:
        half = ref.shape[2] // 2
        return ref.at[:, at(seq, ref.shape[1] // RING, 16), at(rep, half, 128)]
    if kind == HALF:
        half = ref.shape[1] // 2
        return ref.at[at(seq, ref.shape[0] // RING, 16), at(rep, half, 128)]
    return ref.at[at(seq * 2 + rep, ref.shape[0] // (2 * RING), 8 if kind == LINES else 16), :]


class Place:
    def __init__(self):
        self.seq = lax.axis_index("seq")
        self.rep = lax.axis_index("rep")
        self.pos = ring_pos(self.seq)
        self.right = {"seq": ring_seq(self.pos + 1)}
        self.left = {"seq": ring_seq(self.pos - 1)}
        self.twin = {"rep": 1 - self.rep}


class GatherRing:
    def __init__(self, place, kinds, outs, own, sems):
        self.place, self.kinds, self.outs, self.own = place, kinds, outs, own
        self.send, self.recv, self.ssend, self.srecv = sems
        self.where = (place.right, place.left)

    def block(self, way, s, k, rep):
        p = self.place
        origin = ring_seq(p.pos - s) if way == 0 else ring_seq(p.pos + s)
        return piece(self.kinds[k], self.outs[k], origin, rep)

    def hop(self, way, s, k, src=None):
        b = self.block(way, s, k, self.place.rep)
        return remote(b if src is None else src, b, self.send.at[way, s, k], self.recv.at[way, s, k], self.where[way])

    def arrival(self, way, s, k):
        b = self.block(way, s, k, self.place.rep)
        return remote(b, b, self.send.at[way, s - 1, k], self.recv.at[way, s - 1, k], self.where[way])

    def share(self, way, s, k, src=None):
        b = self.block(way, s, k, self.place.rep)
        return remote(b if src is None else src, b, self.ssend.at[way, s, k], self.srecv.at[way, s, k], self.place.twin)

    def shared(self, way, s, k):
        b = self.block(way, s, k, 1 - self.place.rep)
        return remote(b, b, self.ssend.at[way, s, k], self.srecv.at[way, s, k], self.place.twin)

    def start(self):
        for k in range(len(self.kinds)):
            self.hop(0, 0, k, self.own[k]).start()
            self.hop(1, 0, k, self.own[k]).start()
            self.share(0, 0, k, self.own[k]).start()

    def step(self, s):
        for k in range(len(self.kinds)):
            for way in range(2):
                last = 8 - way

                @pl.when(s <= last)
                def _():
                    self.arrival(way, s, k).wait_recv()

                    @pl.when(s < last)
                    def _():
                        self.hop(way, s, k).start()

                    self.share(way, s, k).start()

    def finish(self):
        for k in range(len(self.kinds)):
            self.hop(0, 0, k, self.own[k]).wait_send()
            self.hop(1, 0, k, self.own[k]).wait_send()
            self.share(0, 0, k, self.own[k]).wait_send()
            self.shared(0, 0, k).wait_recv()

        def body(s, _):
            for k in range(len(self.kinds)):
                for way in range(2):
                    last = 8 - way

                    @pl.when(s <= last)
                    def _():
                        @pl.when(s < last)
                        def _():
                            self.hop(way, s, k).wait_send()

                        self.share(way, s, k).wait_send()
                        self.shared(way, s, k).wait_recv()

            return 0

        lax.fori_loop(1, 9, body, 0)

    @staticmethod
    def scratch(k):
        return [DMA((2, 9, k))] * 4


class ScatterRing:
    def __init__(self, place, kinds, grads, mine, twins, inbox, first, sems):
        self.place, self.kinds, self.grads = place, kinds, grads
        self.mine, self.twins, self.inbox, self.opening = mine, twins, inbox, first
        self.lsem, self.tsend, self.trecv, self.send, self.recv = sems
        self.where = (place.left, place.right)

    def load(self, j, k):
        src = piece(self.kinds[k], self.grads[k], ring_seq(self.place.pos + 8 - j), self.place.rep)
        return pltpu.make_async_copy(src, self.mine[k].at[j], self.lsem.at[j, k])

    def give(self, j, k):
        src = piece(self.kinds[k], self.grads[k], ring_seq(self.place.pos + 8 - j), 1 - self.place.rep)
        return remote(src, self.twins[k].at[j], self.tsend.at[j, k], self.trecv.at[j, k], self.place.twin)

    def hop(self, way, s, k, src):
        return remote(src, self.inbox[k].at[way, s], self.send.at[way, s, k], self.recv.at[way, s, k], self.where[way])

    def start(self):
        def body(j, _):
            for k in range(len(self.kinds)):
                for jj in (j, 15 - j):
                    self.give(jj, k).start()
                    self.load(jj, k).start()
            return 0

        lax.fori_loop(0, 8, body, 0)

    def terms(self, j, k):
        self.load(j, k).wait()
        self.give(j, k).wait()
        return self.mine[k][pl.ds(j, 1)].astype(F32) + self.twins[k][pl.ds(j, 1)].astype(F32)

    def one(self, way, s, k):
        own = self.terms(lax.rem(17 - s, RING) if way == 0 else s, k)
        first = self.opening[k]

        @pl.when(s == 1)
        def _():
            first[pl.ds(way, 1)] = own.astype(first.dtype)
            self.hop(way, 1, k, first.at[way]).start()

        @pl.when(s > 1)
        def _():
            self.hop(way, s - 1, k, first.at[way]).wait_recv()
            box = self.inbox[k].at[way]
            box[pl.ds(s - 1, 1)] = (own + box[pl.ds(s - 1, 1)].astype(F32)).astype(first.dtype)
            self.hop(way, s, k, self.inbox[k].at[way, s - 1]).start()

    def step(self, s):
        for k in range(len(self.kinds)):
            self.one(0, s, k)

            @pl.when(s < 8)
            def _():
                self.one(1, s, k)

    def total(self, k):
        own = self.terms(8, k)[0]
        first = self.opening[k]
        self.hop(0, 8, k, first.at[0]).wait_recv()
        self.hop(1, 7, k, first.at[1]).wait_recv()
        return own + (self.inbox[k][0, 8].astype(F32) + self.inbox[k][1, 7].astype(F32))

    def finish(self):
        def body(s, _):
            for k in range(len(self.kinds)):
                self.hop(0, s, k, self.opening[k].at[0]).wait_send()

                @pl.when(s < 8)
                def _():
                    self.hop(1, s, k, self.opening[k].at[1]).wait_send()

            return 0

        lax.fori_loop(1, 9, body, 0)

    @staticmethod
    def scratch(blocks):
        k = len(blocks)
        return (
            [pltpu.VMEM((RING, *s), t) for s, t in blocks]
            + [pltpu.VMEM((RING, *s), t) for s, t in blocks]
            + [pltpu.VMEM((2, 9, *s), t) for s, t in blocks]
            + [pltpu.VMEM((2, *s), t) for s, t in blocks]
            + [DMA((RING, k))] * 3
            + [DMA((2, 9, k))] * 2
        )


def swap_rows(total, out, place, sems):
    rows_own = total.shape[-2] // 2
    half = total.shape[-1]
    theirs, mine = at(1 - place.rep, rows_own, 8), at(place.rep, rows_own, 8)
    cols = at(place.rep, half, 128)
    if len(total.shape) == 3:
        out[:, :, cols] = total[:, mine, :]
        return remote(total.at[:, theirs, :], out.at[:, :, cols], sems.at[0], sems.at[1], place.twin)
    out[:, cols] = total[mine, :]
    return remote(total.at[theirs, :], out.at[:, cols], sems.at[0], sems.at[1], place.twin)


CHUNK = 64
CTILE = 256


def fill_inner(ext, body_ref, start):
    count = ext.shape[1]
    rows_in = pl.ds(pl.multiple_of(start - RAD, RAD), count)
    for c in range(ext.shape[0]):
        ext[c] = body_ref[rows_in, c * 128 : (c + 1) * 128].astype(F32)


def fill_edge(ext, body_ref, left_ref, right_ref, first):
    tile = ext.shape[1] - 2 * RAD
    t = body_ref.shape[0]
    start = pl.multiple_of(jnp.where(first, 0, t - tile), tile)
    for c in range(ext.shape[0]):
        cols = slice(c * 128, (c + 1) * 128)
        ext[c, RAD : RAD + tile, :] = body_ref[pl.ds(start, tile), cols].astype(F32)
        ext[c, 0:RAD, :] = jnp.where(first, left_ref[:, cols], body_ref[t - tile - RAD : t - tile, cols]).astype(F32)
        ext[c, RAD + tile :, :] = jnp.where(first, body_ref[tile : tile + RAD, cols], right_ref[:, cols]).astype(F32)


def conv_forward(ext, tap_ref, out, row0):
    def step(r, _):
        base = pl.multiple_of(r * CHUNK, CHUNK)
        for c in range(ext.shape[0]):
            cols = slice(c * 128, (c + 1) * 128)
            acc = jnp.zeros((CHUNK, 128), F32)
            for b in range(8):
                reach = 4 if b == 0 else 3
                win = ext[c, pl.ds(base + b, CHUNK + 8 * reach), :]
                for m in range(reach + 1):
                    o = 8 * m + b
                    acc = acc + tap_ref[o : o + 1, cols] * win[8 * m : 8 * m + CHUNK]
            out[pl.ds(pl.multiple_of(row0 + base, CHUNK), CHUNK), cols] = acc.astype(out.dtype)
        return 0

    lax.fori_loop(0, CTILE // CHUNK, step, 0)


def conv_backward(vext, gext, tap_ref, out, tapacc, row0):
    def step(r, _):
        base = pl.multiple_of(r * CHUNK, CHUNK)
        for c in range(vext.shape[0]):
            cols = slice(c * 128, (c + 1) * 128)
            acc = jnp.zeros((CHUNK, 128), F32)
            here = gext[c, pl.ds(base + RAD, CHUNK), :]
            for b in range(8):
                reach = 4 if b == 0 else 3
                win = gext[c, pl.ds(base + b, CHUNK + 8 * reach), :]
                for m in range(reach + 1):
                    o = KC - 1 - (8 * m + b)
                    acc = acc + tap_ref[o : o + 1, cols] * win[8 * m : 8 * m + CHUNK]
                win = vext[c, pl.ds(base + b, CHUNK + 8 * reach), :]
                for m in range(reach + 1):
                    o = 8 * m + b
                    tapacc[o, :, cols] += rowsum8(here * win[8 * m : 8 * m + CHUNK])
            out[pl.ds(pl.multiple_of(row0 + base, CHUNK), CHUNK), cols] = acc
        return 0

    lax.fori_loop(0, CTILE // CHUNK, step, 0)


def wide_eye():
    lane = lax.broadcasted_iota(jnp.int32, (M, GROUP), 1) & 63
    return jnp.where(lane == lax.broadcasted_iota(jnp.int32, (M, GROUP), 0), 1.0, 0.0)


def head_sums(row):
    ones = jnp.where(head_mask(), 1.0, 0.0)
    return dot(jnp.broadcast_to(row, (8, GROUP)), ones, HI)[0:1]


def pinv_begin(mq_ref, mk_ref, a_ref, z_ref):
    for g in range(NG):
        s = dot_nt(mq_ref[:, gs(g)], spread(mk_ref[:, gs(g)]))
        e = jnp.exp(s - half_reduce(s, jnp.max, -jnp.inf))
        a = e / half_reduce(e, jnp.sum, 0.0)
        a_ref[:, gs(g)] = a
        col = jnp.sum(a, axis=0, keepdims=True)
        z_ref[0, :, gs(g)] = flip(a) / jnp.sqrt(head_sums(col * col))


def pinv_step(it, a_ref, z_ref, az_ref, t2_ref, t3_ref):
    eye = wide_eye()
    z = [z_ref[it, :, gs(g)] for g in range(NG)]
    az = [dot(a_ref[:, gs(g)], spread(z[g]), HI) for g in range(NG)]
    t2 = [15.0 * eye - dot(az[g], spread(7.0 * eye - az[g]), HI) for g in range(NG)]
    t3 = [13.0 * eye - dot(az[g], spread(t2[g]), HI) for g in range(NG)]
    for g in range(NG):
        z_ref[it + 1, :, gs(g)] = 0.25 * dot(z[g], spread(t3[g]), HI)
        az_ref[it, :, gs(g)] = az[g]
        t2_ref[it, :, gs(g)] = t2[g]
        t3_ref[it, :, gs(g)] = t3[g]


def pinv_back_step(it, a_ref, z_ref, az_ref, t2_ref, t3_ref, gz_ref, da_ref):
    eye = wide_eye()
    R = range(NG)
    gz = [gz_ref[:, gs(g)] for g in R]
    z = [z_ref[it, :, gs(g)] for g in R]
    az = [az_ref[it, :, gs(g)] for g in R]
    t2 = [t2_ref[it, :, gs(g)] for g in R]
    t3 = [t3_ref[it, :, gs(g)] for g in R]
    bg = [spread(0.25 * gz[g]) for g in R]
    d3 = [dot(0.25 * gz[g], spread(z[g]), HI) for g in R]
    baz = [spread(az[g]) for g in R]
    d2 = [-dot(d3[g], baz[g], HI) for g in R]
    d1 = [-dot(d2[g], baz[g], HI) for g in R]
    daz = [-dot(t2[g], spread(d3[g]), HI) - dot(7.0 * eye - az[g], spread(d2[g]), HI) - d1[g] for g in R]
    for g in R:
        da_ref[:, gs(g)] += dot(z[g], spread(daz[g]), HI)
        gz_ref[:, gs(g)] = dot(t3[g], bg[g], HI) + dot(daz[g], spread(a_ref[:, gs(g)]), HI)


def pinv_back_end(g, a_ref, gz_ref, da_ref):
    a = a_ref[:, gs(g)]
    gz = gz_ref[:, gs(g)]
    col = jnp.sum(a, axis=0, keepdims=True)
    bound = jnp.sqrt(head_sums(col * col))
    tot = head_sums(jnp.sum(gz * a, axis=0, keepdims=True))
    full = flip(da_ref[:, gs(g)]) + gz / bound - (tot / (bound * bound * bound)) * col
    return a * (full - half_reduce(full * a, jnp.sum, 0.0))


def gather_marks(slots, outs, n):
    per = 4 * n // M
    half = slots.shape[2]
    for out, base in zip(outs, (0, 4)):
        if per == 1:
            got = [slots[i].astype(F32) for i in range(n)]
            for h in range(2):
                tall = jnp.concatenate([x[8 * h + base : 8 * h + base + 4] for x in got], axis=0)
                out[:, h * half : (h + 1) * half] = tall.astype(BF16)
        else:
            for h in range(2):
                lines = []
                for m in range(M):
                    total = jnp.zeros((1, half), F32)
                    for s in range(per // 4):
                        part = slots[m * (per // 4) + s].astype(F32)[8 * h + base : 8 * h + base + 4]
                        total = total + jnp.sum(part, axis=0, keepdims=True)
                    lines.append(total * (1.0 / per))
                out[:, h * half : (h + 1) * half] = jnp.concatenate(lines, axis=0).astype(BF16)


class Refs:
    def __init__(self, refs):
        self.it = iter(refs)

    def __call__(self, count):
        return [next(self.it) for _ in range(count)]

    def one(self):
        return next(self.it)


def front_kernel(*refs, n, ring):
    take = Refs(refs)
    x_any = take.one()
    if ring:
        wa, wu, wd, wv = take(4)
        wqkv_o, wo_o, up_o, down_o = take(4)
    else:
        wq, vec = take(2)
    gains, taps = take(2)
    outs = take(7)
    mq, mk, uz, a_ref, z_ref, az_ref, t2_ref, t3_ref, vl, vr = take(10)
    xs = take.one()
    stage = take(7)
    h_s, q_s, k_s, v_s, conv_s, f_s, e_s = stage
    means, pay, slots, ext, bdk, bdq, uacc, zacc, upart = take(9)
    xsem, osem, msem, hsem = take(4)
    sum_bufs = take(3)
    me = lax.axis_index("seq")
    t, d = xs.shape
    half = d // 2
    load_x = pltpu.make_async_copy(x_any, xs, xsem.at[0])
    load_x.start()
    drains = [pltpu.make_async_copy(s, o, osem.at[i]) for i, (s, o) in enumerate(zip(stage, outs))]
    if ring:
        wq, vec, sa, su, so, cu, co, cd, psem, lsem = take(10)
        ring_one, ring_two = take(4), take(4)
        place = Place()
        greet(me, n, [place.twin])
        rep, seq = place.rep, place.seq
        rows_own, ff = d // (2 * RING), wu.shape[1]
        mine = at(rep, rows_own, 8)
        theirs = 1 - rep
        swaps = (
            remote(wa.at[0:3, :, at(theirs, half, 128)], sa.at[:, mine, :], psem.at[0], psem.at[1], place.twin),
            remote(wa.at[3, :, at(theirs, half, 128)], so.at[mine, :], psem.at[2], psem.at[3], place.twin),
            remote(wu.at[:, at(theirs, ff // 2, 128)], su.at[mine, :], psem.at[4], psem.at[5], place.twin),
        )
        for c in swaps:
            c.start()
        sa[:, mine, :] = wa[0:3, :, at(rep, half, 128)]
        so[mine, :] = wa[3, :, at(rep, half, 128)]
        su[mine, :] = wu[:, at(rep, ff // 2, 128)]
        vec[at(seq * 2 + rep, rows_own, 8), :] = wv[...]
        swaps[0].wait()
        wq[:, at(seq, 2 * rows_own, 16), at(rep, half, 128)] = sa[...].astype(BF16)
        first = GatherRing(place, (STACK, LINES), (wq, vec), (None, None), ring_one)
        first.start()
        cd[...] = wd[...].astype(BF16)
        swaps[1].wait()
        swaps[2].wait()
        co[...] = so[...].astype(BF16)
        cu[...] = su[...].astype(BF16)
        rest = GatherRing(place, (HALF, HALF, ROWS), (wo_o, up_o, down_o), (co, cu, cd), ring_two)
        local = [
            pltpu.make_async_copy(src, piece(kind, out, seq, rep), lsem.at[i])
            for i, (src, kind, out) in enumerate(zip(rest.own, rest.kinds, rest.outs))
        ]

        def go(s, _):
            first.step(s)
            return 0

        lax.fori_loop(1, 9, go, 0)
        rest.start()
        for c in local:
            c.start()
        first.finish()
        save_w = pltpu.make_async_copy(wq, wqkv_o, xsem.at[1])
        save_w.start()
    else:
        greet(me, n, [])

    def tick(cond, s):
        if ring:

            @pl.when(cond)
            def _():
                rest.step(s)

    turned = jnp.transpose(vec[...]).astype(BF16).astype(F32)
    gains[...] = turned[0:8]
    taps[...] = turned[2:42]
    load_x.wait()

    def project(i, _):
        here = pl.ds(pl.multiple_of(i * (t // 4), t // 4), t // 4)
        normal, _inv = normalize(xs[here, :].astype(F32))
        h = (normal * gains[0:1, :]).astype(BF16)
        h_s[here, :] = h
        q = (dot(h, wq[0]) * QK_SCALE).astype(BF16)
        q_s[here, :] = q
        means[pl.ds(i, 1), :] = jnp.mean(q.astype(F32), axis=0, keepdims=True)
        k = (dot(h, wq[1]) * QK_SCALE).astype(BF16)
        k_s[here, :] = k
        means[pl.ds(i + 4, 1), :] = jnp.mean(k.astype(F32), axis=0, keepdims=True)
        v_s[here, :] = dot(h, wq[2]).astype(BF16)
        tick((i == 1) | (i == 3), lax.div(i + 1, 2))
        return 0

    lax.fori_loop(0, 4, project, 0)

    pay[...] = jnp.concatenate([means[:, :half], means[:, half:]], axis=0).astype(BF16)

    def mark(j, peer):
        return remote(pay, slots.at[me], msem.at[0, j], msem.at[1, j], {"seq": peer})

    halos = halo_copies(v_s, vl, vr, me, n, hsem)
    for c in halos:
        c.start()
    each_peer(me, n, mark, lambda c: c.start())
    slots[pl.ds(me, 1)] = pay[...][None]
    for c in drains[:4]:
        c.start()

    def inner(i, _):
        fill_inner(ext, v_s, i * CTILE)
        conv_forward(ext, taps, conv_s, i * CTILE)
        tick((i == 3) | (i == 6), 2 + lax.div(i, 3))
        return 0

    lax.fori_loop(1, t // CTILE - 1, inner, 0)
    for c in halos:
        c.wait()
    mask_halos(vl, vr, me, n)

    def edge(i, _):
        fill_edge(ext, v_s, vl, vr, i == 0)
        conv_forward(ext, taps, conv_s, i * (t - CTILE))
        return 0

    lax.fori_loop(0, 2, edge, 0)
    drains[4].start()
    each_peer(me, n, mark, lambda c: c.wait())
    gather_marks(slots, (mq, mk), n)
    for g in range(NG):
        bdk[g] = spread(mk[:, gs(g)])
        bdq[g] = spread(mq[:, gs(g)])
    uacc[...] = jnp.zeros_like(uacc)
    zacc[...] = jnp.zeros_like(zacc)
    ones_bd = jnp.where(head_mask(), 1.0, 0.0).astype(BF16)

    def attend(i, _):
        here = pl.ds(pl.multiple_of(i * (t // 4), t // 4), t // 4)
        for g in range(NG):
            s = dot_nt(q_s[here, gs(g)], bdk[g])
            ex = jnp.exp(s - half_reduce(s, jnp.max, -jnp.inf))
            den = dot(ex.astype(BF16), ones_bd)
            f_s[here, gs(g)] = (ex / den).astype(BF16)
            e = jnp.exp(dot_nt(k_s[here, gs(g)], bdq[g])).astype(BF16)
            e_s[here, gs(g)] = e
            uacc[g] += dot_tn(e, v_s[here, gs(g)])
            zacc[g] += dot_tn(e, jnp.ones((t // 4, 128), BF16))
        tick((i == 1) | (i == 3), 5 + lax.div(i, 2))
        return 0

    lax.fori_loop(0, 4, attend, 0)
    for c in drains[5:]:
        c.start()
    lane = lax.broadcasted_iota(jnp.int32, (M, 128), 1)
    zt = jnp.zeros((M, 128), F32)
    for g in range(NG):
        put_tall(upart, g, collect(uacc[g]))
        for h in range(4):
            zt = zt + jnp.where(lane == 4 * g + h, zacc[g, h * 64 : h * 64 + 64, :], 0.0)
    upart[6 * M : 7 * M, :] = zt
    upart[7 * M :, :] = jnp.zeros((upart.shape[0] - 7 * M, 128), F32)
    summing = SeqSum(me, n, upart, uz, *sum_bufs)
    summing.start()
    pinv_begin(mq, mk, a_ref, z_ref)

    def newton(it, _):
        pinv_step(it, a_ref, z_ref, az_ref, t2_ref, t3_ref)
        return 0

    lax.fori_loop(0, NSITER // 2, newton, 0)
    if ring:
        rest.step(7)
    summing.turn()
    lax.fori_loop(NSITER // 2, NSITER, newton, 0)
    if ring:
        rest.step(8)
    summing.finish()
    for c in drains:
        c.wait()
    if ring:
        for c in local:
            c.wait()
        save_w.wait()
        rest.finish()


def front(x, weights, n, ring):
    t, d = x.shape
    if ring:
        wa, wu, wd, wv = weights
        ff = wu.shape[1]
        extra_out = [sds((3, d, d), BF16), sds((d, d), BF16), sds((d, ff), BF16), sds((ff, d), BF16)]
        rown = d // RING
        extra = [
            pltpu.VMEM((3, d, d), BF16),
            pltpu.VMEM((d, 128), F32),
            pltpu.VMEM((3, rown, d // 2), F32),
            pltpu.VMEM((rown, ff // 2), F32),
            pltpu.VMEM((rown, d // 2), F32),
            pltpu.VMEM((rown, ff // 2), BF16),
            pltpu.VMEM((rown, d // 2), BF16),
            pltpu.VMEM((ff // (2 * RING), d), BF16),
            DMA((6,)),
            DMA((3,)),
        ] + GatherRing.scratch(2) + GatherRing.scratch(3)
    else:
        extra_out, extra = [], []
    r = padded_rows(7 * M, n)
    big = sds((t, d), BF16)
    steps = sds((NSITER, M, d), F32)
    res = pl.pallas_call(
        functools.partial(front_kernel, n=n, ring=ring),
        in_specs=[ANYW] + [VM] * len(weights),
        out_specs=[ANYW] * len(extra_out) + [VM] * 2 + [ANYW] * 7 + [VM] * 10,
        out_shape=extra_out
        + [sds((8, d), F32), sds((40, d), F32)]
        + [big] * 7
        + [sds((M, d), BF16)] * 2
        + [sds((r, 128), F32), sds((M, d), F32), sds((NSITER + 1, M, d), F32), steps, steps, steps]
        + [sds((RAD, d), BF16)] * 2,
        scratch_shapes=[pltpu.VMEM((t, d), BF16)] * 8
        + [
            pltpu.VMEM((8, d), F32),
            pltpu.VMEM((16, d // 2), BF16),
            pltpu.VMEM((n, 16, d // 2), BF16),
            pltpu.VMEM((d // 128, CTILE + 2 * RAD, 128), F32),
            pltpu.VMEM((NG, GROUP, GROUP), BF16),
            pltpu.VMEM((NG, GROUP, GROUP), BF16),
            pltpu.VMEM((NG, GROUP, GROUP), F32),
            pltpu.VMEM((NG, GROUP, 128), F32),
            pltpu.VMEM((r, 128), F32),
            DMA((2,)),
            DMA((7,)),
            DMA((2, n)),
            DMA((4,)),
        ]
        + SeqSum.scratch(r, n)
        + extra,
        compiler_params=pltpu.CompilerParams(collective_id=1, has_side_effects=True, vmem_limit_bytes=VMEM_LIMIT),
        name="front",
    )(x, *weights)
    return res if ring else [None] * 4 + list(res)


FCHUNK = 512


def middle_kernel(
    x_ref, dy_ref, f_ref, q_ref, conv_ref, wo_ref, up_ref, down_ref, gain_ref, mk_ref, uz_ref, z_ref,
    out_ref, act_ref, da_ref, h2_ref, mix_ref, dx_ref, dmix_ref, dqf_ref, gw_ref, dkt_ref, dg_ref,
    wbd, gwacc, dktacc, dgacc, oacc, hacc,
):
    i = pl.program_id(0)
    n = pl.num_programs(0)
    tile = x_ref.shape[0]
    d = x_ref.shape[1]

    @pl.when(i == 0)
    def _():
        gwacc[...] = jnp.zeros_like(gwacc)
        dktacc[...] = jnp.zeros_like(dktacc)
        dgacc[...] = jnp.zeros_like(dgacc)
        for g in range(NG):
            bv = u_group(uz_ref, g) / zt_group(uz_ref, g)
            wbd[g] = spread(dot(z_ref[NSITER, :, gs(g)], spread(bv), HI)).astype(BF16)

    for g in range(NG):
        mix_ref[:, gs(g)] = (dot(f_ref[:, gs(g)], wbd[g]) + conv_ref[:, gs(g)].astype(F32)).astype(BF16)
    x1 = x_ref[...].astype(F32) + dot(mix_ref[...], wo_ref[...])
    normal, inv = normalize(x1)
    gain = gain_ref[1:2, :]
    h2 = (normal * gain).astype(BF16)
    h2_ref[...] = h2
    dy = dy_ref[...]
    ff = up_ref.shape[1]
    for j in range(ff // FCHUNK):
        cols = slice(j * FCHUNK, (j + 1) * FCHUNK)
        a = dot(h2, up_ref[:, cols])
        act, slope = gelu_parts(a)
        act = act.astype(BF16)
        act_ref[:, cols] = act
        da = (dot_nt(dy, down_ref[cols, :]) * slope).astype(BF16)
        da_ref[:, cols] = da
        o = dot(act, down_ref[cols, :])
        h = dot_nt(da, up_ref[:, cols])
        if j == 0:
            oacc[...] = o
            hacc[...] = h
        else:
            oacc[...] += o
            hacc[...] += h
    out_ref[...] = (x1 + oacc[...]).astype(BF16)
    dh2 = hacc[...]
    dgacc[...] += rowsum8(dh2 * normal)
    dx1 = norm_back(dh2, normal, inv, gain) + dy.astype(F32)
    do = dx1.astype(BF16)
    dx_ref[...] = do
    dmix = dot_nt(do, wo_ref[...]).astype(BF16)
    dmix_ref[...] = dmix
    ones_bd = jnp.where(head_mask(), 1.0, 0.0).astype(BF16)
    for g in range(NG):
        dm = dmix[:, gs(g)]
        f = f_ref[:, gs(g)]
        df = dot_nt(dm, wbd[g])
        gwacc[g] += dot_tn(f, dm)
        ff32 = f.astype(F32)
        prod = df * ff32
        hi = prod.astype(BF16)
        lo = (prod - hi.astype(F32)).astype(BF16)
        ds = (ff32 * (df - (dot(hi, ones_bd) + dot(lo, ones_bd)))).astype(BF16)
        dqf_ref[:, gs(g)] = dot(ds, spread(mk_ref[:, gs(g)])).astype(BF16)
        dktacc[g] += dot_tn(ds, q_ref[:, gs(g)])

    @pl.when(i == n - 1)
    def _():
        for g in range(NG):
            put_tall(gw_ref, g, collect(gwacc[g]))
            dkt_ref[:, gs(g)] = collect(dktacc[g])
        if gw_ref.shape[0] > 6 * M:
            gw_ref[6 * M :] = jnp.zeros((gw_ref.shape[0] - 6 * M, 128), F32)
        dg_ref[...] = jnp.broadcast_to(jnp.sum(dgacc[...], axis=0, keepdims=True), (8, d))


def middle(x, dy, f, q, conv, wo, up, down, gains, mk, uz, z, gw_rows):
    t, d = x.shape
    ff = up.shape[1]
    tile = 256
    r = rows(tile, d)
    rf = rows(tile, ff)
    return pl.pallas_call(
        middle_kernel,
        grid=(t // tile,),
        in_specs=[r, r, r, r, r, whole((d, d)), whole(up.shape), whole(down.shape), whole(gains.shape), whole((M, d)),
                  whole(uz.shape), whole(z.shape)],
        out_specs=[r, rf, rf, r, r, r, r, r, whole((gw_rows, 128)), whole((M, d)), whole((8, d))],
        out_shape=[sds((t, d), BF16), sds((t, ff), BF16), sds((t, ff), BF16)] + [sds((t, d), BF16)] * 5
        + [sds((gw_rows, 128), F32), sds((M, d), F32), sds((8, d), F32)],
        scratch_shapes=[
            pltpu.VMEM((NG, GROUP, GROUP), BF16),
            pltpu.VMEM((NG, GROUP, GROUP), F32),
            pltpu.VMEM((NG, GROUP, GROUP), F32),
            pltpu.VMEM((8, d), F32),
            pltpu.VMEM((tile, d), F32),
            pltpu.VMEM((tile, d), F32),
        ],
        compiler_params=params(),
        name="middle",
    )(x, dy, f, q, conv, wo, up, down, gains, mk, uz, z)


def rear_kernel(*refs, n, ring):
    take = Refs(refs)
    bodies = take(4)
    if ring:
        grads = take(3)
    gw_part, uz, a_ref, z_ref, az_ref, t2_ref, t3_ref, mq, mk, vl, vr, taps, dkt_ref = take(13)
    dv_o, dkb_o, dtap, own = take(4)
    if ring:
        r_o, r_up, r_down = take(3)
    v_s, g_s, e_s, k_s = take(4)
    dv_s, dkb_s, dvc, vext, gext, tapacc, gl, gr, gw, gz, da, dubd, rowadd, dqtacc, bdq, pay, slots = take(17)
    isem, osem, hsem, wsem = take(4)
    sum_bufs = take(3)
    me = lax.axis_index("seq")
    t, d = v_s.shape
    loads = [pltpu.make_async_copy(b, s, isem.at[i]) for i, (b, s) in enumerate(zip(bodies, (v_s, g_s, e_s, k_s)))]
    for c in loads:
        c.start()
    if ring:
        mine, twins, inbox, opening = take(3), take(3), take(3), take(3)
        sems = take(5)
        fo, fu, fsem = take(3)
        place = Place()
        greet(me, n, [place.twin])
        ringer = ScatterRing(place, (HALF, HALF, ROWS), grads, mine, twins, inbox, opening, sems)
    else:
        greet(me, n, [])
    summing = SeqSum(me, n, gw_part, gw, *sum_bufs)
    loads[1].wait()
    halos = halo_copies(g_s, gl, gr, me, n, hsem)
    for c in halos:
        c.start()
    summing.start()
    if ring:
        ringer.start()

    def tick(cond, s):
        if ring:

            @pl.when(cond)
            def _():
                ringer.step(s)

    tapacc[...] = jnp.zeros_like(tapacc)
    loads[0].wait()

    def inner(i, _):
        fill_inner(vext, v_s, i * CTILE)
        fill_inner(gext, g_s, i * CTILE)
        conv_backward(vext, gext, taps, dvc, tapacc, i * CTILE)
        tick((i == 2) | (i == 4), lax.div(i, 2))

        @pl.when(i == 4)
        def _():
            summing.turn()

        return 0

    lax.fori_loop(1, t // CTILE - 1, inner, 0)
    tick(True, 3)
    for c in halos:
        c.wait()
    mask_halos(gl, gr, me, n)

    def edge(i, _):
        fill_edge(vext, v_s, vl, vr, i == 0)
        fill_edge(gext, g_s, gl, gr, i == 0)
        conv_backward(vext, gext, taps, dvc, tapacc, i * (t - CTILE))
        return 0

    lax.fori_loop(0, 2, edge, 0)
    dtap[...] = jnp.sum(tapacc[...], axis=1)
    tick(True, 4)
    summing.finish()
    for g in range(NG):
        z = zt_group(uz, g)
        bv = u_group(uz, g) / z
        gwg = u_group(gw, g)
        gz[:, gs(g)] = flip(dot_nt(gwg, spread(bv), HI))
        dbv = dot(flip(z_ref[NSITER, :, gs(g)]), spread(gwg), HI)
        dubd[g] = spread(dbv / z).astype(BF16)
        rowadd[g] = dot_nt(jnp.ones((8, GROUP), F32), spread(dbv * bv / z), HI)
        bdq[g] = spread(mq[:, gs(g)])
    da[...] = jnp.zeros_like(da)

    def newton(j, _):
        pinv_back_step(NSITER - 1 - j, a_ref, z_ref, az_ref, t2_ref, t3_ref, gz, da)
        tick((j == 1) | (j == 3), 5 + lax.div(j, 2))
        return 0

    lax.fori_loop(0, NSITER, newton, 0)
    loads[2].wait()
    loads[3].wait()
    dqtacc[...] = jnp.zeros_like(dqtacc)

    def through(i, _):
        here = pl.ds(pl.multiple_of(i * (t // 4), t // 4), t // 4)
        for g in range(NG):
            e = e_s[here, gs(g)]
            de = dot_nt(v_s[here, gs(g)], dubd[g]) - rowadd[g, 0:1, :]
            ds = (e.astype(F32) * de).astype(BF16)
            dv_s[here, gs(g)] = (dot(e, dubd[g]) + dvc[here, gs(g)]).astype(BF16)
            dkb_s[here, gs(g)] = dot(ds, bdq[g]).astype(BF16)
            dqtacc[g] += dot_tn(ds, k_s[here, gs(g)])
        tick((i == 0) | (i == 3), 7 + lax.div(i, 3))
        return 0

    lax.fori_loop(0, 4, through, 0)
    drains = [
        pltpu.make_async_copy(dv_s, dv_o, osem.at[0]),
        pltpu.make_async_copy(dkb_s, dkb_o, osem.at[1]),
    ]
    for c in drains:
        c.start()

    rows_dev = max(M // n, 1)
    per_mark = n * rows_dev // M
    if rows_dev < 4:
        pay[...] = jnp.zeros_like(pay)
    for g in range(NG):
        ds = pinv_back_end(g, a_ref, gz, da)
        dq = collect(dqtacc[g]) + dot(ds, spread(mk[:, gs(g)].astype(F32)), HI) * (1.0 / n)
        dk = dkt_ref[:, gs(g)] + dot(flip(ds), spread(mq[:, gs(g)].astype(F32)), HI) * (1.0 / n)
        for i in range(n):
            row = i * rows_dev // per_mark
            pay[i, 0:rows_dev, gs(g)] = dq[row : row + rows_dev]
            pay[i, 4 : 4 + rows_dev, gs(g)] = dk[row : row + rows_dev]

    def mark(j, peer):
        return remote(pay.at[peer], slots.at[me], wsem.at[0, j], wsem.at[1, j], {"seq": peer})

    each_peer(me, n, mark, lambda c: c.start())
    slots[pl.ds(me, 1)] = pay[pl.ds(me, 1)]
    if ring:
        fo[...] = ringer.total(0)
        fu[...] = ringer.total(1)
        back = (swap_rows(fo, r_o, place, fsem.at[0]), swap_rows(fu, r_up, place, fsem.at[1]))
        for c in back:
            c.start()
        r_down[...] = ringer.total(2)
    each_peer(me, n, mark, lambda c: c.wait())
    own[...] = lax.fori_loop(1, n, lambda i, acc: acc + slots[i], slots[0])
    for c in drains:
        c.wait()
    if ring:
        for c in back:
            c.wait()
        ringer.finish()


def rear(bodies, grads, gw, uz, a, z, az, t2, t3, mq, mk, vl, vr, taps, dkt, n):
    ring = grads is not None
    t, d = bodies[0].shape
    r = gw.shape[0]
    big = sds((t, d), BF16)
    outs = [big, big, sds((40, d), F32), sds((8, d), F32)]
    extra = []
    if ring:
        ff = grads[1].shape[1]
        own = d // (2 * RING)
        outs += [sds((own, d), F32), sds((own, ff), F32), sds((ff // (2 * RING), d), F32)]
        blocks = [((2 * own, d // 2), BF16), ((2 * own, ff // 2), BF16), ((ff // (2 * RING), d), BF16)]
        extra = ScatterRing.scratch(blocks) + [
            pltpu.VMEM((2 * own, d // 2), F32),
            pltpu.VMEM((2 * own, ff // 2), F32),
            DMA((2, 2)),
        ]
    ext = pltpu.VMEM((d // 128, CTILE + 2 * RAD, 128), F32)
    halo = pltpu.VMEM((RAD, d), BF16)
    small = pltpu.VMEM((M, d), F32)
    return pl.pallas_call(
        functools.partial(rear_kernel, n=n, ring=ring),
        in_specs=[ANYW] * (4 + (3 if ring else 0)) + [VM] * 13,
        out_specs=[ANYW] * 2 + [VM] * (len(outs) - 2),
        out_shape=outs,
        scratch_shapes=[pltpu.VMEM((t, d), BF16)] * 6
        + [
            pltpu.VMEM((t, d), F32),
            ext,
            ext,
            pltpu.VMEM((40, 8, d), F32),
            halo,
            halo,
            pltpu.VMEM((r, 128), F32),
            small,
            small,
            pltpu.VMEM((NG, GROUP, GROUP), BF16),
            pltpu.VMEM((NG, 8, GROUP), F32),
            pltpu.VMEM((NG, GROUP, GROUP), F32),
            pltpu.VMEM((NG, GROUP, GROUP), BF16),
            pltpu.VMEM((n, 8, d), F32),
            pltpu.VMEM((n, 8, d), F32),
            DMA((4,)),
            DMA((2,)),
            DMA((4,)),
            DMA((2, n)),
        ]
        + SeqSum.scratch(r, n)
        + extra,
        compiler_params=pltpu.CompilerParams(collective_id=2, has_side_effects=True, vmem_limit_bytes=VMEM_LIMIT),
        name="rear",
    )(*bodies, *(grads if ring else ()), gw, uz, a, z, az, t2, t3, mq, mk, vl, vr, taps, dkt)


def last_kernel(x_ref, dx_ref, dqf_ref, dkb_ref, dv_ref, own_ref, w_ref, gain_ref, dq_ref, dk_ref, ig_ref, dg_ref, dgacc, *, seg_len, rows_dev):
    i = pl.program_id(0)
    n = pl.num_programs(0)
    tile, d = x_ref.shape

    @pl.when(i == 0)
    def _():
        dgacc[...] = jnp.zeros_like(dgacc)

    at = i * rows_dev // 4
    scale = 1.0 / seg_len
    dq = (dqf_ref[...].astype(F32) + own_ref[pl.ds(at, 1), :] * scale).astype(BF16)
    dk = (dkb_ref[...].astype(F32) + own_ref[pl.ds(at + 4, 1), :] * scale).astype(BF16)
    dq_ref[...] = dq
    dk_ref[...] = dk
    dh = (dot_nt(dq, w_ref[0]) + dot_nt(dk, w_ref[1])) * QK_SCALE + dot_nt(dv_ref[...], w_ref[2])
    normal, inv = normalize(x_ref[...].astype(F32))
    dgacc[...] += rowsum8(dh * normal)
    ig = norm_back(dh, normal, inv, gain_ref[0:1, :]) + dx_ref[...].astype(F32)
    ig_ref[...] = ig.astype(BF16)

    @pl.when(i == n - 1)
    def _():
        dg_ref[...] = jnp.broadcast_to(jnp.sum(dgacc[...], axis=0, keepdims=True), (8, d))


def last(x, dx, dqf, dkb, dv, own, w_attn, gains, seg_len, rows_dev):
    t, d = x.shape
    tile = t // 4
    r = rows(tile, d)
    return pl.pallas_call(
        functools.partial(last_kernel, seg_len=seg_len, rows_dev=rows_dev),
        grid=(4,),
        in_specs=[r, r, r, r, r, whole((8, d)), whole(w_attn.shape), whole(gains.shape)],
        out_specs=[r, r, r, whole((8, d))],
        out_shape=[sds((t, d), BF16)] * 3 + [sds((8, d), F32)],
        scratch_shapes=[pltpu.VMEM((8, d), F32)],
        compiler_params=params(),
        name="last",
    )(x, dx, dqf, dkb, dv, own, w_attn, gains)


def adam_step(weight, grad_vec, moment, second, rate_value):
    moment_new = BETA_ONE * moment + (1.0 - BETA_ONE) * grad_vec
    second_new = BETA_TWO * second + (1.0 - BETA_TWO) * grad_vec * grad_vec
    first_hat = moment_new / (1.0 - BETA_ONE**STEP)
    second_hat = second_new / (1.0 - BETA_TWO**STEP)
    weight_new = weight - rate_value * (
        first_hat / (jnp.sqrt(second_hat) + ADAM_EPS) + DECAY_RATE * weight
    )
    return (weight_new, moment_new, second_new)


def tail_kernel(*refs, n):
    take = Refs(refs)
    grads = take(2)
    r_qkv, r_vec = take(2)
    mine, twins, inbox, opening = take(2), take(2), take(2), take(2)
    sems = take(5)
    fq, fsem = take(2)
    place = Place()
    greet(place.seq, n, [place.twin])
    ringer = ScatterRing(place, (STACK, LINES), grads, mine, twins, inbox, opening, sems)
    ringer.start()

    def go(s, _):
        ringer.step(s)
        return 0

    lax.fori_loop(1, 9, go, 0)
    fq[...] = ringer.total(0)
    back = swap_rows(fq, r_qkv, place, fsem)
    back.start()
    r_vec[...] = ringer.total(1)
    ringer.finish()
    back.wait()


def tail(g_qkv, g_vec, n):
    d = g_qkv.shape[1]
    own = d // (2 * RING)
    blocks = [((3, 2 * own, d // 2), BF16), ((own, 128), F32)]
    return pl.pallas_call(
        functools.partial(tail_kernel, n=n),
        in_specs=[ANYW] * 2,
        out_specs=[VM] * 2,
        out_shape=[sds((3, own, d), F32), sds((own, 128), F32)],
        scratch_shapes=ScatterRing.scratch(blocks) + [pltpu.VMEM(blocks[0][0], F32), DMA((2,))],
        compiler_params=pltpu.CompilerParams(collective_id=3, has_side_effects=True, vmem_limit_bytes=VMEM_LIMIT),
        name="tail",
    )(g_qkv, g_vec)


def per_device(tokens, cotangent, attn_w, w_up, w_down, vectors, attn_m, attn_v, up_m, up_v, down_m, down_v, vec_m, vec_v):
    both = ("seq", "rep")
    x = tokens[0]
    dy = cotangent[0]
    t, d = x.shape
    n = lax.axis_size("seq")
    rows_dev = max(M // n, 1)
    seg_len = t * n // M
    ring = n == RING and lax.axis_size("rep") == 2

    if ring:
        weights = (attn_w, w_up, w_down, jnp.pad(vectors, ((0, 0), (0, 128 - vectors.shape[1]))))
    else:
        w_attn = lax.all_gather(attn_w.astype(BF16), both, axis=1, tiled=True)
        vec = lax.all_gather(vectors.astype(BF16), both, axis=0, tiled=True).astype(F32)
        weights = (w_attn[:3], jnp.pad(vec, ((0, 0), (0, 128 - vec.shape[1]))))
    (w_qkv, wo, up, down, gains, taps, h1, q, k, v, conv, f, e, mq, mk, uz, a, z, az, t2, t3, vl, vr) = front(
        x, weights, n, ring
    )
    if not ring:
        w_qkv, wo = w_attn[:3], w_attn[3]
        up = lax.all_gather(w_up.astype(BF16), both, axis=0, tiled=True)
        down = lax.all_gather(w_down.astype(BF16), both, axis=0, tiled=True)
    out, act, da, h2, mix, dx, dmix, dqf, gw, dkt, dg2 = middle(
        x, dy, f, q, conv, wo, up, down, gains, mk, uz, z, padded_rows(6 * M, n)
    )
    dot_xla = functools.partial(jnp.einsum, "ta,tb->ab", preferred_element_type=F32)
    g_down = dot_xla(act, dy).astype(BF16)
    g_up = dot_xla(h2, da).astype(BF16)
    g_o = dot_xla(mix, dx).astype(BF16)
    res = rear((v, dmix, e, k), (g_o, g_up, g_down) if ring else None, gw, uz, a, z, az, t2, t3, mq, mk, vl, vr, taps, dkt, n)
    dv, dkb, dtap, own = res[:4]
    dq, dk, ig, dg1 = last(x, dx, dqf, dkb, dv, own, w_qkv, gains, seg_len, rows_dev)
    g_q = dot_xla(h1, dq) * QK_SCALE
    g_k = dot_xla(h1, dk) * QK_SCALE
    g_v = dot_xla(h1, dv)
    g_qkv = jnp.stack([g_q, g_k, g_v]).astype(BF16)
    g_vec = jnp.concatenate([dg1[:1], dg2[:1], dtap[:KC]], axis=0)
    if ring:
        g_vec = jnp.transpose(jnp.pad(g_vec, ((0, 128 - g_vec.shape[0]), (0, 0))))
        red_o, red_up, red_down = res[4:]
        red_qkv, red_vec = tail(g_qkv, g_vec, n)
        red_attn = jnp.concatenate([red_qkv, red_o[None]], axis=0)
        red_vec = red_vec[:, : vectors.shape[1]]
    else:
        g_attn = jnp.concatenate([g_qkv, g_o[None]], axis=0)
        red_attn = lax.psum_scatter(g_attn, both, scatter_dimension=1, tiled=True).astype(F32)
        red_up = lax.psum_scatter(g_up, both, scatter_dimension=0, tiled=True).astype(F32)
        red_down = lax.psum_scatter(g_down, both, scatter_dimension=0, tiled=True).astype(F32)
        red_vec = lax.psum_scatter(jnp.transpose(g_vec), both, scatter_dimension=0, tiled=True)
    return (
        out[None],
        ig[None],
        *adam_step(attn_w, red_attn, attn_m, attn_v, LEARN_RATE),
        *adam_step(w_up, red_up, up_m, up_v, LEARN_RATE),
        *adam_step(w_down, red_down, down_m, down_v, LEARN_RATE),
        *adam_step(vectors, red_vec, vec_m, vec_v, VECTOR_RATE),
    )


def solution(mesh):
    tok = P("rep", "seq", None)
    att = P(None, ("seq", "rep"), None)
    mat = P(("seq", "rep"), None)
    return jax.shard_map(
        per_device,
        mesh=mesh,
        in_specs=(tok, tok, att, mat, mat, mat, att, att, mat, mat, mat, mat, mat, mat),
        out_specs=(tok, tok, att, att, att) + (mat,) * 9,
        check_vma=False,
    )
```

time: 1200 us -> 434 us (0.36)
  waiting for transfers between devices: 708 us -> 0 us
  blocking collectives: 161 us -> 0 us
  Pallas kernels: 219 us -> 364 us
  local copies, waits for them, and re-layouts: 22.8 us -> 3.92 us
  between operations: 14.8 us -> 1.34 us
    unnamed x13 -> x0, waiting for transfers between devices: 282 us -> none
    reduce_scatter x2 -> x0, waiting for transfers between devices: 222 us -> none  [the longest x1 112 us: per_device(): lax.psum_scatter(g_down, both, scatter_dimension=0, tiled=True).astype(F32)]
    psum x2 -> x0, waiting for transfers between devices: 178 us -> none  [the longest x1 96.1 us: per_device(): gw = lax.psum(gw, 'seq')]
    pallas_call x6 -> x4, Pallas kernels: 202 us -> 348 us  [the longest x1 128 us: front(): pl.pallas_call(functools.partial(front_kernel, n=n, ring=ring), in_specs=...]
    all_gather x2 -> x0, blocking collectives: 83.9 us -> none  [the longest x1 43.8 us: per_device(): vec = lax.all_gather(vectors.astype(BF16), both, axis=0, tiled=True)]
    psum x1 -> x0, blocking collectives: 76.8 us -> none  [per_device(): u, zt = lax.psum((u, zt), 'seq')]
    all_gather x3 -> x0, waiting for transfers between devices: 18.9 us -> none  [the longest x1 18.9 us: per_device(): w_attn = lax.all_gather(attn_w.astype(BF16), both, axis=1, tiled=True)]
    unnamed x52 -> x44, local copies, waits for them, and re-layouts: 14.3 us -> 0.1 us
  transfers between devices with their start and end apart: 14 -> 0, of which waited for: 10 -> 0; matrix products, arithmetic and copies ran while one was open for 6% -> 0% of each run, Pallas kernels for 3% -> 0%
where the time goes in v3:
time: 434 us; the launch traced here: 425 us
  Pallas kernels  364 us (84%)
  matrix products  45.9 us (11%)
  other arithmetic  9.67 us (2%)
    pallas_call x1, Pallas kernels, front(): pl.pallas_call(functools.partial(front_kernel, n=n, ring=ring), in_specs=...  128 us
    pallas_call x1, Pallas kernels, rear(): pl.pallas_call(functools.partial(rear_kernel, n=n, ring=ring), in_specs=[...  92.6 us
    pallas_call x1, Pallas kernels, middle(): pl.pallas_call(middle_kernel, grid=(t // tile,), in_specs=[r, r, r, r, r,...  83.2 us
    pallas_call x1, Pallas kernels, tail(): pl.pallas_call(functools.partial(tail_kernel, n=n), in_specs=[ANYW] * 2,...  44 us
    pallas_call x1, Pallas kernels, last(): pl.pallas_call(functools.partial(last_kernel, seg_len=seg_len, rows_dev=r...  16.2 us
    dot_general x1, matrix products, per_device(): g_up = dot_xla(h2, da).astype(BF16)  14.9 us
    dot_general x1, matrix products, per_device(): g_down = dot_xla(act, dy).astype(BF16)  12.2 us

profile of v3, /device:TPU:0, one launch (start us, length us, event | category | flops | bytes accessed | tf_op | source)
XLA Modules:
  0.0 425.3 jit_solution(1032617246073323536)
XLA Ops:
  0.6 1.3 pad.8.refs_4_
  2.0 128.4 %front.1 = (bf16[3,768,768]{2,1,0:T(8,128)(2,1)}, bf16[768,768]{1,0:T(8,128)(2,1)}, bf16[768,3072]{1,0:T(8,128)(2,1)}, bf16[3072,768]{1,0:T(8,128)(2,1)}, f32[8,...) custom-call(bf16[2048,768]{1,0:T(8,128)(2,1)} %bitcast.27, ...), custom_call_target="tpu_custom_call" | custom-call | tf_op jit(solution)/shard_map/front/pallas_call | solution.py:828
  130.4 83.2 %middle.1 = (bf16[2048,768]{1,0:T(8,128)(2,1)}, bf16[2048,3072]{1,0:T(8,128)(2,1)}, bf16[2048,3072]{1,0:T(8,128)(2,1)}, bf16[2048,768]{1,0:T(8,128)(2,1)}, bf16[...) custom-call(bf16[2048,768]{1,0:T(8,128)(2,1)} %bitcast.28, ...), custom_call_target="tpu_custom_call" | custom-call | tf_op jit(solution)/shard_map/middle/pallas_call | solution.py:947
  213.6 0.7 slice.13
  214.3 0.0 copy-start.18
  214.3 0.0 slice-start
  214.3 6.7 %convolution_convert_fusion.3.refs_4_ = bf16[768,768]{1,0:T(8,128)(2,1)} fusion(bf16[2048,768]{1,0:T(8,128)(2,1)} %get-tuple-element.78, bf16[2048,768]{1,0:T(8,128)(2,1)} %get-tuple-element.72.dx_ref), kind=kOutput, calls=%fused_computation.6 | convolution fusion | flops 2416508928 | bytes 7471104 | tf_op jit(solution)/shard_map/ta,tb->ab/dot_general | solution.py:1294
  221.0 0.0 copy-done.18
  221.0 0.0 copy-start
  221.0 0.0 slice-start.1
  221.0 0.0 slice-start.2
  221.0 14.9 %convolution_convert_fusion.1.refs_5_ = bf16[768,3072]{1,0:T(8,128)(2,1)} fusion(bf16[2048,768]{1,0:T(8,128)(2,1)S(1)} %copy-done.18, bf16[2048,3072]{1,0:T(8,128)(2,1)} %get-tuple-element.80), kind=kOutput, calls=%fused_computation.1 | convolution fusion | flops 9666035712 | bytes 20447232 | tf_op jit(solution)/shard_map/ta,tb->ab/dot_general | solution.py:1293
  235.9 0.0 slice-done
  235.9 0.0 copy-done
  235.9 0.0 slice-done.1
  235.9 0.0 slice-done.2
  235.9 12.2 %convolution_convert_fusion.refs_6_ = bf16[3072,768]{1,0:T(8,128)(2,1)} fusion(bf16[2048,3072]{1,0:T(8,128)(2,1)S(1)} %bitcast.34, bf16[1,2048,768]{2,1,0:T(8,128)(2,1)S(1)} %copy-done), kind=kOutput, calls=%fused_computation | convolution fusion | flops 9666035712 | bytes 20447232 | tf_op jit(solution)/shard_map/ta,tb->ab/dot_general | solution.py:1292
  248.1 92.6 %rear.1 = (bf16[2048,768]{1,0:T(8,128)(2,1)}, bf16[2048,768]{1,0:T(8,128)(2,1)}, f32[40,768]{1,0:T(8,128)}, f32[8,768]{1,0:T(8,128)}, f32[24,768]{1,0:T(8,128)}, /*index=5*/f32[24,3072]{1,0:T(8,128)}, f32[96,768]{1,0:T(8,128)}) custom-call(bf16[2048,768]{1,0:T(8,128)(2,1)} %get-tuple-element.74.refs_0_, bf16[2048,768]{1,0:T(8,128)(2,1)} %get-tuple-element.75.refs_1_, ...), custom_call_target="tpu_custom_call" | custom-call | tf_op jit(solution)/shard_map/rear/pallas_call | solution.py:1138
  340.7 0.0 copy-start.1
  340.7 16.2 %last.1 = (bf16[2048,768]{1,0:T(8,128)(2,1)}, bf16[2048,768]{1,0:T(8,128)(2,1)}, bf16[2048,768]{1,0:T(8,128)(2,1)}, f32[8,768]{1,0:T(8,128)}) custom-call(bf16[2048,768]{1,0:T(8,128)(2,1)} %bitcast.29, bf16[2048,768]{1,0:T(8,128)(2,1)} %get-tuple-element.72.dx_ref, bf16[2048,768]{1,0:T(8,128)(2,1)} %get-tuple-element.73.dqf_ref, ...), custom_call_target="tpu_custom_call" | custom-call | tf_op jit(solution)/shard_map/last/pallas_call | solution.py:1202
  356.9 0.0 copy-done.1
  356.9 0.0 copy-start.11
  357.0 0.0 copy-start.2
  357.0 0.0 copy-start.5
  357.0 0.0 copy-start.6
  357.0 4.6 %fusion = bf16[1,768,768]{2,1,0:T(8,128)(2,1)S(1)} fusion(bf16[2048,768]{1,0:T(8,128)(2,1)} %get-tuple-element.97, bf16[2048,768]{1,0:T(8,128)(2,1)S(1)} %copy-done.1), kind=kOutput, calls=%fused_computation.7 | convolution fusion | flops 2416508928 | bytes 7471104 | tf_op jit(solution)/shard_map/ta,tb->ab/dot_general | solution.py:1300
  361.6 0.0 copy-start.3
  361.6 0.0 copy-start.7
  361.7 0.0 copy-start.8
  361.7 0.8 slice.12
  362.5 0.0 copy-done.11
  362.5 0.2 copy.31
  362.7 0.0 copy-start.16
  362.7 0.8 pad_bitcast_fusion.refs_1_
  363.5 0.0 copy-done.2
  363.5 0.0 copy-done.5
  363.5 0.0 copy-done.6
  363.5 2.3 multiply_subtract_fusion.1
  365.8 0.0 copy-done.3
  365.8 0.0 copy-done.7
  365.8 0.0 copy-done.8
  365.8 2.0 multiply_subtract_fusion
  367.8 0.0 copy-done.16
  367.8 0.0 copy-start.17
  367.8 4.8 %fusion.1 = bf16[1,768,768]{2,1,0:T(8,128)(2,1)S(1)} fusion(bf16[2048,768]{1,0:T(8,128)(2,1)S(1)} %copy-done.16, bf16[2048,768]{1,0:T(8,128)(2,1)} %get-tuple-element.98), kind=kOutput, calls=%fused_computation.8 | convolution fusion | flops 2417098752 | bytes 7471104 | tf_op jit(solution)/shard_map/ta,tb->ab/dot_general | solution.py:1298
  372.6 0.0 copy-done.17
  372.6 2.8 fusion.2
  375.4 2.0 pad_maximum_fusion.refs_0_
  377.4 0.0 copy-start.13
  377.4 0.0 copy-start.14
  377.4 0.0 copy-start.15
  377.4 0.0 copy-start.9
  377.4 0.0 copy-start.10
  377.4 0.0 copy-start.12
  377.4 44.0 %tail.1 = (f32[3,24,768]{2,1,0:T(8,128)}, f32[24,128]{1,0:T(8,128)}) custom-call(bf16[3,768,768]{2,1,0:T(8,128)(2,1)} %pad_maximum_fusion.refs_0_, f32[768,128]{1,0:T(8,128)} %pad_bitcast_fusion.refs_1_), custom_call_target="tpu_custom_call" | custom-call | tf_op jit(solution)/shard_map/tail/pallas_call | solution.py:1254
  421.5 0.0 copy-done.13
  421.5 0.0 copy-done.14
  421.5 0.0 copy-done.15
  421.5 1.3 multiply_subtract_fusion.3
  422.8 0.0 copy-done.4
  422.8 0.0 copy-done.9
  422.8 0.0 copy-done.10
  422.8 0.0 copy-done.12
  422.8 2.0 multiply_subtract_fusion.2
  (3 shorter events, 0.0 us)
Async XLA Ops:
  214.3 6.7 %copy-start.18 = (bf16[2048,768]{1,0:T(8,128)(2,1)S(1)}, bf16[2048,768]{1,0:T(8,128)(2,1)}, u32[]{:S(2)}) copy-start(bf16[2048,768]{1,0:T(8,128)(2,1)} %get-tuple-element.79) | copy-start | bytes 9437188
  214.3 21.6 %slice-start = ((s8[12582912]{0:T(1024)(128)(4,1)}), s8[4194304]{0:T(1024)(128)(4,1)S(1)}, s32[]{:S(2)}) async-start(s8[12582912]{0:T(1024)(128)(4,1)} %bitcast.33), calls=%async_computation | async-start | bytes 8388608
  221.0 14.9 %copy-start = (bf16[1,2048,768]{2,1,0:T(8,128)(2,1)S(1)}, bf16[1,2048,768]{2,1,0:T(8,128)(2,1)}, u32[]{:S(2)}) copy-start(bf16[1,2048,768]{2,1,0:T(8,128)(2,1)} %param.15) | copy-start | bytes 9437188
  221.0 14.9 %slice-start.1 = ((s8[12582912]{0:T(1024)(128)(4,1)}), s8[4194304]{0:T(1024)(128)(4,1)S(1)}, s32[]{:S(2)}) async-start(s8[12582912]{0:T(1024)(128)(4,1)} %bitcast.33), calls=%async_computation.1 | async-start | bytes 8388608
  221.0 14.9 %slice-start.2 = ((s8[12582912]{0:T(1024)(128)(4,1)}), s8[4194304]{0:T(1024)(128)(4,1)S(1)}, s32[]{:S(2)}) async-start(s8[12582912]{0:T(1024)(128)(4,1)} %bitcast.33), calls=%async_computation.2 | async-start | bytes 8388608
  340.7 16.3 %copy-start.1 = (bf16[2048,768]{1,0:T(8,128)(2,1)S(1)}, bf16[2048,768]{1,0:T(8,128)(2,1)}, u32[]{:S(2)}) copy-start(bf16[2048,768]{1,0:T(8,128)(2,1)} %get-tuple-element.93.dv_ref) | copy-start | bytes 9437188
  356.9 5.5 %copy-start.11 = (f32[40,768]{1,0:T(8,128)S(1)}, f32[40,768]{1,0:T(8,128)}, u32[]{:S(2)}) copy-start(f32[40,768]{1,0:T(8,128)} %get-tuple-element.102) | copy-start | bytes 368644
  357.0 6.5 %copy-start.2 = (f32[24,3072]{1,0:T(8,128)S(1)}, f32[24,3072]{1,0:T(8,128)}, u32[]{:S(2)}) copy-start(f32[24,3072]{1,0:T(8,128)} %refs_2_.1) | copy-start | bytes 884740
  357.0 6.5 %copy-start.5 = (f32[24,3072]{1,0:T(8,128)S(1)}, f32[24,3072]{1,0:T(8,128)}, u32[]{:S(2)}) copy-start(f32[24,3072]{1,0:T(8,128)} %param.22) | copy-start | bytes 884740
  357.0 6.5 %copy-start.6 = (f32[24,3072]{1,0:T(8,128)S(1)}, f32[24,3072]{1,0:T(8,128)}, u32[]{:S(2)}) copy-start(f32[24,3072]{1,0:T(8,128)} %param.23) | copy-start | bytes 884740
  361.6 4.2 copy-start.3
  361.6 4.2 copy-start.7
  361.7 4.1 copy-start.8
  362.7 5.2 %copy-start.16 = (bf16[2048,768]{1,0:T(8,128)(2,1)S(1)}, bf16[2048,768]{1,0:T(8,128)(2,1)}, u32[]{:S(2)}) copy-start(bf16[2048,768]{1,0:T(8,128)(2,1)} %get-tuple-element.97) | copy-start | bytes 9437188
  367.8 4.8 %copy-start.17 = (bf16[2048,768]{1,0:T(8,128)(2,1)S(1)}, bf16[2048,768]{1,0:T(8,128)(2,1)}, u32[]{:S(2)}) copy-start(bf16[2048,768]{1,0:T(8,128)(2,1)} %get-tuple-element.99) | copy-start | bytes 9437188
  377.4 44.1 %copy-start.13 = (f32[24,35]{1,0:T(8,128)S(1)}, f32[24,35]{1,0:T(8,128)}, u32[]{:S(2)}) copy-start(f32[24,35]{1,0:T(8,128)} %param.19) | copy-start | bytes 10084
  377.4 44.1 %copy-start.14 = (f32[24,35]{1,0:T(8,128)S(1)}, f32[24,35]{1,0:T(8,128)}, u32[]{:S(2)}) copy-start(f32[24,35]{1,0:T(8,128)} %param.26) | copy-start | bytes 10084
  377.4 44.1 %copy-start.15 = (f32[24,35]{1,0:T(8,128)S(1)}, f32[24,35]{1,0:T(8,128)}, u32[]{:S(2)}) copy-start(f32[24,35]{1,0:T(8,128)} %param.27) | copy-start | bytes 10084
  377.4 45.4 %copy-start.4 = (f32[4,24,768]{2,1,0:T(8,128)S(1)}, f32[4,24,768]{2,1,0:T(8,128)}, u32[]{:S(2)}) copy-start(f32[4,24,768]{2,1,0:T(8,128)} %refs_1_.1) | copy-start | bytes 884740
  377.4 45.4 %copy-start.9 = (f32[4,24,768]{2,1,0:T(8,128)S(1)}, f32[4,24,768]{2,1,0:T(8,128)}, u32[]{:S(2)}) copy-start(f32[4,24,768]{2,1,0:T(8,128)} %param.20) | copy-start | bytes 884740
  377.4 45.4 %copy-start.10 = (f32[4,24,768]{2,1,0:T(8,128)S(1)}, f32[4,24,768]{2,1,0:T(8,128)}, u32[]{:S(2)}) copy-start(f32[4,24,768]{2,1,0:T(8,128)} %param.21) | copy-start | bytes 884740
  377.4 45.4 %copy-start.12 = (f32[24,768]{1,0:T(8,128)S(1)}, f32[24,768]{1,0:T(8,128)}, u32[]{:S(2)}) copy-start(f32[24,768]{1,0:T(8,128)} %get-tuple-element.104) | copy-start | bytes 221188
